TPU v7x, 32 devices: a whole 2x2x4 slice. The times are simulated.
32 devices in a mesh: groups: 2 (over y), nodes: 4 (over z), feat: 2 (over x), chan: 2 (over core).
Axes of the slice: x: 2, y: 2, z: 4, core: 2. Of those that a mesh axis runs over, the one named last changes fastest.
Arguments:
- node_latents: bfloat16 [3072, 512], P(('groups', 'nodes'), 'chan'), parts along dimension 0, may hold values from -6 to 6
- edge_latents: bfloat16 [24576, 512], P(('groups', 'nodes'), 'chan'), parts along dimension 0, may hold values from -6 to 6
- sender_latents: bfloat16 [24576, 512], P(('groups', 'nodes'), 'chan'), parts along dimension 0, may hold values from -6 to 6
- pre_hidden: bfloat16 [24576, 512], P(('groups', 'nodes'), 'feat'), parts along dimension 0, may hold values from -6 to 6
- pre_norm: bfloat16 [24576, 512], P(('groups', 'nodes'), 'chan'), parts along dimension 0, may hold values from -300 to 300
- norm_gain: float32 [512], P('chan'), may hold values from 0.5 to 1.5
- w_in: bfloat16 [3, 512, 512], P(None, 'chan'), may hold values from -0.15625 to 0.15625
- w_out: bfloat16 [512, 512], P('feat', 'chan'), may hold values from -0.25 to 0.25
- senders: int32 [24576], P(('groups', 'nodes')), parts along dimension 0, may hold values from 0 to 1535, as said below
- receivers: int32 [24576], P(('groups', 'nodes')), parts along dimension 0, may hold values from 0 to 1535, as said below
- edge_cotangent: bfloat16 [24576, 512], P(('groups', 'nodes'), 'chan'), parts along dimension 0, may hold values from -6 to 6
- agg_cotangent: bfloat16 [3072, 512], P(('groups', 'nodes'), 'chan'), parts along dimension 0, may hold values from -6 to 6
Outputs:
- node_grad: float32 [3072, 512], P(('groups', 'nodes'), 'chan'), parts along dimension 0
- edge_grad: bfloat16 [24576, 512], P(('groups', 'nodes'), 'chan'), parts along dimension 0
- w_in_grad: float32 [6, 512, 512], P('groups', 'chan', 'feat'), parts along dimension 0
- w_out_grad: float32 [1024, 512], P(('groups', 'feat'), 'chan'), parts along dimension 0
- gain_grad: float32 [1024], P(('groups', 'chan')), parts along dimension 0
There are 2 independent parts, one for each index of `groups`. A program takes and returns all parts, laid end to end along the dimension named above; an argument that names none is the same for every part. Nothing has to cross between parts.
Inputs may be any that keep to these rules, and one draw needn't show every extreme that they name: Of the 3072 edges of one index of nodes (edges 3072 * i to 3072 * i + 3071, whose nodes are 384 * i to 384 * i + 383), exactly 1536 have senders on other indices, and at most 1024 on any one other index; some index receives exactly 1024 from every other index. `receivers`: each edge's receiver lies among the 384 nodes of the index of nodes that holds the edge.
All inputs are finite; a program needn't handle non-finite values.
Results may differ from a plain program's by a relative error of at most 0.0055.
Values may be sent and summed in bfloat16 or wider, within the bound.
No kernel may reach another device: no remote copies, remote signals or barrier semaphores. Data moves between devices by JAX's collectives and lax.ppermute only.
A program may use at most 128 MiB of HBM per device.

v0:
```python
import math

import jax
import jax.numpy as jnp
from jax import lax
from jax.sharding import PartitionSpec as P

D = 512


def silu_parts(pre_hidden):
    pre_value = pre_hidden.astype(jnp.float32)
    sig_value = jax.nn.sigmoid(pre_value)
    activation = (pre_value * sig_value).astype(jnp.bfloat16)
    derivative = sig_value * (1.0 + pre_value * (1.0 - sig_value))
    return (activation, derivative)


def contract_rows(left_side, right_side):
    return lax.dot_general(
        left_side, right_side, (((0,), (0,)), ((), ())), preferred_element_type=jnp.float32
    )


def contract_cols(left_side, right_side):
    return lax.dot_general(
        left_side, right_side, (((1,), (1,)), ((), ())), preferred_element_type=jnp.float32
    )


def body(
    node_latents,
    edge_latents,
    sender_latents,
    pre_hidden,
    pre_norm,
    norm_gain,
    w_in,
    w_out,
    senders,
    receivers,
    edge_cotangent,
    agg_cotangent,
):
    shards = lax.axis_size("nodes")
    node_count = node_latents.shape[0]
    edge_count = edge_latents.shape[0]
    half_width = edge_latents.shape[1]
    my_shard = lax.axis_index("nodes")
    first_node = my_shard * node_count
    local_recv = receivers - first_node
    grad_scale = 1.0 / math.sqrt(edge_count * shards)
    stored = pre_norm.astype(jnp.float32)
    upstream = edge_cotangent.astype(jnp.float32) + agg_cotangent.astype(jnp.float32)[local_recv]
    weighted = norm_gain * upstream
    row_total, row_square, row_first, row_cross = lax.psum(
        (
            jnp.sum(stored, axis=1),
            jnp.sum(stored * stored, axis=1),
            jnp.sum(weighted, axis=1),
            jnp.sum(weighted * stored, axis=1),
        ),
        "chan",
    )
    center = row_total / D
    spread = row_square / D - center * center
    inv_std = lax.rsqrt(spread + 1e-05)
    normed = (stored - center[:, None]) * inv_std[:, None]
    mean_first = row_first / D
    mean_cross = inv_std * (row_cross / D - center * mean_first)
    norm_grad = (
        inv_std[:, None] * (weighted - mean_first[:, None] - normed * mean_cross[:, None])
    ).astype(jnp.bfloat16)
    hidden_grad = lax.psum(contract_cols(norm_grad, w_out), "chan")
    activation, derivative = silu_parts(pre_hidden)
    pre_grad = (hidden_grad * derivative).astype(jnp.bfloat16)
    w_flat = w_in.reshape(3 * half_width, w_in.shape[2])
    input_grad = contract_cols(lax.all_gather(pre_grad, "feat", axis=1, tiled=True), w_flat)
    edge_grad = (edge_cotangent.astype(jnp.float32) + input_grad[:, :half_width]).astype(
        jnp.bfloat16
    )
    sender_term = input_grad[:, half_width : 2 * half_width].astype(jnp.bfloat16)
    node_grad = jax.ops.segment_sum(
        input_grad[:, 2 * half_width :], local_recv, num_segments=node_count
    )
    pooled = jax.ops.segment_sum(
        sender_term.astype(jnp.float32), senders, num_segments=node_count * shards
    )
    node_grad = node_grad + lax.psum_scatter(
        pooled.astype(jnp.bfloat16), "nodes", scatter_dimension=0, tiled=True
    ).astype(jnp.float32)
    gathered_nodes = node_latents[local_recv]
    w_in_local = (
        jnp.stack(
            [
                contract_rows(edge_latents, pre_grad),
                contract_rows(sender_latents, pre_grad),
                contract_rows(gathered_nodes, pre_grad),
            ]
        )
        * grad_scale
    )
    w_out_local = contract_rows(activation, norm_grad) * grad_scale
    gain_local = jnp.sum(upstream * normed, axis=0) * grad_scale
    w_in_grad, w_out_grad, gain_grad = lax.psum((w_in_local, w_out_local, gain_local), "nodes")
    return (node_grad, edge_grad, w_in_grad, w_out_grad, gain_grad)


def solution(mesh):
    placed = (
        P(("groups", "nodes"), "chan"),
        P(("groups", "nodes"), "chan"),
        P(("groups", "nodes"), "chan"),
        P(("groups", "nodes"), "feat"),
        P(("groups", "nodes"), "chan"),
        P("chan"),
        P(None, "chan", None),
        P("feat", "chan"),
        P(("groups", "nodes")),
        P(("groups", "nodes")),
        P(("groups", "nodes"), "chan"),
        P(("groups", "nodes"), "chan"),
    )
    return jax.shard_map(
        body,
        mesh=mesh,
        in_specs=placed,
        out_specs=(
            P(("groups", "nodes"), "chan"),
            P(("groups", "nodes"), "chan"),
            P("groups", "chan", "feat"),
            P(("groups", "feat"), "chan"),
            P(("groups", "chan")),
        ),
        check_vma=False,
    )
```

profile of v0, /device:TPU:0, one launch (start us, length us, event | category | flops | bytes accessed | tf_op | source)
XLA Modules:
  0.0 227.2 jit_solution(533135385217720974)
XLA Ops:
  7.2 0.0 copy-start
  7.2 0.0 all-reduce.6.cloned.1.call-start
  7.2 2.4 %convert_reduce_fusion = (f32[3072]{0:T(1024)S(1)}, f32[3072]{0:T(1024)S(1)}) fusion(bf16[3072,256]{1,0:T(8,128)(2,1)} %param.16), kind=kLoop, calls=%fused_computation.6 | loop fusion | flops 3139584 | bytes 1597440 | tf_op jit(solution)/shard_map/reduce_sum | solution.py:58
  9.6 1.0 convert_element_type.37
  10.6 3.7 %all-reduce.2 = (f32[3072]{0:T(1024)S(1)}, f32[3072]{0:T(1024)S(1)}) all-reduce(f32[3072]{0:T(1024)S(1)} %get-tuple-element.18, f32[3072]{0:T(1024)S(1)} %get-tuple-element.19), channel_id=1, replica_groups=mesh['groups'=2,'nodes'=4,'feat'=2,'chan'=2] {'chan'}, use_global_device_ids=true, to_apply=%region_3.0 | all-reduce | flops 6144 | bytes 49152 | tf_op jit(solution)/shard_map/psum | solution.py:56
  14.3 0.0 copy-start.14
  14.3 0.0 copy-start.16
  14.3 0.6 add_rsqrt_fusion
  14.9 1.3 fusion.28
  16.3 0.0 copy-done.14
  16.3 0.0 copy-done.16
  16.3 12.3 %gather_fusion = f32[3072,256]{1,0:T(8,128)} fusion(f32[384,256]{1,0:T(8,128)S(1)} %convert_element_type.37, s32[3072]{0:T(1024)S(1)} %get-tuple-element.26), kind=kCustom, calls=%fused_computation | custom fusion | bytes 6303744 | tf_op jit(solution)/shard_map/gather | solution.py:54
  28.6 0.0 copy-done.2
  28.6 0.0 copy-done.18
  28.6 0.0 copy-start.17
  28.6 0.0 copy-start.12
  28.6 0.0 copy-start.13
  28.6 4.4 %fusion.16 = (f32[256]{0:T(256)S(1)}, f32[3072]{0:T(1024)S(1)}, f32[3072]{0:T(1024)S(1)}) fusion(bf16[3072,256]{1,0:T(8,128)(2,1)S(1)} %copy-done.2, f32[3072]{0:T(1024)} %get-tuple-element.31, f32[3072]{0:T(1024)} %get-tuple-element.30, f32[3072,256]{1,0:T(8,128)} %gather_fusion, bf16[3072,256]{1,0:T(8,128)(2,1)} %param.22, f32[256]{0:T(256)S(1)} %copy-done.18), kind=kLoop, calls=%fused_computation.29 | loop fusion | flops 8644352 | bytes 6342656 | tf_op jit(solution)/shard_map/reduce_sum | solution.py:104
  33.1 3.4 %all-reduce.1 = (f32[3072]{0:T(1024)S(1)}, f32[3072]{0:T(1024)S(1)}) all-reduce(f32[3072]{0:T(1024)S(1)} %get-tuple-element.16, f32[3072]{0:T(1024)S(1)} %get-tuple-element.17), channel_id=1, replica_groups=mesh['groups'=2,'nodes'=4,'feat'=2,'chan'=2] {'chan'}, use_global_device_ids=true, to_apply=%region_7.0 | all-reduce | flops 6144 | bytes 49152 | tf_op jit(solution)/shard_map/psum | solution.py:56
  36.5 0.0 copy-done.15
  36.5 0.0 copy-done.17
  36.5 0.0 copy-done.12
  36.6 0.0 copy-done.13
  36.6 0.0 copy-start.11
  36.6 4.4 %fusion.15 = bf16[3072,256]{1,0:T(8,128)(2,1)S(1)} fusion(bf16[3072,256]{1,0:T(8,128)(2,1)S(1)} %copy-done.2, f32[3072]{0:T(1024)S(1)} %get-tuple-element.29, f32[3072]{0:T(1024)S(1)} %copy-done.13, f32[3072]{0:T(1024)S(1)} %get-tuple-element.28, f32[256]{0:T(256)S(1)} %copy-done.18, f32[3072]{0:T(1024)S(1)} %copy-done.12, f32[3072,256]{1,0:T(8,128)} %gather_fusion, ...), kind=kLoop, calls=%fused_computation.28 | loop fusion | flops 8650752 | bytes 7914496 | tf_op jit(solution)/shard_map/convert_element_type | solution.py:73
  40.9 0.0 copy-start.4
  41.0 1.1 copy-done.4
  42.1 2.3 fusion.30
  44.4 0.0 all-reduce.6.cloned.1.call-update
  44.4 0.0 copy-start.1
  44.4 0.0 all-gather.2.cloned.1.call-start
  44.4 25.9 %all-reduce.6.cloned.1.call-done = f32[3072,256]{1,0:T(8,128)} async-done(((f32[3072,256]{1,0:T(8,128)}), f32[3072,256]{1,0:T(8,128)}) %all-reduce.6.cloned.1.call-update) | async-done | bytes 3145744 | tf_op jit(solution)/shard_map/psum | solution.py:74
  70.3 4.2 %fusion.7 = bf16[3072,256]{1,0:T(8,128)(2,1)} fusion(f32[3072,256]{1,0:T(8,128)} %all-reduce.6.cloned.1.call-done, bf16[3072,256]{1,0:T(8,128)(2,1)S(1)} %copy-done.8), kind=kLoop, calls=%fused_computation.20 | loop fusion | flops 7864320 | bytes 6291456 | tf_op jit(solution)/shard_map/convert_element_type | solution.py:76
  74.6 0.0 all-gather.2.cloned.1.call-update
  74.6 0.0 copy-start.5
  74.6 0.0 all-reduce.8.cloned.1.call-start
  74.6 0.0 copy-done.1
  74.7 13.0 %gather_fusion.1 = bf16[3072,256]{1,0:T(8,128)(2,1)} fusion(bf16[384,256]{1,0:T(8,128)(2,1)S(1)} %copy-done.1, s32[3072]{0:T(1024)S(1)} %get-tuple-element.26), kind=kCustom, calls=%fused_computation.1 | custom fusion | bytes 3158016 | tf_op jit(solution)/shard_map/gather | solution.py:92
  87.6 3.3 %fusion.24 = f32[256,256]{1,0:T(8,128)} fusion(bf16[3072,256]{1,0:T(8,128)(2,1)S(1)} %copy-done.5, bf16[3072,256]{1,0:T(8,128)(2,1)} %param.15), kind=kOutput, calls=%fused_computation.41 | convolution fusion | flops 407437312 | bytes 3407872 | tf_op jit(solution)/shard_map/dot_general | solution.py:20
  90.9 0.7 convolution_bitcast_fusion
  91.7 0.0 copy-done
  91.7 0.6 convolution_bitcast_fusion.1
  92.3 0.1 copy-done.19
  92.4 0.6 convolution_bitcast_fusion.2
  93.0 0.9 maximum_multiply_fusion
  93.9 0.0 all-reduce.8.cloned.1.call-update
  94.0 0.2 reduce-scatter.2.cloned.1.call-start
  94.2 26.6 %all-gather.2.cloned.1.call-done = bf16[3072,512]{1,0:T(8,128)(2,1)} async-done(((bf16[3072,256]{1,0:T(8,128)(2,1)}), bf16[3072,512]{1,0:T(8,128)(2,1)}) %all-gather.2.cloned.1.call-update) | async-done | bytes 3145744 | tf_op jit(solution)/shard_map/all_gather | solution.py:78
  120.8 0.0 copy-done.20
  120.8 8.2 %fusion.31 = f32[3072,768]{1,0:T(8,128)} fusion(bf16[3072,512]{1,0:T(8,128)(2,1)} %all-gather.2.cloned.1.call-done, bf16[768,512]{1,0:T(8,128)(2,1)S(1)} %bitcast.22), kind=kOutput, calls=%fused_computation.54 | convolution fusion | flops 2415919104 | bytes 13369344 | tf_op jit(solution)/shard_map/dot_general | solution.py:26
  129.0 18.8 %scatter_custom_fusion = f32[1536,256]{1,0:T(8,128)} fusion(s32[3072]{0:T(1024)} %param.20, f32[3072,768]{1,0:T(8,128)} %fusion.31, f32[]{:T(128)} %constant.9.clone.1), kind=kCustom, calls=%fused_computation.34 | custom fusion | flops 1572864 | bytes 3146240 | tf_op jit(solution)/shard_map/scatter-add | solution.py:86
  147.8 2.5 %convert_element_type.42 = bf16[1536,256]{1,0:T(8,128)(2,1)} convert(f32[1536,256]{1,0:T(8,128)} %scatter_custom_fusion) | non-fusion elementwise | flops 393216 | bytes 2359296 | tf_op jit(solution)/shard_map/convert_element_type | solution.py:90
  150.3 0.0 reduce-scatter.2.cloned.1.call-update
  150.3 12.5 %psum.63 = f32[256]{0:T(256)} all-reduce(f32[256]{0:T(256)S(1)} %broadcast_multiply_fusion.2), channel_id=1, replica_groups=mesh['groups'=2,'nodes'=4,'feat'=2,'chan'=2] {'nodes'}, use_global_device_ids=true, to_apply=%region_15.0 | all-reduce | flops 256 | bytes 2048 | tf_op jit(solution)/shard_map/psum | solution.py:105
  162.9 13.3 %all-reduce.8.cloned.1.call-done = (f32[3,256,256]{1,2,0:T(8,128)}, f32[256,256]{1,0:T(8,128)}) async-done(((f32[3,256,256]{1,2,0:T(8,128)}, f32[256,256]{1,0:T(8,128)}), (f32[3,256,256]{1,2,0:T(8,128)}, f32[256,256]{1,0:T(8,128)})) %all-reduce.8.cloned.1.call-update) | async-done | bytes 1048592 | tf_op jit(solution)/shard_map/psum | solution.py:105
  176.2 2.3 %copy.20 = f32[3,256,256]{2,1,0:T(8,128)} copy(f32[3,256,256]{1,2,0:T(8,128)} %get-tuple-element.20) | data formatting | bytes 1572864
  178.5 0.0 copy-done.3
  178.5 3.4 %fusion = bf16[3072,256]{1,0:T(8,128)(2,1)} fusion(bf16[3072,256]{1,0:T(8,128)(2,1)S(1)} %copy-done.3, f32[3072,768]{1,0:T(8,128)} %fusion.31), kind=kLoop, calls=%fused_computation.13 | loop fusion | flops 2359296 | bytes 6291456 | tf_op jit(solution)/shard_map/convert_element_type | solution.py:79
  181.9 19.2 %reduce-scatter.2.cloned.1.call-done = bf16[384,256]{1,0:T(8,128)(2,1)} async-done(((bf16[1536,256]{1,0:T(8,128)(2,1)}), bf16[384,256]{1,0:T(8,128)(2,1)}) %reduce-scatter.2.cloned.1.call-update) | async-done | bytes 196624 | tf_op jit(solution)/shard_map/reduce_scatter | solution.py:89
  201.0 1.0 convert_element_type.43
  202.0 17.8 %scatter_custom_fusion.1 = f32[384,256]{1,0:T(8,128)S(1)} fusion(f32[384,256]{1,0:T(8,128)S(1)} %convert_element_type.43, s32[3072]{0:T(1024)} %get-tuple-element.27, f32[3072,768]{1,0:T(8,128)} %fusion.31), kind=kCustom, calls=%fused_computation.31 | custom fusion | flops 786432 | bytes 3538944 | tf_op jit(solution)/shard_map/scatter-add | solution.py:83
  219.8 0.0 copy-start.9
  219.8 0.8 copy.26
  220.6 0.1 copy-done.9
  (18 shorter events, 0.0 us)
Async XLA Ops:
  7.2 84.5 %copy-start = (bf16[3072,256]{1,0:T(8,128)(2,1)S(1)}, bf16[3072,256]{1,0:T(8,128)(2,1)}, u32[]{:S(2)}) copy-start(bf16[3072,256]{1,0:T(8,128)(2,1)} %param.14) | copy-start | bytes 4718596
  7.2 63.1 %all-reduce.6.cloned.1.call-start = ((), (), s32[]{:S(2)}) async-start(), calls=%async_computation.1 | async-start | bytes 6291456 | tf_op jit(solution)/shard_map/psum | solution.py:74
  14.3 1.9 copy-start.14
  14.3 1.9 copy-start.16
  16.3 12.3 %copy-start.2 = (bf16[3072,256]{1,0:T(8,128)(2,1)S(1)}, bf16[3072,256]{1,0:T(8,128)(2,1)}, u32[]{:S(2)}) copy-start(bf16[3072,256]{1,0:T(8,128)(2,1)} %param.16) | copy-start | bytes 4718596
  16.3 12.3 %copy-start.18 = (f32[256]{0:T(256)S(1)}, f32[256]{0:T(256)}, u32[]{:S(2)}) copy-start(f32[256]{0:T(256)} %param.17) | copy-start | bytes 3076
  28.6 7.9 %copy-start.15 = (f32[3072]{0:T(1024)S(1)}, f32[3072]{0:T(1024)}, u32[]{:S(2)}) copy-start(f32[3072]{0:T(1024)} %copy-done.14) | copy-start | bytes 36868
  28.6 7.9 %copy-start.17 = (f32[3072]{0:T(1024)S(1)}, f32[3072]{0:T(1024)}, u32[]{:S(2)}) copy-start(f32[3072]{0:T(1024)} %copy-done.16) | copy-start | bytes 36868
  28.6 8.0 %copy-start.12 = (f32[3072]{0:T(1024)S(1)}, f32[3072]{0:T(1024)}, u32[]{:S(2)}) copy-start(f32[3072]{0:T(1024)} %get-tuple-element.30) | copy-start | bytes 36868
  28.6 8.0 %copy-start.13 = (f32[3072]{0:T(1024)S(1)}, f32[3072]{0:T(1024)}, u32[]{:S(2)}) copy-start(f32[3072]{0:T(1024)} %get-tuple-element.31) | copy-start | bytes 36868
  36.6 5.5 %copy-start.11 = (bf16[256,256]{1,0:T(8,128)(2,1)S(1)}, bf16[256,256]{1,0:T(8,128)(2,1)}, u32[]{:S(2)}) copy-start(bf16[256,256]{1,0:T(8,128)(2,1)} %param.19) | copy-start | bytes 393220
  40.9 1.1 copy-start.4
  44.4 26.0 %copy-start.8 = (bf16[3072,256]{1,0:T(8,128)(2,1)S(1)}, bf16[3072,256]{1,0:T(8,128)(2,1)}, u32[]{:S(2)}) copy-start(bf16[3072,256]{1,0:T(8,128)(2,1)} %param.15) | copy-start | bytes 4718596
  44.4 30.3 %copy-start.1 = (bf16[384,256]{1,0:T(8,128)(2,1)S(1)}, bf16[384,256]{1,0:T(8,128)(2,1)}, u32[]{:S(2)}) copy-start(bf16[384,256]{1,0:T(8,128)(2,1)} %param.12) | copy-start | bytes 589828
  44.4 76.4 %all-gather.2.cloned.1.call-start = ((), (), s32[]{:S(2)}) async-start(), calls=%async_computation.2 | async-start | bytes 4718592 | tf_op jit(solution)/shard_map/all_gather | solution.py:78
  74.6 13.0 %copy-start.5 = (bf16[3072,256]{1,0:T(8,128)(2,1)S(1)}, bf16[3072,256]{1,0:T(8,128)(2,1)}, u32[]{:S(2)}) copy-start(bf16[3072,256]{1,0:T(8,128)(2,1)} %copy-done.4) | copy-start | bytes 4718596
  74.6 101.6 %all-reduce.8.cloned.1.call-start = ((), (), s32[]{:S(2)}) async-start(), calls=%async_computation.4 | async-start | bytes 2097152 | tf_op jit(solution)/shard_map/psum | solution.py:105
  87.6 3.3 %copy-start.6 = (bf16[3072,256]{1,0:T(8,128)(2,1)S(1)}, bf16[3072,256]{1,0:T(8,128)(2,1)}, u32[]{:S(2)}) copy-start(bf16[3072,256]{1,0:T(8,128)(2,1)} %fusion.7) | copy-start | bytes 4718596
  87.6 3.3 %copy-start.7 = (bf16[3072,256]{1,0:T(8,128)(2,1)S(1)}, bf16[3072,256]{1,0:T(8,128)(2,1)}, u32[]{:S(2)}) copy-start(bf16[3072,256]{1,0:T(8,128)(2,1)} %gather_fusion.1) | copy-start | bytes 4718596
  90.9 1.4 copy-start.19
  92.4 28.4 %copy-start.20 = (bf16[3,256,512]{2,1,0:T(8,128)(2,1)S(1)}, bf16[3,256,512]{2,1,0:T(8,128)(2,1)}, u32[]{:S(2)}) copy-start(bf16[3,256,512]{2,1,0:T(8,128)(2,1)} %param.18) | copy-start | bytes 2359300
  94.0 107.1 %reduce-scatter.2.cloned.1.call-start = ((), (), s32[]{:S(2)}) async-start(), calls=%async_computation.3 | async-start | bytes 983040 | tf_op jit(solution)/shard_map/reduce_scatter | solution.py:89
  147.8 30.7 %copy-start.3 = (bf16[3072,256]{1,0:T(8,128)(2,1)S(1)}, bf16[3072,256]{1,0:T(8,128)(2,1)}, u32[]{:S(2)}) copy-start(bf16[3072,256]{1,0:T(8,128)(2,1)} %param.22) | copy-start | bytes 4718596
  181.9 38.0 %copy-start.10 = (f32[256,256]{1,0:T(8,128)S(1)}, f32[256,256]{1,0:T(8,128)}, u32[]{:S(2)}) copy-start(f32[256,256]{1,0:T(8,128)} %get-tuple-element.35) | copy-start | bytes 786436
  219.8 0.8 copy-start.9
Sparse Core Ops, SparseCore 0:
  44.5 25.7 all-reduce.5
  74.7 46.0 all-gather.1
  124.0 52.2 all-reduce.7
  178.4 22.6 reduce-scatter.1
where the time goes:
time: 228 us; the launch traced here: 227 us
  waiting for transfers between devices  85.1 us (37%)
  other arithmetic  62.7 us (28%)
  local copies, waits for them, and re-layouts  29.7 us (13%)
  blocking collectives  19.7 us (9%)
  matrix products  15.7 us (7%)
  between operations  14 us (6%)
    all_gather x1, waiting for transfers between devices, body(): lax.all_gather(pre_grad, 'feat', axis=1, tiled=True)  26.6 us
    psum x1, waiting for transfers between devices, body(): hidden_grad = lax.psum(contract_cols(norm_grad, w_out), 'chan')  25.9 us
    reduce_scatter x1, waiting for transfers between devices, body(): lax.psum_scatter(pooled.astype(jnp.bfloat16), 'nodes', scatter_dimension=...  19.2 us
    scatter-add x1, other arithmetic, body(): jax.ops.segment_sum(sender_term.astype(jnp.float32), senders, num_segment...  18.8 us
    scatter-add x1, other arithmetic, body(): jax.ops.segment_sum(input_grad[:, 2 * half_width:], local_recv, num_segme...  17.8 us
    psum x1, waiting for transfers between devices, body(): lax.psum((w_in_local, w_out_local, gain_local), 'nodes')  13.3 us
    gather x1, local copies, waits for them, and re-layouts, body(): gathered_nodes = node_latents[local_recv]  13 us
    psum x1, blocking collectives, body(): lax.psum((w_in_local, w_out_local, gain_local), 'nodes')  12.5 us
  transfers between devices with their start and end apart: 4, of which 4 were waited for; matrix products, arithmetic and copies ran while one was open for 24% of the time, Pallas kernels for 0%

commit v1 on v0

v1 whole, which is shorter than its diff:
```python
import functools
import math

import jax
import jax.numpy as jnp
from jax import lax
from jax.experimental import pallas as pl
from jax.experimental.pallas import tpu as pltpu
from jax.sharding import PartitionSpec as P

F32 = jnp.float32
BF16 = jnp.bfloat16
VMEM_LIMIT = 48 * 1024 * 1024
PAD = 16


def dot_nn(a, b):
    return lax.dot_general(a, b, (((1,), (0,)), ((), ())), preferred_element_type=F32)


def dot_nt(a, b):
    return lax.dot_general(a, b, (((1,), (1,)), ((), ())), preferred_element_type=F32)


def dot_tn(a, b):
    return lax.dot_general(a, b, (((0,), (0,)), ((), ())), preferred_element_type=F32)


def params():
    return pltpu.CompilerParams(vmem_limit_bytes=VMEM_LIMIT)


def cost(flops, nbytes):
    return pl.CostEstimate(flops=int(flops), bytes_accessed=int(nbytes), transcendentals=0)


def whole(shape):
    return pl.BlockSpec(shape, lambda *_: (0,) * len(shape))


def ring(size, step):
    return [(i, (i + step) % size) for i in range(size)]


def split_rows(row, width):
    parts = [row[:, j * width : (j + 1) * width] for j in range(row.shape[1] // width)]
    parts.append(jnp.zeros((PAD - len(parts), width), row.dtype))
    return jnp.concatenate(parts, axis=0)


def edge_kernel(
    nodes_dev, steps, idx, x_own, x_sib, cot_own, cot_sib, hid, recv, agg_own, agg_sib, gain_own, gain_sib,
    w_own, w_sib, pre_grad, wo_own, gain_out, small, acc_sib, gsum_own, gsum_sib,
):
    step = pl.program_id(0)
    first_node = idx[1] * nodes_dev
    rows, half_width = x_own.shape
    width = 2 * half_width

    @pl.when(step == 0)
    def _():
        wo_own[...] = jnp.zeros_like(wo_own)
        acc_sib[...] = jnp.zeros_like(acc_sib)
        gsum_own[...] = jnp.zeros_like(gsum_own)
        gsum_sib[...] = jnp.zeros_like(gsum_sib)

    column = jnp.transpose(jnp.broadcast_to(recv[...], (8, rows)))[:, :1] - first_node
    picks = lax.broadcasted_iota(jnp.int32, (rows, nodes_dev), 1) == column
    picks = jnp.where(picks, 1.0, 0.0).astype(BF16)
    up_own = cot_own[...].astype(F32) + dot_nn(picks, agg_own[...])
    up_sib = cot_sib[...].astype(F32) + dot_nn(picks, agg_sib[...])

    def row_mean(a, b):
        return jnp.sum(a + b, axis=1, keepdims=True) * (1.0 / width)

    v_own = x_own[...].astype(F32)
    v_sib = x_sib[...].astype(F32)
    mean = row_mean(v_own, v_sib)
    v_own = v_own - mean
    v_sib = v_sib - mean
    inv = lax.rsqrt(row_mean(v_own * v_own, v_sib * v_sib) + 1e-05)
    n_own = v_own * inv
    n_sib = v_sib * inv
    wt_own = gain_own[...] * up_own
    wt_sib = gain_sib[...] * up_sib
    mean_first = row_mean(wt_own, wt_sib)
    mean_cross = row_mean(wt_own * n_own, wt_sib * n_sib)
    g_own = (inv * (wt_own - mean_first - n_own * mean_cross)).astype(BF16)
    g_sib = (inv * (wt_sib - mean_first - n_sib * mean_cross)).astype(BF16)
    hidden = dot_nt(g_own, w_own[...]) + dot_nt(g_sib, w_sib[...])
    value = hid[...].astype(F32)
    sig = 1.0 / (1.0 + jnp.exp(-value))
    act = (value * sig).astype(BF16)
    pre_grad[...] = (hidden * (sig * (1.0 + value * (1.0 - sig)))).astype(BF16)
    wo_own[...] += dot_tn(g_own, act)
    acc_sib[...] += dot_tn(g_sib, act)
    gsum_own[...] += jnp.sum(up_own * n_own, axis=0, keepdims=True)
    gsum_sib[...] += jnp.sum(up_sib * n_sib, axis=0, keepdims=True)

    @pl.when(step == steps - 1)
    def _():
        gain_out[...] = gsum_own[...]
        small[: acc_sib.shape[0], :] = acc_sib[...].astype(BF16)
        small[acc_sib.shape[0] :, :] = split_rows(gsum_sib[...], small.shape[1]).astype(BF16)


def pool_kernel(
    shards, steps, idx, g_own, g_sib, edge_lat, send_lat, node_lat, senders, recv, wo_own, gain_own, small, *rest
):
    w_out = rest[:shards]
    s_out = rest[shards : 2 * shards]
    recv_out, grads, pooled, by_recv = rest[2 * shards :]
    step = pl.program_id(0)
    core, shard = idx[0], idx[1]
    nodes_dev, half_width = node_lat.shape
    half_nodes = nodes_dev // 2
    rows, feat_width = g_own.shape

    @pl.when(step == 0)
    def _():
        grads[...] = jnp.zeros_like(grads)
        pooled[...] = jnp.zeros_like(pooled)
        by_recv[...] = jnp.zeros_like(by_recv)

    grad = jnp.where(step < steps // 2, g_own[...], g_sib[...])
    node_id = lax.broadcasted_iota(jnp.int32, (nodes_dev, rows), 0)
    picks = jnp.where(node_id + shard * nodes_dev == recv[...], 1.0, 0.0).astype(BF16)
    by_recv[...] += dot_nn(picks, grad)
    half_id = lax.broadcasted_iota(jnp.int32, (half_nodes, rows), 0) + core * half_nodes
    for dest in range(shards):
        picks = jnp.where(half_id + dest * nodes_dev == senders[...], 1.0, 0.0).astype(BF16)
        pooled[dest * half_nodes : (dest + 1) * half_nodes, :] += dot_nn(picks, grad)
    grads[:half_width, :] += dot_tn(edge_lat[...], grad)
    grads[half_width : 2 * half_width, :] += dot_tn(send_lat[...], grad)

    @pl.when(step == steps - 1)
    def _():
        sums = by_recv[...]
        high = sums.astype(BF16)
        low = (sums - high.astype(F32)).astype(BF16)
        grads[2 * half_width : 3 * half_width, :] = dot_tn(node_lat[...], high) + dot_tn(node_lat[...], low)
        grads[3 * half_width :, :] = wo_own[...] + small[:half_width, :].astype(F32)
        gain = split_rows(gain_own[...], feat_width) + small[half_width:, :].astype(F32)
        recv_out[...] = high
        block = 4 * half_width // shards
        for k in range(shards):
            dest = lax.rem(shard + k, shards)
            w_rows = grads[pl.ds(pl.multiple_of(dest * block, 16), block), :]
            w_out[k][:block, :] = w_rows.astype(w_out[k].dtype)
            w_out[k][block:, :] = gain.astype(w_out[k].dtype)
            s_rows = pooled[pl.ds(pl.multiple_of(dest * half_nodes, 16), half_nodes), :]
            s_out[k][...] = s_rows.astype(s_out[k].dtype)


def sum_kernel(*refs):
    total = refs[0][...].astype(F32)
    for ref in refs[1:-1]:
        total = total + ref[...].astype(F32)
    refs[-1][...] = total.astype(refs[-1].dtype)


def add_up(parts):
    return pl.pallas_call(
        sum_kernel,
        out_shape=jax.ShapeDtypeStruct(parts[0].shape, BF16),
        compiler_params=params(),
        cost_estimate=cost(parts[0].size * len(parts), parts[0].size * 10),
    )(*parts)


def sum_send_kernel(idx, by_recv, *refs):
    total = refs[0][...].astype(F32)
    for ref in refs[1:-2]:
        total = total + ref[...].astype(F32)
    alone, both = refs[-2:]
    total = total.astype(BF16)
    rows = total.shape[0]
    alone[...] = total
    both[:rows, :] = total
    both[rows:, :] = by_recv[pl.ds(pl.multiple_of(idx[0] * rows, 16), rows), :]


def place_kernel(shards, scale, idx, *refs):
    totals = refs[:shards]
    w_in_grad, w_out_grad, gain_grad, held = refs[shards:]
    half_width, feat_width = w_in_grad.shape[1:]
    block = 4 * half_width // shards
    for k in range(shards):
        source = lax.rem(idx[1] - k + shards, shards)
        held[pl.ds(pl.multiple_of(source * block, 16), block), :] = totals[k][:block, :].astype(F32) * scale

        @pl.when(source == 0)
        def _(k=k):
            rows = totals[k][block:, :].astype(F32) * scale
            for j in range(half_width // feat_width):
                gain_grad[:, j * feat_width : (j + 1) * feat_width] = rows[j : j + 1, :]

    for k in range(3):
        w_in_grad[k] = held[k * half_width : (k + 1) * half_width, :]
    w_out_grad[...] = jnp.transpose(held[3 * half_width :, :])


def edge_out_kernel(feats, steps, idx, cot, w_edge, *refs):
    own = refs[:feats]
    sib = refs[feats : 2 * feats]
    out, held = refs[2 * feats :]
    step = pl.program_id(0)
    feat_width = own[0].shape[1]
    for k in range(feats):
        source = lax.rem(idx[2] - k + feats, feats)
        piece = jnp.where(step < steps // 2, own[k][...], sib[k][...])
        held[:, pl.ds(pl.multiple_of(source * feat_width, 128), feat_width)] = piece
    out[...] = (cot[...].astype(F32) + dot_nt(held[...], w_edge[...])).astype(BF16)


def node_out_kernel(feats, idx, by_recv, w_send, w_recv, *refs):
    sums = refs[:2]
    crossed = refs[2 : 2 + 2 * (feats - 1)]
    out, held_send, held_recv = refs[-3:]
    rows, feat_width = sums[0].shape
    core, feat = idx[0], idx[2]
    mine = pl.ds(pl.multiple_of(feat * feat_width, 128), feat_width)
    held_recv[:, mine] = by_recv[...]
    for side in range(2):
        at = pl.ds(pl.multiple_of((core if side == 0 else 1 - core) * rows, 16), rows)
        held_send[at, mine] = sums[side][...]
        for k in range(1, feats):
            source = lax.rem(feat - k + feats, feats)
            there = pl.ds(pl.multiple_of(source * feat_width, 128), feat_width)
            held_send[at, there] = crossed[2 * (k - 1) + side][:rows, :]
            held_recv[at, there] = crossed[2 * (k - 1) + side][rows:, :]
    out[...] = dot_nt(held_send[...], w_send[...]) + dot_nt(held_recv[...], w_recv[...])


def body(
    node_latents, edge_latents, sender_latents, pre_hidden, pre_norm, norm_gain, w_in, w_out, senders, receivers,
    edge_cotangent, agg_cotangent,
):
    shards = lax.axis_size("nodes")
    feats = lax.axis_size("feat")
    core, shard, feat = (lax.axis_index(name) for name in ("chan", "nodes", "feat"))
    idx = jnp.stack([core, shard, feat]).astype(jnp.int32)
    nodes_dev, half_width = node_latents.shape
    edges = edge_latents.shape[0]
    feat_width = pre_hidden.shape[1]
    hidden_width = w_in.shape[2]
    half = edges // 2
    half_nodes = nodes_dev // 2
    scale = 1.0 / math.sqrt(edges * shards)

    def over_chan(x):
        return lax.ppermute(x, "chan", [(0, 1), (1, 0)])

    theirs = (1 - core) * half
    gap = -(2 * half + nodes_dev) % feat_width
    sent = jnp.concatenate(
        [
            lax.dynamic_slice_in_dim(pre_norm, theirs, half),
            lax.dynamic_slice_in_dim(edge_cotangent, theirs, half),
            agg_cotangent,
            jnp.zeros((gap, half_width), BF16),
            w_out,
        ]
    )
    got = over_chan(sent)
    gain_own = norm_gain.reshape(1, half_width)
    gain_sib = over_chan(gain_own)
    recv_row = receivers.reshape(1, edges)
    send_row = senders.reshape(1, edges)

    tile = 512
    steps = half // tile
    wide = (tile, half_width)
    narrow = (tile, feat_width)
    own = lambda i, s: (s[0] * steps + i, 0)
    pre_own, wo_own, gain_sum, small = pl.pallas_call(
        functools.partial(edge_kernel, nodes_dev, steps),
        grid_spec=pltpu.PrefetchScalarGridSpec(
            num_scalar_prefetch=1,
            grid=(steps,),
            in_specs=[
                pl.BlockSpec(wide, own),
                pl.BlockSpec(wide, lambda i, s: (i, 0)),
                pl.BlockSpec(wide, own),
                pl.BlockSpec(wide, lambda i, s: (steps + i, 0)),
                pl.BlockSpec(narrow, own),
                pl.BlockSpec((1, tile), lambda i, s: (0, s[0] * steps + i)),
                whole((nodes_dev, half_width)),
                pl.BlockSpec((nodes_dev, half_width), lambda i, s: (2 * half // nodes_dev, 0)),
                whole((1, half_width)),
                whole((1, half_width)),
                whole((feat_width, half_width)),
                pl.BlockSpec((feat_width, half_width), lambda i, s: ((2 * half + nodes_dev + gap) // feat_width, 0)),
            ],
            out_specs=[
                pl.BlockSpec(narrow, lambda i, s: (i, 0)),
                whole((half_width, feat_width)),
                whole((1, half_width)),
                whole((half_width + PAD, feat_width)),
            ],
            scratch_shapes=[
                pltpu.VMEM((half_width, feat_width), F32),
                pltpu.VMEM((1, half_width), F32),
                pltpu.VMEM((1, half_width), F32),
            ],
        ),
        out_shape=[
            jax.ShapeDtypeStruct((half, feat_width), BF16),
            jax.ShapeDtypeStruct((half_width, feat_width), F32),
            jax.ShapeDtypeStruct((1, half_width), F32),
            jax.ShapeDtypeStruct((half_width + PAD, feat_width), BF16),
        ],
        compiler_params=params(),
        cost_estimate=cost(4 * half * (nodes_dev + 2 * feat_width) * half_width, 10 * half * half_width),
        name="edge_norm",
    )(
        idx, pre_norm, got, edge_cotangent, got, pre_hidden, recv_row, agg_cotangent, got, gain_own, gain_sib,
        w_out, got,
    )

    pre_sib = over_chan(pre_own)
    small_sib = over_chan(small)
    crossed_own = [pre_own] + [lax.ppermute(pre_own, "feat", ring(feats, k)) for k in range(1, feats)]
    crossed_sib = [pre_sib] + [over_chan(x) for x in crossed_own[1:]]

    def by_edge(i, s):
        return jnp.where(i < steps, s[0] * steps + i, (1 - s[0]) * steps + i - steps)

    def first_half(i, s):
        return (jnp.minimum(i, steps - 1), 0)

    def second_half(i, s):
        return (jnp.maximum(i - steps, 0), 0)

    block = 4 * half_width // shards
    w_shapes = [
        jax.ShapeDtypeStruct((block + PAD, feat_width), F32 if k == 0 else BF16) for k in range(shards)
    ]
    s_shapes = [jax.ShapeDtypeStruct((half_nodes, feat_width), F32 if k == 0 else BF16) for k in range(shards)]
    pool_outs = w_shapes + s_shapes + [jax.ShapeDtypeStruct((nodes_dev, feat_width), BF16)]
    pooled = pl.pallas_call(
        functools.partial(pool_kernel, shards, 2 * steps),
        grid_spec=pltpu.PrefetchScalarGridSpec(
            num_scalar_prefetch=1,
            grid=(2 * steps,),
            in_specs=[
                pl.BlockSpec(narrow, first_half),
                pl.BlockSpec(narrow, second_half),
                pl.BlockSpec(wide, lambda i, s: (by_edge(i, s), 0)),
                pl.BlockSpec(wide, lambda i, s: (by_edge(i, s), 0)),
                whole((nodes_dev, half_width)),
                pl.BlockSpec((1, tile), lambda i, s: (0, by_edge(i, s))),
                pl.BlockSpec((1, tile), lambda i, s: (0, by_edge(i, s))),
                whole((half_width, feat_width)),
                whole((1, half_width)),
                whole((half_width + PAD, feat_width)),
            ],
            out_specs=[whole(x.shape) for x in pool_outs],
            scratch_shapes=[
                pltpu.VMEM((4 * half_width, feat_width), F32),
                pltpu.VMEM((shards * half_nodes, feat_width), F32),
                pltpu.VMEM((nodes_dev, feat_width), F32),
            ],
        ),
        out_shape=pool_outs,
        compiler_params=params(),
        cost_estimate=cost(
            2 * edges * feat_width * (nodes_dev + shards * half_nodes + 2 * half_width), 8 * edges * half_width
        ),
        name="pool",
    )(
        idx, pre_own, pre_sib, edge_latents, sender_latents, node_latents, send_row, recv_row, wo_own, gain_sum,
        small_sib,
    )
    w_parts, s_parts, by_recv = pooled[:shards], pooled[shards : 2 * shards], pooled[-1]

    w_got = [w_parts[0]] + [lax.ppermute(w_parts[k], "nodes", ring(shards, k)) for k in range(1, shards)]
    w_total = add_up(w_got)
    s_got = [s_parts[0]] + [lax.ppermute(s_parts[k], "nodes", ring(shards, k)) for k in range(1, shards)]
    w_all = [w_total] + [lax.ppermute(w_total, "nodes", ring(shards, k)) for k in range(1, shards)]
    smem = pl.BlockSpec(memory_space=pltpu.SMEM)
    vmem = pl.BlockSpec(memory_space=pltpu.VMEM)

    s_alone, s_both = pl.pallas_call(
        sum_send_kernel,
        in_specs=[smem] + [vmem] * (1 + shards),
        out_shape=[
            jax.ShapeDtypeStruct((half_nodes, feat_width), BF16),
            jax.ShapeDtypeStruct((nodes_dev, feat_width), BF16),
        ],
        compiler_params=params(),
        cost_estimate=cost(half_nodes * feat_width * shards, 10 * half_nodes * feat_width),
        name="sum_send",
    )(idx, by_recv, *s_got)
    s_cross = []
    for k in range(1, feats):
        from_feat = lax.ppermute(s_both, "feat", ring(feats, k))
        s_cross += [from_feat, over_chan(from_feat)]
    s_sib = over_chan(s_alone)

    edge_grad = pl.pallas_call(
        functools.partial(edge_out_kernel, feats, 2 * steps),
        grid_spec=pltpu.PrefetchScalarGridSpec(
            num_scalar_prefetch=1,
            grid=(2 * steps,),
            in_specs=[
                pl.BlockSpec(wide, lambda i, s: (by_edge(i, s), 0)),
                pl.BlockSpec((None, half_width, hidden_width), lambda i, s: (0, 0, 0)),
            ]
            + [pl.BlockSpec(narrow, first_half)] * feats
            + [pl.BlockSpec(narrow, second_half)] * feats,
            out_specs=pl.BlockSpec(wide, lambda i, s: (by_edge(i, s), 0)),
            scratch_shapes=[pltpu.VMEM((tile, hidden_width), BF16)],
        ),
        out_shape=jax.ShapeDtypeStruct((edges, half_width), BF16),
        compiler_params=params(),
        cost_estimate=cost(2 * edges * hidden_width * half_width, 8 * edges * half_width),
        name="edge_out",
    )(idx, edge_cotangent, w_in, *crossed_own, *crossed_sib)

    node_grad = pl.pallas_call(
        functools.partial(node_out_kernel, feats),
        grid=(1,),
        in_specs=[
            smem,
            whole((nodes_dev, feat_width)),
            pl.BlockSpec((None, half_width, hidden_width), lambda *_: (1, 0, 0)),
            pl.BlockSpec((None, half_width, hidden_width), lambda *_: (2, 0, 0)),
            whole((half_nodes, feat_width)),
            whole((half_nodes, feat_width)),
        ]
        + [whole((nodes_dev, feat_width))] * (2 * (feats - 1)),
        out_specs=whole((nodes_dev, half_width)),
        out_shape=jax.ShapeDtypeStruct((nodes_dev, half_width), F32),
        scratch_shapes=[
            pltpu.VMEM((nodes_dev, hidden_width), BF16),
            pltpu.VMEM((nodes_dev, hidden_width), BF16),
        ],
        compiler_params=params(),
        cost_estimate=cost(4 * nodes_dev * hidden_width * half_width, 8 * nodes_dev * hidden_width),
        name="node_out",
    )(idx, by_recv, w_in, w_in, s_alone, s_sib, *s_cross)

    w_in_grad, w_out_grad, gain_grad = pl.pallas_call(
        functools.partial(place_kernel, shards, scale),
        in_specs=[smem] + [vmem] * shards,
        out_shape=[
            jax.ShapeDtypeStruct((3, half_width, feat_width), F32),
            jax.ShapeDtypeStruct((feat_width, half_width), F32),
            jax.ShapeDtypeStruct((1, half_width), F32),
        ],
        scratch_shapes=[pltpu.VMEM((4 * half_width, feat_width), F32)],
        compiler_params=params(),
        cost_estimate=cost(8 * half_width * feat_width, 24 * half_width * feat_width),
        name="place",
    )(idx, *w_all)
    return (node_grad, edge_grad, w_in_grad, w_out_grad, gain_grad.reshape(half_width))


def solution(mesh):
    placed = (
        P(("groups", "nodes"), "chan"),
        P(("groups", "nodes"), "chan"),
        P(("groups", "nodes"), "chan"),
        P(("groups", "nodes"), "feat"),
        P(("groups", "nodes"), "chan"),
        P("chan"),
        P(None, "chan", None),
        P("feat", "chan"),
        P(("groups", "nodes")),
        P(("groups", "nodes")),
        P(("groups", "nodes"), "chan"),
        P(("groups", "nodes"), "chan"),
    )
    return jax.shard_map(
        body,
        mesh=mesh,
        in_specs=placed,
        out_specs=(
            P(("groups", "nodes"), "chan"),
            P(("groups", "nodes"), "chan"),
            P("groups", "chan", "feat"),
            P(("groups", "feat"), "chan"),
            P(("groups", "chan")),
        ),
        check_vma=False,
    )
```

time: 228 us -> 98.1 us (0.43)
  other arithmetic: 62.7 us -> 0.08 us
  waiting for transfers between devices: 85.1 us -> 47.5 us
  local copies, waits for them, and re-layouts: 29.7 us -> 6.18 us
  Pallas kernels: 0 us -> 21.9 us
  starting transfers between devices: 0.34 us -> 21.4 us
  blocking collectives: 19.7 us -> 0 us
  matrix products: 15.7 us -> 0 us
  between operations: 14 us -> 0.79 us
    ppermute x0 -> x18, waiting for transfers between devices: none -> 47.5 us  [the longest x1 17.3 us: body(): lax.ppermute(pre_own, 'feat', ring(feats, k))]
    psum x2 -> x0, waiting for transfers between devices: 39.2 us -> none  [the longest x1 25.9 us: body(): hidden_grad = lax.psum(contract_cols(norm_grad, w_out), 'chan')]
    scatter-add x2 -> x0, other arithmetic: 36.6 us -> none  [the longest x1 18.8 us: body(): jax.ops.segment_sum(sender_term.astype(jnp.float32), senders, num_segment...]
    all_gather x1 -> x0, waiting for transfers between devices: 26.6 us -> none  [body(): lax.all_gather(pre_grad, 'feat', axis=1, tiled=True)]
    gather x2 -> x0, local copies, waits for them, and re-layouts: 25.3 us -> none  [the longest x1 13 us: body(): gathered_nodes = node_latents[local_recv]]
    pallas_call x0 -> x7, Pallas kernels: none -> 21.9 us  [the longest x1 6.89 us: body(): pl.pallas_call(functools.partial(edge_kernel, nodes_dev, steps), grid_spe...]
    ppermute x0 -> x18, starting transfers between devices: none -> 21.4 us  [the longest x3 5.8 us: body(): lax.ppermute(s_parts[k], 'nodes', ring(shards, k))]
    psum x3 -> x0, blocking collectives: 19.7 us -> none  [the longest x1 12.5 us: body(): lax.psum((w_in_local, w_out_local, gain_local), 'nodes')]
  transfers between devices with their start and end apart: 4 -> 18, of which waited for: 4 -> 9; matrix products, arithmetic and copies ran while one was open for 24% -> 0% of each run, Pallas kernels for 0% -> 11%
where the time goes in v1:
time: 98.1 us; the launch traced here: 97.8 us
  waiting for transfers between devices  47.5 us (48%)
  Pallas kernels  21.9 us (22%)
  starting transfers between devices  21.4 us (22%)
  local copies, waits for them, and re-layouts  6.18 us (6%)
    ppermute x1, waiting for transfers between devices, body(): lax.ppermute(pre_own, 'feat', ring(feats, k))  17.3 us
    ppermute x3, waiting for transfers between devices, body(): lax.ppermute(w_total, 'nodes', ring(shards, k))  12.3 us
    ppermute x3, waiting for transfers between devices, body(): lax.ppermute(w_parts[k], 'nodes', ring(shards, k))  8.17 us
    pallas_call x1, Pallas kernels, body(): pl.pallas_call(functools.partial(edge_kernel, nodes_dev, steps), grid_spe...  6.89 us
    pallas_call x1, Pallas kernels, body(): pl.pallas_call(functools.partial(pool_kernel, shards, 2 * steps), grid_sp...  6.67 us
    ppermute x3, waiting for transfers between devices, body(): lax.ppermute(s_parts[k], 'nodes', ring(shards, k))  5.84 us
    ppermute x3, starting transfers between devices, body(): lax.ppermute(s_parts[k], 'nodes', ring(shards, k))  5.8 us
    unnamed x24, local copies, waits for them, and re-layouts  5.53 us
  transfers between devices with their start and end apart: 18, of which 9 were waited for; matrix products, arithmetic and copies ran while one was open for 0% of the time, Pallas kernels for 11%

profile of v1, /device:TPU:0, one launch (start us, length us, event | category | flops | bytes accessed | tf_op | source)
XLA Modules:
  0.0 97.8 jit_solution(6434427170134749622)
XLA Ops:
  0.6 0.0 copy-start
  0.6 0.0 copy-start.2
  0.7 0.0 copy-start.3
  0.7 0.0 copy-start.4
  0.7 0.0 copy-start.6
  0.7 0.0 copy-start.5
  0.7 2.2 %dynamic-slice_dynamic-update-slice_fusion.1 = bf16[3840,256]{1,0:T(8,128)(2,1)} fusion(bf16[3072,256]{1,0:T(8,128)(2,1)} %x_own.1, s32[]{:T(128)S(6)} %select_n.4), kind=kLoop, calls=%fused_computation.1 | loop fusion | bytes 1572868
  2.9 0.0 copy-done
  2.9 1.0 %dynamic-slice_dynamic-update-slice_fusion = bf16[3840,256]{1,0:T(8,128)(2,1)} fusion(bf16[3840,256]{1,0:T(8,128)(2,1)} %dynamic-slice_dynamic-update-slice_fusion.1, bf16[3072,256]{1,0:T(8,128)(2,1)S(1)} %copy-done, s32[]{:T(128)S(6)} %select_n.4), kind=kLoop, calls=%fused_computation | loop fusion | bytes 1572868
  3.9 1.6 %constant_dynamic-update-slice_fusion.1 = bf16[3840,256]{1,0:T(8,128)(2,1)} fusion(bf16[3840,256]{1,0:T(8,128)(2,1)} %dynamic-slice_dynamic-update-slice_fusion, bf16[384,256]{1,0:T(8,128)(2,1)} %agg_own.1), kind=kLoop, calls=%fused_computation.4 | loop fusion | bytes 393216
  5.6 0.6 broadcast_dynamic-update-slice_fusion
  6.2 0.0 copy-done.4
  6.2 0.7 constant_dynamic-update-slice_fusion
  6.8 0.5 collective-permute-start
  7.3 0.0 copy-done.6
  7.3 0.1 collective-permute-start.1
  7.4 0.1 pad_add_fusion.idx
  7.4 3.4 %collective-permute-done.1.gain_sib = f32[1,256]{1,0:T(1,128)S(1)} collective-permute-done((f32[1,256]{1,0:T(1,128)S(1)}, f32[1,256]{1,0:T(1,128)S(1)}, u32[]{:S(2)}, u32[]{:S(2)}) %collective-permute-start.1) | collective-permute-done | bytes 1056 | tf_op jit(solution)/shard_map/ppermute | solution.py:252
  10.8 0.4 collective-permute-done.x_sib.cot_sib.agg_sib.w_sib
  11.2 0.0 copy-done.2
  11.2 0.0 copy-done.3
  11.2 0.0 copy-done.5
  11.2 0.0 copy-start.8
  11.3 0.0 copy-start.9
  11.3 6.9 %edge_norm.1 = (bf16[1536,256]{1,0:T(8,128)(2,1)S(1)}, f32[256,256]{1,0:T(8,128)S(1)}, f32[1,256]{1,0:T(1,128)S(1)}, bf16[272,256]{1,0:T(8,128)(2,1)S(1)}) custom-call(s32[3]{0:T(128)S(1)} %pad_add_fusion.idx, bf16[3072,256]{1,0:T(8,128)(2,1)S(1)} %copy-done.2, bf16[3840,256]{1,0:T(8,128)(2,1)} %collective-permute-done.x_sib.cot_sib.agg_sib.w_sib, ...), custom_call_target="tpu_custom_call" | custom-call | flops 1409286144 | bytes 3932160 | tf_op jit(solution)/shard_map/edge_norm/pallas_call | solution.py:276
  18.2 2.9 %collective-permute-start.10 = (bf16[1536,256]{1,0:T(8,128)(2,1)S(1)}, bf16[1536,256]{1,0:T(8,128)(2,1)S(1)}, u32[]{:S(2)}, u32[]{:S(2)}) collective-permute-start(bf16[1536,256]{1,0:T(8,128)(2,1)S(1)} %get-tuple-element.23.g_own.refs_0_), channel_id=1, source_target_pairs={{0,2},{2,0},{1,3},{3,1},{4,6},{6,4},{5,7},{7,5},{8,10},{10,8},{9,1... | collective-permute-start | bytes 2359304 | tf_op jit(solution)/shard_map/ppermute | solution.py:323
  21.1 0.0 collective-permute-start.2
  21.1 0.5 collective-permute-start.3
  21.6 17.3 %collective-permute-done.10.refs_1_ = bf16[1536,256]{1,0:T(8,128)(2,1)S(1)} collective-permute-done((bf16[1536,256]{1,0:T(8,128)(2,1)S(1)}, bf16[1536,256]{1,0:T(8,128)(2,1)S(1)}, u32[]{:S(2)}, u32[]{:S(2)}) %collective-permute-start.10) | collective-permute-done | bytes 786464 | tf_op jit(solution)/shard_map/ppermute | solution.py:323
  38.9 0.0 collective-permute-start.11
  38.9 0.0 collective-permute-done.3.small
  38.9 0.0 collective-permute-done.2.g_sib.refs_2_
  39.0 6.7 %pool.1 = (f32[272,256]{1,0:T(8,128)S(1)}, bf16[272,256]{1,0:T(8,128)(2,1)S(1)}, bf16[272,256]{1,0:T(8,128)(2,1)S(1)}, bf16[272,256]{1,0:T(8,128)(2,1)S(1)}, f32...) custom-call(s32[3]{0:T(128)S(1)} %pad_add_fusion.idx, ...), custom_call_target="tpu_custom_call" | custom-call | flops 2617245696 | bytes 6291456 | tf_op jit(solution)/shard_map/pool/pallas_call | solution.py:341
  45.7 0.0 copy-start.1
  45.7 1.9 %collective-permute-start.4 = (bf16[192,256]{1,0:T(8,128)(2,1)S(1)}, bf16[192,256]{1,0:T(8,128)(2,1)S(1)}, u32[]{:S(2)}, u32[]{:S(2)}) collective-permute-start(bf16[192,256]{1,0:T(8,128)(2,1)S(1)} %get-tuple-element.29), channel_id=1, source_target_pairs={{0,4},{4,8},{8,12},{12,0},{1,5},{5,9},{9,13},{13,1},{2,6},{6,10},{... | collective-permute-start | bytes 294920 | tf_op jit(solution)/shard_map/ppermute | solution.py:379
  47.5 2.6 %collective-permute-start.5 = (bf16[192,256]{1,0:T(8,128)(2,1)S(1)}, bf16[192,256]{1,0:T(8,128)(2,1)S(1)}, u32[]{:S(2)}, u32[]{:S(2)}) collective-permute-start(bf16[192,256]{1,0:T(8,128)(2,1)S(1)} %get-tuple-element.30), channel_id=1, source_target_pairs={{0,8},{4,12},{8,0},{12,4},{1,9},{5,13},{9,1},{13,5},{2,10},{6,14},... | collective-permute-start | bytes 294920 | tf_op jit(solution)/shard_map/ppermute | solution.py:379
  50.1 1.3 %collective-permute-start.6 = (bf16[192,256]{1,0:T(8,128)(2,1)S(1)}, bf16[192,256]{1,0:T(8,128)(2,1)S(1)}, u32[]{:S(2)}, u32[]{:S(2)}) collective-permute-start(bf16[192,256]{1,0:T(8,128)(2,1)S(1)} %get-tuple-element.31), channel_id=1, source_target_pairs={{0,12},{4,0},{8,4},{12,8},{1,13},{5,1},{9,5},{13,9},{2,14},{6,2},{... | collective-permute-start | bytes 294920 | tf_op jit(solution)/shard_map/ppermute | solution.py:379
  51.5 1.9 %collective-permute-done.4.refs_1_ = bf16[192,256]{1,0:T(8,128)(2,1)S(1)} collective-permute-done((bf16[192,256]{1,0:T(8,128)(2,1)S(1)}, bf16[192,256]{1,0:T(8,128)(2,1)S(1)}, u32[]{:S(2)}, u32[]{:S(2)}) %collective-permute-start.4) | collective-permute-done | bytes 98336 | tf_op jit(solution)/shard_map/ppermute | solution.py:379
  53.3 4.0 %collective-permute-done.5.refs_2_ = bf16[192,256]{1,0:T(8,128)(2,1)S(1)} collective-permute-done((bf16[192,256]{1,0:T(8,128)(2,1)S(1)}, bf16[192,256]{1,0:T(8,128)(2,1)S(1)}, u32[]{:S(2)}, u32[]{:S(2)}) %collective-permute-start.5) | collective-permute-done | bytes 98336 | tf_op jit(solution)/shard_map/ppermute | solution.py:379
  57.3 0.0 collective-permute-done.6.refs_3_
  57.3 0.6 sum_send.1
  57.9 1.5 %collective-permute-start.8 = (bf16[384,256]{1,0:T(8,128)(2,1)S(1)}, bf16[384,256]{1,0:T(8,128)(2,1)S(1)}, u32[]{:S(2)}, u32[]{:S(2)}) collective-permute-start(bf16[384,256]{1,0:T(8,128)(2,1)S(1)} %get-tuple-element.33), channel_id=1, source_target_pairs={{0,2},{2,0},{1,3},{3,1},{4,6},{6,4},{5,7},{7,5},{8,10},{10,8},{9,1... | collective-permute-start | bytes 589832 | tf_op jit(solution)/shard_map/ppermute | solution.py:397
  59.5 2.6 %collective-permute-start.12 = (bf16[272,256]{1,0:T(8,128)(2,1)S(1)}, bf16[272,256]{1,0:T(8,128)(2,1)S(1)}, u32[]{:S(2)}, u32[]{:S(2)}) collective-permute-start(bf16[272,256]{1,0:T(8,128)(2,1)S(1)} %get-tuple-element.35), channel_id=1, source_target_pairs={{0,4},{4,8},{8,12},{12,0},{1,5},{5,9},{9,13},{13,1},{2,6},{6,10},{... | collective-permute-start | bytes 417800 | tf_op jit(solution)/shard_map/ppermute | solution.py:377
  62.1 1.6 %collective-permute-start.13 = (bf16[272,256]{1,0:T(8,128)(2,1)S(1)}, bf16[272,256]{1,0:T(8,128)(2,1)S(1)}, u32[]{:S(2)}, u32[]{:S(2)}) collective-permute-start(bf16[272,256]{1,0:T(8,128)(2,1)S(1)} %get-tuple-element.36), channel_id=1, source_target_pairs={{0,8},{4,12},{8,0},{12,4},{1,9},{5,13},{9,1},{13,5},{2,10},{6,14},... | collective-permute-start | bytes 417800 | tf_op jit(solution)/shard_map/ppermute | solution.py:377
  63.7 0.7 collective-permute-start.14
  64.4 3.5 %collective-permute-done.12.refs_1_ = bf16[272,256]{1,0:T(8,128)(2,1)S(1)} collective-permute-done((bf16[272,256]{1,0:T(8,128)(2,1)S(1)}, bf16[272,256]{1,0:T(8,128)(2,1)S(1)}, u32[]{:S(2)}, u32[]{:S(2)}) %collective-permute-start.12) | collective-permute-done | bytes 139296 | tf_op jit(solution)/shard_map/ppermute | solution.py:377
  67.9 4.7 %collective-permute-done.13.refs_2_ = bf16[272,256]{1,0:T(8,128)(2,1)S(1)} collective-permute-done((bf16[272,256]{1,0:T(8,128)(2,1)S(1)}, bf16[272,256]{1,0:T(8,128)(2,1)S(1)}, u32[]{:S(2)}, u32[]{:S(2)}) %collective-permute-start.13) | collective-permute-done | bytes 139296 | tf_op jit(solution)/shard_map/ppermute | solution.py:377
  72.6 0.0 collective-permute-done.14.refs_3_
  72.6 0.1 shard_map.155.refs_0_
  72.7 4.4 %collective-permute-start.17 = (bf16[272,256]{1,0:T(8,128)(2,1)S(1)}, bf16[272,256]{1,0:T(8,128)(2,1)S(1)}, u32[]{:S(2)}, u32[]{:S(2)}) collective-permute-start(bf16[272,256]{1,0:T(8,128)(2,1)S(1)} %shard_map.155.refs_0_), channel_id=1, source_target_pairs={{0,12},{4,0},{8,4},{12,8},{1,13},{5,1},{9,5},{13,9},{2,14},{6,2},{... | collective-permute-start | bytes 417800 | tf_op jit(solution)/shard_map/ppermute | solution.py:380
  77.1 0.0 collective-permute-done.8.refs_2_
  77.1 0.0 collective-permute-start.9
  77.1 0.5 collective-permute-start.16
  77.6 0.2 collective-permute-start.15
  77.8 3.3 %collective-permute-done.17.refs_3_ = bf16[272,256]{1,0:T(8,128)(2,1)S(1)} collective-permute-done((bf16[272,256]{1,0:T(8,128)(2,1)S(1)}, bf16[272,256]{1,0:T(8,128)(2,1)S(1)}, u32[]{:S(2)}, u32[]{:S(2)}) %collective-permute-start.17) | collective-permute-done | bytes 139296 | tf_op jit(solution)/shard_map/ppermute | solution.py:380
  81.1 0.0 collective-permute-start.7
  81.1 9.1 %collective-permute-done.16.refs_2_ = bf16[272,256]{1,0:T(8,128)(2,1)S(1)} collective-permute-done((bf16[272,256]{1,0:T(8,128)(2,1)S(1)}, bf16[272,256]{1,0:T(8,128)(2,1)S(1)}, u32[]{:S(2)}, u32[]{:S(2)}) %collective-permute-start.16) | collective-permute-done | bytes 139296 | tf_op jit(solution)/shard_map/ppermute | solution.py:380
  90.2 0.0 collective-permute-done.15.refs_1_
  90.2 1.7 %place.1 = (f32[3,256,256]{2,1,0:T(8,128)}, f32[256,256]{1,0:T(8,128)}, f32[1,256]{1,0:T(1,128)}) custom-call(s32[3]{0:T(128)S(1)} %pad_add_fusion.idx, bf16[272,256]{1,0:T(8,128)(2,1)S(1)} %shard_map.155.refs_0_, bf16[272,256]{1,0:T(8,128)(2,1)S(1)} %collective-permute-done.15.refs_1_, bf16[272,256]{1,0:T(8,128)(2,1)S(1)} %collective-permute-done.16.refs_2_, ...), custom_call_target="tpu_custom_call" | custom-call | flops 524288 | bytes 1572864 | tf_op jit(solution)/shard_map/place/pallas_call | solution.py:444
  91.9 0.0 collective-permute-done.7.refs_1_
  91.9 0.0 collective-permute-done.9.refs_3_
  91.9 1.7 %node_out.1 = f32[384,256]{1,0:T(8,128)} custom-call(s32[3]{0:T(128)S(1)} %pad_add_fusion.idx, bf16[384,256]{1,0:T(8,128)(2,1)S(1)} %get-tuple-element.27.by_recv, bf16[3,256,512]{2,1,0:T(8,128)(2,1)S(1)} %copy-done.1, bf16[3,256,512]{2,1,0:T(8,128)(2,1)S(1)} %copy-done.1, bf16[192,256]{1,0:T(8,128)(2,1)S(1)} %get-tuple-element.32.refs_0_, ...), custom_call_target="tpu_custom_call" | custom-call | flops 201326592 | bytes 1572864 | tf_op jit(solution)/shard_map/node_out/pallas_call | solution.py:421
  93.6 0.0 collective-permute-done.11.refs_3_
  93.6 4.2 %edge_out.1 = bf16[3072,256]{1,0:T(8,128)(2,1)} custom-call(s32[3]{0:T(128)S(1)} %pad_add_fusion.idx, bf16[3072,256]{1,0:T(8,128)(2,1)S(1)} %copy-done, bf16[3,256,512]{2,1,0:T(8,128)(2,1)S(1)} %copy-done.1, bf16[1536,256]{1,0:T(8,128)(2,1)S(1)} %get-tuple-element.23.g_own.refs_0_, bf16[1536,256]{1,0:T(8,128)(2,1)S(1)} %collective-permute-done.10.refs_1_, ...), custom_call_target="tpu_custom_call" | custom-call | flops 805306368 | bytes 6291456 | tf_op jit(solution)/shard_map/edge_out/pallas_call | solution.py:401
  (5 shorter events, 0.0 us)
Async XLA Ops:
  0.6 2.3 %copy-start = (bf16[3072,256]{1,0:T(8,128)(2,1)S(1)}, bf16[3072,256]{1,0:T(8,128)(2,1)}, u32[]{:S(2)}) copy-start(bf16[3072,256]{1,0:T(8,128)(2,1)} %cot.1) | copy-start | bytes 4718596
  0.6 10.6 %copy-start.2 = (bf16[3072,256]{1,0:T(8,128)(2,1)S(1)}, bf16[3072,256]{1,0:T(8,128)(2,1)}, u32[]{:S(2)}) copy-start(bf16[3072,256]{1,0:T(8,128)(2,1)} %x_own.1) | copy-start | bytes 4718596
  0.7 10.6 %copy-start.3 = (bf16[384,256]{1,0:T(8,128)(2,1)S(1)}, bf16[384,256]{1,0:T(8,128)(2,1)}, u32[]{:S(2)}) copy-start(bf16[384,256]{1,0:T(8,128)(2,1)} %agg_own.1) | copy-start | bytes 589828
  0.7 5.5 %copy-start.4 = (bf16[256,256]{1,0:T(8,128)(2,1)S(1)}, bf16[256,256]{1,0:T(8,128)(2,1)}, u32[]{:S(2)}) copy-start(bf16[256,256]{1,0:T(8,128)(2,1)} %w_own.1) | copy-start | bytes 393220
  0.7 6.6 %copy-start.6 = (f32[256]{0:T(256)S(1)}, f32[256]{0:T(256)}, u32[]{:S(2)}) copy-start(f32[256]{0:T(256)} %param.17) | copy-start | bytes 3076
  0.7 10.6 %copy-start.5 = (s32[3072]{0:T(1024)S(1)}, s32[3072]{0:T(1024)}, u32[]{:S(2)}) copy-start(s32[3072]{0:T(1024)} %param.21) | copy-start | bytes 36868
  6.8 4.4 %collective-permute-start = (bf16[3840,256]{1,0:T(8,128)(2,1)}, bf16[3840,256]{1,0:T(8,128)(2,1)}, u32[]{:S(2)}, u32[]{:S(2)}) collective-permute-start(bf16[3840,256]{1,0:T(8,128)(2,1)} %constant_dynamic-update-slice_fusion), channel_id=1, source_target_pairs={{0,1},{1,0},{2,3},{3,2},{4,5},{5,4},{6,7},{7,6},{8,9},{9,8},{10,11... | collective-permute-start | bytes 5898248 | tf_op jit(solution)/shard_map/ppermute | solution.py:252
  7.3 3.5 %collective-permute-start.1 = (f32[1,256]{1,0:T(1,128)S(1)}, f32[1,256]{1,0:T(1,128)S(1)}, u32[]{:S(2)}, u32[]{:S(2)}) collective-permute-start(f32[1,256]{1,0:T(1,128)S(1)} %bitcast.9), channel_id=1, source_target_pairs={{0,1},{1,0},{2,3},{3,2},{4,5},{5,4},{6,7},{7,6},{8,9},{9,8},{10,11... | collective-permute-start | bytes 3080 | tf_op jit(solution)/shard_map/ppermute | solution.py:252
  11.2 27.7 %copy-start.7 = (bf16[3072,256]{1,0:T(8,128)(2,1)S(1)}, bf16[3072,256]{1,0:T(8,128)(2,1)}, u32[]{:S(2)}) copy-start(bf16[3072,256]{1,0:T(8,128)(2,1)} %edge_lat.1) | copy-start | bytes 4718596
  11.2 27.7 %copy-start.8 = (bf16[384,256]{1,0:T(8,128)(2,1)S(1)}, bf16[384,256]{1,0:T(8,128)(2,1)}, u32[]{:S(2)}) copy-start(bf16[384,256]{1,0:T(8,128)(2,1)} %node_lat.1) | copy-start | bytes 589828
  11.3 27.7 %copy-start.9 = (s32[3072]{0:T(1024)S(1)}, s32[3072]{0:T(1024)}, u32[]{:S(2)}) copy-start(s32[3072]{0:T(1024)} %param.20) | copy-start | bytes 36868
  18.2 20.8 %collective-permute-start.10 = (bf16[1536,256]{1,0:T(8,128)(2,1)S(1)}, bf16[1536,256]{1,0:T(8,128)(2,1)S(1)}, u32[]{:S(2)}, u32[]{:S(2)}) collective-permute-start(bf16[1536,256]{1,0:T(8,128)(2,1)S(1)} %get-tuple-element.23.g_own.refs_0_), channel_id=1, source_target_pairs={{0,2},{2,0},{1,3},{3,1},{4,6},{6,4},{5,7},{7,5},{8,10},{10,8},{9,1... | collective-permute-start | bytes 2359304 | tf_op jit(solution)/shard_map/ppermute | solution.py:323
  21.1 17.8 %collective-permute-start.2 = (bf16[1536,256]{1,0:T(8,128)(2,1)S(1)}, bf16[1536,256]{1,0:T(8,128)(2,1)S(1)}, u32[]{:S(2)}, u32[]{:S(2)}) collective-permute-start(bf16[1536,256]{1,0:T(8,128)(2,1)S(1)} %get-tuple-element.23.g_own.refs_0_), channel_id=1, source_target_pairs={{0,1},{1,0},{2,3},{3,2},{4,5},{5,4},{6,7},{7,6},{8,9},{9,8},{10,11... | collective-permute-start | bytes 2359304 | tf_op jit(solution)/shard_map/ppermute | solution.py:252
  21.1 17.8 %collective-permute-start.3 = (bf16[272,256]{1,0:T(8,128)(2,1)S(1)}, bf16[272,256]{1,0:T(8,128)(2,1)S(1)}, u32[]{:S(2)}, u32[]{:S(2)}) collective-permute-start(bf16[272,256]{1,0:T(8,128)(2,1)S(1)} %get-tuple-element.26), channel_id=1, source_target_pairs={{0,1},{1,0},{2,3},{3,2},{4,5},{5,4},{6,7},{7,6},{8,9},{9,8},{10,11... | collective-permute-start | bytes 417800 | tf_op jit(solution)/shard_map/ppermute | solution.py:252
  38.9 54.6 %collective-permute-start.11 = (bf16[1536,256]{1,0:T(8,128)(2,1)S(1)}, bf16[1536,256]{1,0:T(8,128)(2,1)S(1)}, u32[]{:S(2)}, u32[]{:S(2)}) collective-permute-start(bf16[1536,256]{1,0:T(8,128)(2,1)S(1)} %collective-permute-done.10.refs_1_), channel_id=1, source_target_pairs={{0,1},{1,0},{2,3},{3,2},{4,5},{5,4},{6,7},{7,6},{8,9},{9,8},{10,11... | collective-permute-start | bytes 2359304 | tf_op jit(solution)/shard_map/ppermute | solution.py:252
  45.7 46.2 %copy-start.1 = (bf16[3,256,512]{2,1,0:T(8,128)(2,1)S(1)}, bf16[3,256,512]{2,1,0:T(8,128)(2,1)}, u32[]{:S(2)}) copy-start(bf16[3,256,512]{2,1,0:T(8,128)(2,1)} %w_edge.1) | copy-start | bytes 2359300
  45.7 7.7 %collective-permute-start.4 = (bf16[192,256]{1,0:T(8,128)(2,1)S(1)}, bf16[192,256]{1,0:T(8,128)(2,1)S(1)}, u32[]{:S(2)}, u32[]{:S(2)}) collective-permute-start(bf16[192,256]{1,0:T(8,128)(2,1)S(1)} %get-tuple-element.29), channel_id=1, source_target_pairs={{0,4},{4,8},{8,12},{12,0},{1,5},{5,9},{9,13},{13,1},{2,6},{6,10},{... | collective-permute-start | bytes 294920 | tf_op jit(solution)/shard_map/ppermute | solution.py:379
  47.5 9.8 %collective-permute-start.5 = (bf16[192,256]{1,0:T(8,128)(2,1)S(1)}, bf16[192,256]{1,0:T(8,128)(2,1)S(1)}, u32[]{:S(2)}, u32[]{:S(2)}) collective-permute-start(bf16[192,256]{1,0:T(8,128)(2,1)S(1)} %get-tuple-element.30), channel_id=1, source_target_pairs={{0,8},{4,12},{8,0},{12,4},{1,9},{5,13},{9,1},{13,5},{2,10},{6,14},... | collective-permute-start | bytes 294920 | tf_op jit(solution)/shard_map/ppermute | solution.py:379
  50.1 7.2 %collective-permute-start.6 = (bf16[192,256]{1,0:T(8,128)(2,1)S(1)}, bf16[192,256]{1,0:T(8,128)(2,1)S(1)}, u32[]{:S(2)}, u32[]{:S(2)}) collective-permute-start(bf16[192,256]{1,0:T(8,128)(2,1)S(1)} %get-tuple-element.31), channel_id=1, source_target_pairs={{0,12},{4,0},{8,4},{12,8},{1,13},{5,1},{9,5},{13,9},{2,14},{6,2},{... | collective-permute-start | bytes 294920 | tf_op jit(solution)/shard_map/ppermute | solution.py:379
  57.9 19.2 %collective-permute-start.8 = (bf16[384,256]{1,0:T(8,128)(2,1)S(1)}, bf16[384,256]{1,0:T(8,128)(2,1)S(1)}, u32[]{:S(2)}, u32[]{:S(2)}) collective-permute-start(bf16[384,256]{1,0:T(8,128)(2,1)S(1)} %get-tuple-element.33), channel_id=1, source_target_pairs={{0,2},{2,0},{1,3},{3,1},{4,6},{6,4},{5,7},{7,5},{8,10},{10,8},{9,1... | collective-permute-start | bytes 589832 | tf_op jit(solution)/shard_map/ppermute | solution.py:397
  59.5 8.5 %collective-permute-start.12 = (bf16[272,256]{1,0:T(8,128)(2,1)S(1)}, bf16[272,256]{1,0:T(8,128)(2,1)S(1)}, u32[]{:S(2)}, u32[]{:S(2)}) collective-permute-start(bf16[272,256]{1,0:T(8,128)(2,1)S(1)} %get-tuple-element.35), channel_id=1, source_target_pairs={{0,4},{4,8},{8,12},{12,0},{1,5},{5,9},{9,13},{13,1},{2,6},{6,10},{... | collective-permute-start | bytes 417800 | tf_op jit(solution)/shard_map/ppermute | solution.py:377
  62.1 10.5 %collective-permute-start.13 = (bf16[272,256]{1,0:T(8,128)(2,1)S(1)}, bf16[272,256]{1,0:T(8,128)(2,1)S(1)}, u32[]{:S(2)}, u32[]{:S(2)}) collective-permute-start(bf16[272,256]{1,0:T(8,128)(2,1)S(1)} %get-tuple-element.36), channel_id=1, source_target_pairs={{0,8},{4,12},{8,0},{12,4},{1,9},{5,13},{9,1},{13,5},{2,10},{6,14},... | collective-permute-start | bytes 417800 | tf_op jit(solution)/shard_map/ppermute | solution.py:377
  63.7 8.9 %collective-permute-start.14 = (bf16[272,256]{1,0:T(8,128)(2,1)S(1)}, bf16[272,256]{1,0:T(8,128)(2,1)S(1)}, u32[]{:S(2)}, u32[]{:S(2)}) collective-permute-start(bf16[272,256]{1,0:T(8,128)(2,1)S(1)} %get-tuple-element.37), channel_id=1, source_target_pairs={{0,12},{4,0},{8,4},{12,8},{1,13},{5,1},{9,5},{13,9},{2,14},{6,2},{... | collective-permute-start | bytes 417800 | tf_op jit(solution)/shard_map/ppermute | solution.py:377
  72.7 8.4 %collective-permute-start.17 = (bf16[272,256]{1,0:T(8,128)(2,1)S(1)}, bf16[272,256]{1,0:T(8,128)(2,1)S(1)}, u32[]{:S(2)}, u32[]{:S(2)}) collective-permute-start(bf16[272,256]{1,0:T(8,128)(2,1)S(1)} %shard_map.155.refs_0_), channel_id=1, source_target_pairs={{0,12},{4,0},{8,4},{12,8},{1,13},{5,1},{9,5},{13,9},{2,14},{6,2},{... | collective-permute-start | bytes 417800 | tf_op jit(solution)/shard_map/ppermute | solution.py:380
  77.1 14.8 %collective-permute-start.9 = (bf16[384,256]{1,0:T(8,128)(2,1)S(1)}, bf16[384,256]{1,0:T(8,128)(2,1)S(1)}, u32[]{:S(2)}, u32[]{:S(2)}) collective-permute-start(bf16[384,256]{1,0:T(8,128)(2,1)S(1)} %collective-permute-done.8.refs_2_), channel_id=1, source_target_pairs={{0,1},{1,0},{2,3},{3,2},{4,5},{5,4},{6,7},{7,6},{8,9},{9,8},{10,11... | collective-permute-start | bytes 589832 | tf_op jit(solution)/shard_map/ppermute | solution.py:252
  77.1 13.1 %collective-permute-start.16 = (bf16[272,256]{1,0:T(8,128)(2,1)S(1)}, bf16[272,256]{1,0:T(8,128)(2,1)S(1)}, u32[]{:S(2)}, u32[]{:S(2)}) collective-permute-start(bf16[272,256]{1,0:T(8,128)(2,1)S(1)} %shard_map.155.refs_0_), channel_id=1, source_target_pairs={{0,8},{4,12},{8,0},{12,4},{1,9},{5,13},{9,1},{13,5},{2,10},{6,14},... | collective-permute-start | bytes 417800 | tf_op jit(solution)/shard_map/ppermute | solution.py:380
  77.6 12.5 %collective-permute-start.15 = (bf16[272,256]{1,0:T(8,128)(2,1)S(1)}, bf16[272,256]{1,0:T(8,128)(2,1)S(1)}, u32[]{:S(2)}, u32[]{:S(2)}) collective-permute-start(bf16[272,256]{1,0:T(8,128)(2,1)S(1)} %shard_map.155.refs_0_), channel_id=1, source_target_pairs={{0,4},{4,8},{8,12},{12,0},{1,5},{5,9},{9,13},{13,1},{2,6},{6,10},{... | collective-permute-start | bytes 417800 | tf_op jit(solution)/shard_map/ppermute | solution.py:380
  81.1 10.8 %collective-permute-start.7 = (bf16[192,256]{1,0:T(8,128)(2,1)S(1)}, bf16[192,256]{1,0:T(8,128)(2,1)S(1)}, u32[]{:S(2)}, u32[]{:S(2)}) collective-permute-start(bf16[192,256]{1,0:T(8,128)(2,1)S(1)} %get-tuple-element.32.refs_0_), channel_id=1, source_target_pairs={{0,1},{1,0},{2,3},{3,2},{4,5},{5,4},{6,7},{7,6},{8,9},{9,8},{10,11... | collective-permute-start | bytes 294920 | tf_op jit(solution)/shard_map/ppermute | solution.py:252

commit v2 on v1

v2 whole, which is shorter than its diff:
```python
import functools
import math

import jax
import jax.numpy as jnp
from jax import lax
from jax.experimental import pallas as pl
from jax.experimental.pallas import tpu as pltpu
from jax.sharding import PartitionSpec as P

F32 = jnp.float32
BF16 = jnp.bfloat16
PAD = 16


def dot_nn(a, b):
    return lax.dot_general(a, b, (((1,), (0,)), ((), ())), preferred_element_type=F32)


def dot_nt(a, b):
    return lax.dot_general(a, b, (((1,), (1,)), ((), ())), preferred_element_type=F32)


def dot_tn(a, b):
    return lax.dot_general(a, b, (((0,), (0,)), ((), ())), preferred_element_type=F32)


def params(mib=48):
    return pltpu.CompilerParams(vmem_limit_bytes=mib * 1024 * 1024)


def cost(flops, nbytes):
    return pl.CostEstimate(flops=int(flops), bytes_accessed=int(nbytes), transcendentals=0)


def whole(shape):
    return pl.BlockSpec(shape, lambda *_: (0,) * len(shape))


def in_hbm(x):
    return pltpu.with_memory_space_constraint(x, pltpu.HBM)


def ring(size, step):
    return [(i, (i + step) % size) for i in range(size)]


def split_rows(row, width):
    parts = [row[:, j * width : (j + 1) * width] for j in range(row.shape[1] // width)]
    parts.append(jnp.zeros((PAD - len(parts), width), row.dtype))
    return jnp.concatenate(parts, axis=0)


def edge_kernel(steps, idx, *refs):
    small_in, tiled_in = refs[:7], refs[7:12]
    pre_grad, wo_own, gain_out, small = refs[12:16]
    small_held, tiled_held = refs[16:23], refs[23:28]
    acc_sib, small_sems, tiled_sems = refs[28:]
    half, feat_width = pre_grad.shape
    rows = half // steps
    first = pl.multiple_of(idx[0] * half, 128)

    def tile_copies(step):
        out = []
        for j, (src, dst) in enumerate(zip(tiled_in, tiled_held)):
            here = pl.ds(step * rows, rows)
            there = pl.ds(pl.multiple_of(first + step * rows, 128), rows)
            out.append(pltpu.make_async_copy(src.at[there, :], dst.at[here, :], tiled_sems.at[j, step]))
        return out

    small_copies = []
    for j, (src, dst) in enumerate(zip(small_in, small_held)):
        if j == 0:
            src = src.at[:, pl.ds(first, half)]
        small_copies.append(pltpu.make_async_copy(src, dst, small_sems.at[j]))
    tiles = [tile_copies(step) for step in range(steps)]
    for copy in small_copies[:3] + tiles[0] + small_copies[3:]:
        copy.start()
    for copies in tiles[1:]:
        for copy in copies:
            copy.start()
    for copy in small_copies:
        copy.wait()

    recv, agg_own, agg_sib, gain_own, gain_sib, w_own, w_sib = small_held
    nodes_dev, half_width = agg_own.shape
    width = 2 * half_width
    first_node = idx[1] * nodes_dev
    gsum_own = jnp.zeros((1, half_width), F32)
    gsum_sib = jnp.zeros((1, half_width), F32)

    def row_mean(a, b):
        return jnp.sum(a + b, axis=1, keepdims=True) * (1.0 / width)

    for step in range(steps):
        at = slice(step * rows, (step + 1) * rows)
        column = jnp.transpose(jnp.broadcast_to(recv[:, at], (8, rows)))[:, :1] - first_node
        picks = lax.broadcasted_iota(jnp.int32, (rows, nodes_dev), 1) == column
        picks = jnp.where(picks, 1.0, 0.0).astype(BF16)
        for copy in tiles[step]:
            copy.wait()
        x_own, x_sib, cot_own, cot_sib, hid = (ref[at, :] for ref in tiled_held)
        v_own = x_own.astype(F32)
        v_sib = x_sib.astype(F32)
        mean = row_mean(v_own, v_sib)
        v_own = v_own - mean
        v_sib = v_sib - mean
        inv = lax.rsqrt(row_mean(v_own * v_own, v_sib * v_sib) + 1e-05)
        n_own = v_own * inv
        n_sib = v_sib * inv
        up_own = cot_own.astype(F32) + dot_nn(picks, agg_own[...])
        up_sib = cot_sib.astype(F32) + dot_nn(picks, agg_sib[...])
        wt_own = gain_own[...] * up_own
        wt_sib = gain_sib[...] * up_sib
        mean_first = row_mean(wt_own, wt_sib)
        mean_cross = row_mean(wt_own * n_own, wt_sib * n_sib)
        g_own = (inv * (wt_own - mean_first - n_own * mean_cross)).astype(BF16)
        g_sib = (inv * (wt_sib - mean_first - n_sib * mean_cross)).astype(BF16)
        hidden = dot_nt(g_own, w_own[...]) + dot_nt(g_sib, w_sib[...])
        value = hid.astype(F32)
        sig = 1.0 / (1.0 + jnp.exp(-value))
        act = (value * sig).astype(BF16)
        pre_grad[at, :] = (hidden * (sig * (1.0 + value * (1.0 - sig)))).astype(BF16)
        if step == 0:
            wo_own[...] = dot_tn(g_own, act)
            acc_sib[...] = dot_tn(g_sib, act)
        else:
            wo_own[...] += dot_tn(g_own, act)
            acc_sib[...] += dot_tn(g_sib, act)
        gsum_own = gsum_own + jnp.sum(up_own * n_own, axis=0, keepdims=True)
        gsum_sib = gsum_sib + jnp.sum(up_sib * n_sib, axis=0, keepdims=True)

    gain_out[...] = gsum_own
    small[:half_width, :] = acc_sib[...].astype(BF16)
    small[half_width:, :] = split_rows(gsum_sib, feat_width).astype(BF16)


def pool_kernel(
    shards, steps, idx, g_own, g_sib, edge_lat, send_lat, node_lat, senders, recv, wo_own, gain_own, small, *rest
):
    outs = rest[:shards]
    recv_out, grads, pooled, by_recv = rest[shards:]
    step = pl.program_id(0)
    core, shard = idx[0], idx[1]
    nodes_dev, half_width = node_lat.shape
    half_nodes = nodes_dev // 2
    rows, feat_width = g_own.shape

    @pl.when(step == 0)
    def _():
        grads[...] = jnp.zeros_like(grads)
        pooled[...] = jnp.zeros_like(pooled)
        by_recv[...] = jnp.zeros_like(by_recv)

    grad = jnp.where(step < steps // 2, g_own[...], g_sib[...])
    node_id = lax.broadcasted_iota(jnp.int32, (nodes_dev, rows), 0)
    picks = jnp.where(node_id + shard * nodes_dev == recv[...], 1.0, 0.0).astype(BF16)
    by_recv[...] += dot_nn(picks, grad)
    half_id = lax.broadcasted_iota(jnp.int32, (half_nodes, rows), 0) + core * half_nodes
    for dest in range(shards):
        picks = jnp.where(half_id + dest * nodes_dev == senders[...], 1.0, 0.0).astype(BF16)
        pooled[dest * half_nodes : (dest + 1) * half_nodes, :] += dot_nn(picks, grad)
    grads[:half_width, :] += dot_tn(edge_lat[...], grad)
    grads[half_width : 2 * half_width, :] += dot_tn(send_lat[...], grad)

    @pl.when(step == steps - 1)
    def _():
        sums = by_recv[...]
        high = sums.astype(BF16)
        low = (sums - high.astype(F32)).astype(BF16)
        grads[2 * half_width : 3 * half_width, :] = dot_tn(node_lat[...], high) + dot_tn(node_lat[...], low)
        grads[3 * half_width :, :] = wo_own[...] + small[:half_width, :].astype(F32)
        gain = split_rows(gain_own[...], feat_width) + small[half_width:, :].astype(F32)
        recv_out[...] = high
        block = 4 * half_width // shards
        for k in range(shards):
            dest = lax.rem(shard + k, shards)
            kind = outs[k].dtype
            w_rows = grads[pl.ds(pl.multiple_of(dest * block, 16), block), :]
            outs[k][:block, :] = w_rows.astype(kind)
            outs[k][block : block + PAD, :] = gain.astype(kind)
            s_rows = pooled[pl.ds(pl.multiple_of(dest * half_nodes, 16), half_nodes), :]
            outs[k][block + PAD :, :] = s_rows.astype(kind)


def sum_kernel(shards, *refs):
    w_total, s_total = refs[-2:]
    total = refs[0][...].astype(F32)
    for ref in refs[1:shards]:
        total = total + ref[...].astype(F32)
    rows = w_total.shape[0]
    w_total[...] = total[:rows].astype(BF16)
    s_total[...] = total[rows:].astype(BF16)


def place_kernel(shards, scale, idx, *refs):
    totals = refs[:shards]
    w_in_grad, w_out_grad, gain_grad, held = refs[-4:]
    half_width, feat_width = w_in_grad.shape[1:]
    block = 4 * half_width // shards
    for k in range(shards):
        source = lax.rem(idx[1] - k + shards, shards)
        held[pl.ds(pl.multiple_of(source * block, 16), block), :] = totals[k][:block, :].astype(F32) * scale

        @pl.when(source == 0)
        def _(k=k):
            rows = totals[k][block:, :].astype(F32) * scale
            for j in range(half_width // feat_width):
                gain_grad[:, j * feat_width : (j + 1) * feat_width] = rows[j : j + 1, :]

    for k in range(3):
        w_in_grad[k] = held[k * half_width : (k + 1) * half_width, :]
    w_out_grad[...] = jnp.transpose(held[3 * half_width :, :])


def edge_out_kernel(feats, steps, idx, cot, w_edge, *refs):
    own = refs[:feats]
    sib = refs[feats : 2 * feats]
    out, token, held = refs[2 * feats :]
    token[...] = jnp.zeros_like(token)
    step = pl.program_id(0)
    feat_width = own[0].shape[1]
    for k in range(feats):
        source = lax.rem(idx[2] - k + feats, feats)
        piece = jnp.where(step < steps // 2, own[k][...], sib[k][...])
        held[:, pl.ds(pl.multiple_of(source * feat_width, 128), feat_width)] = piece
    out[...] = (cot[...].astype(F32) + dot_nt(held[...], w_edge[...])).astype(BF16)


def node_out_kernel(feats, idx, w_send, w_recv, *refs):
    by_recv = refs[:feats]
    sums = refs[feats : 3 * feats]
    out, held_send, held_recv = refs[-3:]
    rows, feat_width = sums[0].shape
    for k in range(feats):
        source = lax.rem(idx[2] - k + feats, feats)
        there = pl.ds(pl.multiple_of(source * feat_width, 128), feat_width)
        held_recv[:, there] = by_recv[k][...]
        for side in range(2):
            at = pl.ds(pl.multiple_of((idx[0] if side == 0 else 1 - idx[0]) * rows, 16), rows)
            held_send[at, there] = sums[2 * k + side][...]
    out[...] = dot_nt(held_send[...], w_send[...]) + dot_nt(held_recv[...], w_recv[...])


def body(
    node_latents, edge_latents, sender_latents, pre_hidden, pre_norm, norm_gain, w_in, w_out, senders, receivers,
    edge_cotangent, agg_cotangent,
):
    shards = lax.axis_size("nodes")
    feats = lax.axis_size("feat")
    core, shard, feat = (lax.axis_index(name) for name in ("chan", "nodes", "feat"))
    idx = jnp.stack([core, shard, feat]).astype(jnp.int32)
    nodes_dev, half_width = node_latents.shape
    edges = edge_latents.shape[0]
    feat_width = pre_hidden.shape[1]
    hidden_width = w_in.shape[2]
    half = edges // 2
    half_nodes = nodes_dev // 2
    scale = 1.0 / math.sqrt(edges * shards)

    def over_chan(x):
        return lax.ppermute(x, "chan", [(0, 1), (1, 0)])

    pre_norm_sib = over_chan(pre_norm)
    cot_sib = over_chan(edge_cotangent)
    agg_sib = over_chan(agg_cotangent)
    w_out_sib = over_chan(w_out)
    gain_own = norm_gain.reshape(1, half_width)
    gain_sib = over_chan(gain_own)
    recv_row = receivers.reshape(1, edges)
    send_row = senders.reshape(1, edges)

    tile = 768
    steps = half // tile
    wide = (tile, half_width)
    narrow = (tile, feat_width)
    smem = pl.BlockSpec(memory_space=pltpu.SMEM)
    vmem = pl.BlockSpec(memory_space=pltpu.VMEM)
    edge_steps = 3
    pre_own, wo_own, gain_sum, small = pl.pallas_call(
        functools.partial(edge_kernel, edge_steps),
        in_specs=[smem] + [pl.BlockSpec(memory_space=pl.ANY)] * 12,
        out_specs=[vmem] * 4,
        out_shape=[
            jax.ShapeDtypeStruct((half, feat_width), BF16),
            jax.ShapeDtypeStruct((half_width, feat_width), F32),
            jax.ShapeDtypeStruct((1, half_width), F32),
            jax.ShapeDtypeStruct((half_width + PAD, feat_width), BF16),
        ],
        scratch_shapes=[
            pltpu.VMEM((1, half), jnp.int32),
            pltpu.VMEM((nodes_dev, half_width), BF16),
            pltpu.VMEM((nodes_dev, half_width), BF16),
            pltpu.VMEM((1, half_width), F32),
            pltpu.VMEM((1, half_width), F32),
            pltpu.VMEM((feat_width, half_width), BF16),
            pltpu.VMEM((feat_width, half_width), BF16),
            pltpu.VMEM((half, half_width), BF16),
            pltpu.VMEM((half, half_width), BF16),
            pltpu.VMEM((half, half_width), BF16),
            pltpu.VMEM((half, half_width), BF16),
            pltpu.VMEM((half, feat_width), BF16),
            pltpu.VMEM((half_width, feat_width), F32),
            pltpu.SemaphoreType.DMA((7,)),
            pltpu.SemaphoreType.DMA((5, edge_steps)),
        ],
        compiler_params=params(),
        cost_estimate=cost(4 * half * (nodes_dev + 2 * feat_width) * half_width, 10 * half * half_width),
        name="edge_norm",
    )(
        idx, in_hbm(recv_row), in_hbm(agg_cotangent), agg_sib, in_hbm(gain_own), gain_sib, in_hbm(w_out), w_out_sib,
        in_hbm(pre_norm), in_hbm(pre_norm_sib), in_hbm(edge_cotangent), in_hbm(cot_sib), in_hbm(pre_hidden),
    )

    pre_sib = over_chan(pre_own)
    small_sib = over_chan(small)
    crossed_own = [pre_own] + [lax.ppermute(pre_own, "feat", ring(feats, k)) for k in range(1, feats)]

    def by_edge(i, s):
        return jnp.where(i < steps, s[0] * steps + i, (1 - s[0]) * steps + i - steps)

    def first_half(i, s):
        return (jnp.minimum(i, steps - 1), 0)

    def second_half(i, s):
        return (jnp.maximum(i - steps, 0), 0)

    block = 4 * half_width // shards
    rows_out = block + PAD + half_nodes
    pool_outs = [jax.ShapeDtypeStruct((rows_out, feat_width), F32 if k == 0 else BF16) for k in range(shards)]
    pool_outs.append(jax.ShapeDtypeStruct((nodes_dev, feat_width), BF16))
    *parts, by_recv = pl.pallas_call(
        functools.partial(pool_kernel, shards, 2 * steps),
        grid_spec=pltpu.PrefetchScalarGridSpec(
            num_scalar_prefetch=1,
            grid=(2 * steps,),
            in_specs=[
                pl.BlockSpec(narrow, first_half),
                pl.BlockSpec(narrow, second_half),
                pl.BlockSpec(wide, lambda i, s: (by_edge(i, s), 0)),
                pl.BlockSpec(wide, lambda i, s: (by_edge(i, s), 0)),
                whole((nodes_dev, half_width)),
                pl.BlockSpec((1, tile), lambda i, s: (0, by_edge(i, s))),
                pl.BlockSpec((1, tile), lambda i, s: (0, by_edge(i, s))),
                whole((half_width, feat_width)),
                whole((1, half_width)),
                whole((half_width + PAD, feat_width)),
            ],
            out_specs=[whole(x.shape) for x in pool_outs],
            scratch_shapes=[
                pltpu.VMEM((4 * half_width, feat_width), F32),
                pltpu.VMEM((shards * half_nodes, feat_width), F32),
                pltpu.VMEM((nodes_dev, feat_width), F32),
            ],
        ),
        out_shape=pool_outs,
        compiler_params=params(),
        cost_estimate=cost(
            2 * edges * feat_width * (nodes_dev + shards * half_nodes + 2 * half_width), 8 * edges * half_width
        ),
        name="pool",
    )(
        idx, pre_own, pre_sib, edge_latents, sender_latents, node_latents, send_row, recv_row, wo_own, gain_sum,
        small_sib,
    )
    arrived = [parts[0]] + [lax.ppermute(parts[k], "nodes", ring(shards, k)) for k in range(1, shards)]
    recv_all = [by_recv] + [lax.ppermute(by_recv, "feat", ring(feats, k)) for k in range(1, feats)]
    w_total, s_total = pl.pallas_call(
        functools.partial(sum_kernel, shards),
        in_specs=[vmem] * shards + [pl.BlockSpec(memory_space=pl.ANY)] * (feats - 1),
        out_shape=[
            jax.ShapeDtypeStruct((block + PAD, feat_width), BF16),
            jax.ShapeDtypeStruct((half_nodes, feat_width), BF16),
        ],
        compiler_params=params(),
        cost_estimate=cost(rows_out * feat_width * shards, 4 * rows_out * feat_width * shards),
        name="sum_parts",
    )(*arrived, *recv_all[1:])
    w_all = [w_total] + [lax.ppermute(w_total, "nodes", ring(shards, k)) for k in range(1, shards)]
    s_all = [s_total, over_chan(s_total)]
    for k in range(1, feats):
        s_all.append(lax.ppermute(s_total, "feat", ring(feats, k)))
        flip = [(2 * f + c, 2 * ((f + k) % feats) + 1 - c) for f in range(feats) for c in range(2)]
        s_all.append(lax.ppermute(s_total, ("feat", "chan"), flip))

    passed, _ = lax.optimization_barrier((crossed_own[1:], s_total))
    crossed_own = [pre_own] + passed
    crossed_sib = [pre_sib] + [over_chan(x) for x in passed]

    edge_grad, edge_token = pl.pallas_call(
        functools.partial(edge_out_kernel, feats, 2 * steps),
        grid_spec=pltpu.PrefetchScalarGridSpec(
            num_scalar_prefetch=1,
            grid=(2 * steps,),
            in_specs=[
                pl.BlockSpec(wide, lambda i, s: (by_edge(i, s), 0)),
                pl.BlockSpec((None, half_width, hidden_width), lambda i, s: (0, 0, 0)),
            ]
            + [pl.BlockSpec(narrow, first_half)] * feats
            + [pl.BlockSpec(narrow, second_half)] * feats,
            out_specs=[pl.BlockSpec(wide, lambda i, s: (by_edge(i, s), 0)), whole((8, 128))],
            scratch_shapes=[pltpu.VMEM((tile, hidden_width), BF16)],
        ),
        out_shape=[jax.ShapeDtypeStruct((edges, half_width), BF16), jax.ShapeDtypeStruct((8, 128), F32)],
        compiler_params=params(),
        cost_estimate=cost(2 * edges * hidden_width * half_width, 8 * edges * half_width),
        name="edge_out",
    )(idx, edge_cotangent, w_in, *crossed_own, *crossed_sib)

    w_in_grad, w_out_grad, gain_grad = pl.pallas_call(
        functools.partial(place_kernel, shards, scale),
        in_specs=[smem] + [vmem] * shards + [pl.BlockSpec(memory_space=pl.ANY)],
        out_shape=[
            jax.ShapeDtypeStruct((3, half_width, feat_width), F32),
            jax.ShapeDtypeStruct((feat_width, half_width), F32),
            jax.ShapeDtypeStruct((1, half_width), F32),
        ],
        scratch_shapes=[pltpu.VMEM((4 * half_width, feat_width), F32)],
        compiler_params=params(),
        cost_estimate=cost(8 * half_width * feat_width, 24 * half_width * feat_width),
        name="place",
    )(idx, *w_all, edge_token)
    node_grad = pl.pallas_call(
        functools.partial(node_out_kernel, feats),
        grid=(1,),
        in_specs=[
            smem,
            pl.BlockSpec((None, half_width, hidden_width), lambda *_: (1, 0, 0)),
            pl.BlockSpec((None, half_width, hidden_width), lambda *_: (2, 0, 0)),
        ]
        + [whole((nodes_dev, feat_width))] * feats
        + [whole((half_nodes, feat_width))] * (2 * feats)
        + [pl.BlockSpec(memory_space=pl.ANY)],
        out_specs=whole((nodes_dev, half_width)),
        out_shape=jax.ShapeDtypeStruct((nodes_dev, half_width), F32),
        scratch_shapes=[
            pltpu.VMEM((nodes_dev, hidden_width), BF16),
            pltpu.VMEM((nodes_dev, hidden_width), BF16),
        ],
        compiler_params=params(),
        cost_estimate=cost(4 * nodes_dev * hidden_width * half_width, 8 * nodes_dev * hidden_width),
        name="node_out",
    )(idx, w_in, w_in, *recv_all, *s_all, gain_grad)

    return (node_grad, edge_grad, w_in_grad, w_out_grad, gain_grad.reshape(half_width))


def solution(mesh):
    placed = (
        P(("groups", "nodes"), "chan"),
        P(("groups", "nodes"), "chan"),
        P(("groups", "nodes"), "chan"),
        P(("groups", "nodes"), "feat"),
        P(("groups", "nodes"), "chan"),
        P("chan"),
        P(None, "chan", None),
        P("feat", "chan"),
        P(("groups", "nodes")),
        P(("groups", "nodes")),
        P(("groups", "nodes"), "chan"),
        P(("groups", "nodes"), "chan"),
    )
    return jax.shard_map(
        body,
        mesh=mesh,
        in_specs=placed,
        out_specs=(
            P(("groups", "nodes"), "chan"),
            P(("groups", "nodes"), "chan"),
            P("groups", "chan", "feat"),
            P(("groups", "feat"), "chan"),
            P(("groups", "chan")),
        ),
        check_vma=False,
    )
```

time: 98.1 us -> 68 us (0.69)
  waiting for transfers between devices: 47.5 us -> 30.1 us
  starting transfers between devices: 21.4 us -> 15.2 us
  local copies, waits for them, and re-layouts: 6.18 us -> 2.39 us
  Pallas kernels: 21.9 us -> 19.2 us
    ppermute x1, waiting for transfers between devices: 17.3 us -> 0.01 us  [body(): lax.ppermute(pre_own, 'feat', ring(feats, k))]
    ppermute x3, waiting for transfers between devices: 12.3 us -> 5.35 us  [body(): lax.ppermute(w_total, 'nodes', ring(shards, k))]
    ppermute x7 -> x6, starting transfers between devices: 12.3 us -> 6.6 us  [the longest x3 4.68 us: body(): lax.ppermute(parts[k], 'nodes', ring(shards, k))]
    ppermute x7 -> x6, waiting for transfers between devices: 14 us -> 18.5 us  [the longest x1 9.34 us: body(): lax.ppermute(by_recv, 'feat', ring(feats, k))]
    unnamed x24 -> x18, local copies, waits for them, and re-layouts: 5.53 us -> 2.39 us
    ppermute x7 -> x9, waiting for transfers between devices: 3.82 us -> 6.17 us  [over_chan(): return lax.ppermute(x, 'chan', [(0, 1), (1, 0)])]
    ppermute x3, starting transfers between devices: 5.15 us -> 3.87 us  [body(): lax.ppermute(w_total, 'nodes', ring(shards, k))]
    pallas_call x3 -> x2, Pallas kernels: 7.55 us -> 6.42 us  [the longest x1 6.31 us: body(): pl.pallas_call(functools.partial(edge_kernel, edge_steps), in_specs=[smem...]
  transfers between devices with their start and end apart: 18 -> 19, of which waited for: 9 -> 7; matrix products, arithmetic and copies ran while one was open for 0% -> 0% of each run, Pallas kernels for 11% -> 17%
where the time goes in v2:
time: 68 us; the launch traced here: 67.7 us
  waiting for transfers between devices  30.1 us (44%)
  Pallas kernels  19.2 us (28%)
  starting transfers between devices  15.2 us (22%)
  local copies, waits for them, and re-layouts  2.39 us (4%)
  between operations  0.78 us (1%)
    ppermute x1, waiting for transfers between devices, body(): lax.ppermute(by_recv, 'feat', ring(feats, k))  9.34 us
    ppermute x3, waiting for transfers between devices, body(): lax.ppermute(parts[k], 'nodes', ring(shards, k))  9.19 us
    pallas_call x1, Pallas kernels, body(): pl.pallas_call(functools.partial(edge_kernel, edge_steps), in_specs=[smem...  6.31 us
    ppermute x9, waiting for transfers between devices, over_chan(): return lax.ppermute(x, 'chan', [(0, 1), (1, 0)])  6.17 us
    pallas_call x1, Pallas kernels, body(): pl.pallas_call(functools.partial(pool_kernel, shards, 2 * steps), grid_sp...  5.88 us
    ppermute x3, waiting for transfers between devices, body(): lax.ppermute(w_total, 'nodes', ring(shards, k))  5.35 us
    ppermute x3, starting transfers between devices, body(): lax.ppermute(parts[k], 'nodes', ring(shards, k))  4.68 us
    ppermute x3, starting transfers between devices, body(): lax.ppermute(w_total, 'nodes', ring(shards, k))  3.87 us
  transfers between devices with their start and end apart: 19, of which 7 were waited for; matrix products, arithmetic and copies ran while one was open for 0% of the time, Pallas kernels for 17%

profile of v2, /device:TPU:0, one launch (start us, length us, event | category | flops | bytes accessed | tf_op | source)
XLA Modules:
  0.0 67.7 jit_solution(12780000593249309236)
XLA Ops:
  0.6 0.5 collective-permute-start.3
  1.1 0.1 collective-permute-start.4
  1.2 0.4 collective-permute-start
  1.7 0.1 collective-permute-start.2
  1.7 0.4 collective-permute-start.1
  2.2 0.1 pad_add_fusion.idx
  2.2 4.9 %collective-permute-done.1.refs_4_ = f32[1,256]{1,0:T(1,128)S(1)} collective-permute-done((f32[1,256]{1,0:T(1,128)}, f32[1,256]{1,0:T(1,128)S(1)}, u32[]{:S(2)}, u32[]{:S(2)}) %collective-permute-start.1) | collective-permute-done | bytes 1056 | tf_op jit(solution)/shard_map/ppermute | solution.py:262
  7.1 0.0 collective-permute-done.2.refs_6_
  7.1 0.0 collective-permute-done.refs_2_
  7.1 0.0 collective-permute-done.3.refs_8_
  7.1 0.0 copy-start.7
  7.1 0.0 collective-permute-done.4.refs_10_
  7.2 0.0 copy-start.8
  7.2 1.1 %copy-done.7 = bf16[3072,256]{1,0:T(8,128)(2,1)} copy-done((bf16[3072,256]{1,0:T(8,128)(2,1)}, bf16[3072,256]{1,0:T(8,128)(2,1)S(1)}, u32[]{:S(2)}) %copy-start.7) | copy-done | bytes 1572888
  8.3 0.6 copy-done.8
  8.8 0.0 copy-start.2
  8.8 0.0 copy-start.4
  8.8 0.0 copy-start.5
  8.8 0.0 copy-start.6
  8.8 6.3 %edge_norm.1 = (bf16[1536,256]{1,0:T(8,128)(2,1)S(1)}, f32[256,256]{1,0:T(8,128)S(1)}, f32[1,256]{1,0:T(1,128)S(1)}, bf16[272,256]{1,0:T(8,128)(2,1)S(1)}) custom-call(s32[3]{0:T(128)S(1)} %pad_add_fusion.idx, s32[1,3072]{1,0:T(1,128)} %bitcast.7, bf16[384,256]{1,0:T(8,128)(2,1)} %refs_1_.1, bf16[384,256]{1,0:T(8,128)(2,1)S(1)} %collective-permute-done.refs_2_, ...), custom_call_target="tpu_custom_call" | custom-call | flops 1409286144 | bytes 3932160 | tf_op jit(solution)/shard_map/edge_norm/pallas_call | solution.py:280
  15.2 0.4 collective-permute-start.5
  15.6 2.6 %collective-permute-start.17 = (bf16[1536,256]{1,0:T(8,128)(2,1)S(1)}, bf16[1536,256]{1,0:T(8,128)(2,1)S(1)}, u32[]{:S(2)}, u32[]{:S(2)}) collective-permute-start(bf16[1536,256]{1,0:T(8,128)(2,1)S(1)} %get-tuple-element.22.g_own.refs_0_), channel_id=1, source_target_pairs={{0,2},{2,0},{1,3},{3,1},{4,6},{6,4},{5,7},{7,5},{8,10},{10,8},{9,1... | collective-permute-start | bytes 2359304 | tf_op jit(solution)/shard_map/ppermute | solution.py:317
  18.2 0.1 collective-permute-start.6
  18.3 1.3 %collective-permute-done.6.small = bf16[272,256]{1,0:T(8,128)(2,1)S(1)} collective-permute-done((bf16[272,256]{1,0:T(8,128)(2,1)S(1)}, bf16[272,256]{1,0:T(8,128)(2,1)S(1)}, u32[]{:S(2)}, u32[]{:S(2)}) %collective-permute-start.6) | collective-permute-done | bytes 139296 | tf_op jit(solution)/shard_map/ppermute | solution.py:262
  19.6 0.0 collective-permute-done.5.g_sib.refs_2_
  19.6 0.0 copy-done.2
  19.6 0.0 copy-done.4
  19.6 0.0 copy-done.5
  19.6 0.0 copy-done.6
  19.6 0.0 copy-start.1
  19.6 5.9 %pool.1 = (f32[464,256]{1,0:T(8,128)S(1)}, bf16[464,256]{1,0:T(8,128)(2,1)S(1)}, bf16[464,256]{1,0:T(8,128)(2,1)S(1)}, bf16[464,256]{1,0:T(8,128)(2,1)S(1)}, bf16[384,256]{1,0:T(8,128)(2,1)S(1)}) custom-call(s32[3]{0:T(128)S(1)} %pad_add_fusion.idx, bf16[1536,256]{1,0:T(8,128)(2,1)S(1)} %get-tuple-element.22.g_own.refs_0_, ...), custom_call_target="tpu_custom_call" | custom-call | flops 2617245696 | bytes 6291456 | tf_op jit(solution)/shard_map/pool/pallas_call | solution.py:332
  25.5 0.0 copy-start
  25.5 3.7 %collective-permute-start.10 = (bf16[464,256]{1,0:T(8,128)(2,1)S(1)}, bf16[464,256]{1,0:T(8,128)(2,1)S(1)}, u32[]{:S(2)}, u32[]{:S(2)}) collective-permute-start(bf16[464,256]{1,0:T(8,128)(2,1)S(1)} %get-tuple-element.30), channel_id=1, source_target_pairs={{0,12},{4,0},{8,4},{12,8},{1,13},{5,1},{9,5},{13,9},{2,14},{6,2},{... | collective-permute-start | bytes 712712 | tf_op jit(solution)/shard_map/ppermute | solution.py:366
  29.2 0.0 collective-permute-start.8
  29.2 1.0 %collective-permute-start.9 = (bf16[464,256]{1,0:T(8,128)(2,1)S(1)}, bf16[464,256]{1,0:T(8,128)(2,1)S(1)}, u32[]{:S(2)}, u32[]{:S(2)}) collective-permute-start(bf16[464,256]{1,0:T(8,128)(2,1)S(1)} %get-tuple-element.29), channel_id=1, source_target_pairs={{0,8},{4,12},{8,0},{12,4},{1,9},{5,13},{9,1},{13,5},{2,10},{6,14},... | collective-permute-start | bytes 712712 | tf_op jit(solution)/shard_map/ppermute | solution.py:366
  30.2 1.0 %collective-permute-start.7 = (bf16[384,256]{1,0:T(8,128)(2,1)S(1)}, bf16[384,256]{1,0:T(8,128)(2,1)S(1)}, u32[]{:S(2)}, u32[]{:S(2)}) collective-permute-start(bf16[384,256]{1,0:T(8,128)(2,1)S(1)} %get-tuple-element.26.refs_0_), channel_id=1, source_target_pairs={{0,2},{2,0},{1,3},{3,1},{4,6},{6,4},{5,7},{7,5},{8,10},{10,8},{9,1... | collective-permute-start | bytes 589832 | tf_op jit(solution)/shard_map/ppermute | solution.py:367
  31.2 9.3 %collective-permute-done.7.refs_4_.refs_1_ = bf16[384,256]{1,0:T(8,128)(2,1)S(1)} collective-permute-done((bf16[384,256]{1,0:T(8,128)(2,1)S(1)}, bf16[384,256]{1,0:T(8,128)(2,1)S(1)}, u32[]{:S(2)}, u32[]{:S(2)}) %collective-permute-start.7) | collective-permute-done | bytes 196640 | tf_op jit(solution)/shard_map/ppermute | solution.py:367
  40.5 0.0 collective-permute-done.10.refs_3_
  40.5 0.9 %collective-permute-done.8.refs_1_ = bf16[464,256]{1,0:T(8,128)(2,1)S(1)} collective-permute-done((bf16[464,256]{1,0:T(8,128)(2,1)S(1)}, bf16[464,256]{1,0:T(8,128)(2,1)S(1)}, u32[]{:S(2)}, u32[]{:S(2)}) %collective-permute-start.8) | collective-permute-done | bytes 237600 | tf_op jit(solution)/shard_map/ppermute | solution.py:366
  41.4 8.3 %collective-permute-done.9.refs_2_ = bf16[464,256]{1,0:T(8,128)(2,1)S(1)} collective-permute-done((bf16[464,256]{1,0:T(8,128)(2,1)S(1)}, bf16[464,256]{1,0:T(8,128)(2,1)S(1)}, u32[]{:S(2)}, u32[]{:S(2)}) %collective-permute-start.9) | collective-permute-done | bytes 237600 | tf_op jit(solution)/shard_map/ppermute | solution.py:366
  49.7 0.1 sum_parts.1
  49.8 0.0 collective-permute-done.17.refs_1_
  49.8 0.1 collective-permute-start.18
  49.9 0.1 collective-permute-start.14
  50.0 3.2 %collective-permute-start.15 = (bf16[272,256]{1,0:T(8,128)(2,1)S(1)}, bf16[272,256]{1,0:T(8,128)(2,1)S(1)}, u32[]{:S(2)}, u32[]{:S(2)}) collective-permute-start(bf16[272,256]{1,0:T(8,128)(2,1)S(1)} %get-tuple-element.32.refs_0_), channel_id=1, source_target_pairs={{0,8},{4,12},{8,0},{12,4},{1,9},{5,13},{9,1},{13,5},{2,10},{6,14},... | collective-permute-start | bytes 417800 | tf_op jit(solution)/shard_map/ppermute | solution.py:379
  53.2 0.6 collective-permute-start.16
  53.8 0.0 collective-permute-start.11
  53.8 4.6 %collective-permute-done.14.refs_1_ = bf16[272,256]{1,0:T(8,128)(2,1)S(1)} collective-permute-done((bf16[272,256]{1,0:T(8,128)(2,1)S(1)}, bf16[272,256]{1,0:T(8,128)(2,1)S(1)}, u32[]{:S(2)}, u32[]{:S(2)}) %collective-permute-start.14) | collective-permute-done | bytes 139296 | tf_op jit(solution)/shard_map/ppermute | solution.py:379
  58.4 1.0 %collective-permute-start.12 = (bf16[192,256]{1,0:T(8,128)(2,1)S(1)}, bf16[192,256]{1,0:T(8,128)(2,1)S(1)}, u32[]{:S(2)}, u32[]{:S(2)}) collective-permute-start(bf16[192,256]{1,0:T(8,128)(2,1)S(1)} %get-tuple-element.31.refs_2_), channel_id=1, source_target_pairs={{0,2},{2,0},{1,3},{3,1},{4,6},{6,4},{5,7},{7,5},{8,10},{10,8},{9,1... | collective-permute-start | bytes 294920 | tf_op jit(solution)/shard_map/ppermute | solution.py:382
  59.3 0.0 collective-permute-done.18.refs_3_
  59.3 0.0 collective-permute-start.13
  59.3 0.0 copy-done.1
  59.3 0.0 copy-done
  59.3 3.5 %edge_out.1 = (bf16[3072,256]{1,0:T(8,128)(2,1)}, f32[8,128]{1,0:T(8,128)S(1)}) custom-call(s32[3]{0:T(128)S(1)} %pad_add_fusion.idx, bf16[3072,256]{1,0:T(8,128)(2,1)S(1)} %copy-done.1, bf16[3,256,512]{2,1,0:T(8,128)(2,1)S(1)} %copy-done, bf16[1536,256]{1,0:T(8,128)(2,1)S(1)} %get-tuple-element.22.g_own.refs_0_, ...), custom_call_target="tpu_custom_call" | custom-call | flops 805306368 | bytes 6291456 | tf_op jit(solution)/shard_map/edge_out/pallas_call | solution.py:390
  62.8 0.8 %collective-permute-done.15.refs_2_ = bf16[272,256]{1,0:T(8,128)(2,1)S(1)} collective-permute-done((bf16[272,256]{1,0:T(8,128)(2,1)S(1)}, bf16[272,256]{1,0:T(8,128)(2,1)S(1)}, u32[]{:S(2)}, u32[]{:S(2)}) %collective-permute-start.15) | collective-permute-done | bytes 139296 | tf_op jit(solution)/shard_map/ppermute | solution.py:379
  63.6 0.0 collective-permute-done.16.refs_3_
  63.6 1.7 %place.1 = (f32[3,256,256]{2,1,0:T(8,128)}, f32[256,256]{1,0:T(8,128)}, f32[1,256]{1,0:T(1,128)}) custom-call(s32[3]{0:T(128)S(1)} %pad_add_fusion.idx, bf16[272,256]{1,0:T(8,128)(2,1)S(1)} %get-tuple-element.32.refs_0_, bf16[272,256]{1,0:T(8,128)(2,1)S(1)} %collective-permute-done.14.refs_1_, bf16[272,256]{1,0:T(8,128)(2,1)S(1)} %collective-permute-done.15.refs_2_, ...), custom_call_target="tpu_custom_call" | custom-call | flops 524288 | bytes 1572864 | tf_op jit(solution)/shard_map/place/pallas_call | solution.py:410
  65.3 0.0 collective-permute-done.11.refs_3_
  65.3 0.0 collective-permute-done.12.refs_4_
  65.3 0.0 collective-permute-done.13.refs_5_
  65.3 0.0 copy-start.3
  65.3 0.7 copy-done.3
  66.0 1.7 %node_out.1 = f32[384,256]{1,0:T(8,128)} custom-call(s32[3]{0:T(128)S(1)} %pad_add_fusion.idx, bf16[3,256,512]{2,1,0:T(8,128)(2,1)S(1)} %copy-done, bf16[3,256,512]{2,1,0:T(8,128)(2,1)S(1)} %copy-done, bf16[384,256]{1,0:T(8,128)(2,1)S(1)} %get-tuple-element.26.refs_0_, bf16[384,256]{1,0:T(8,128)(2,1)S(1)} %collective-permute-done.7.refs_4_.refs_1_, ...), custom_call_target="tpu_custom_call" | custom-call | flops 201326592 | bytes 1572864 | tf_op jit(solution)/shard_map/node_out/pallas_call | solution.py:423
Async XLA Ops:
  0.6 6.5 %collective-permute-start.3 = (bf16[3072,256]{1,0:T(8,128)(2,1)}, bf16[3072,256]{1,0:T(8,128)(2,1)S(1)}, u32[]{:S(2)}, u32[]{:S(2)}) collective-permute-start(bf16[3072,256]{1,0:T(8,128)(2,1)} %refs_7_.1), channel_id=1, source_target_pairs={{0,1},{1,0},{2,3},{3,2},{4,5},{5,4},{6,7},{7,6},{8,9},{9,8},{10,11... | collective-permute-start | bytes 4718600 | tf_op jit(solution)/shard_map/ppermute | solution.py:262
  1.1 6.0 %collective-permute-start.4 = (bf16[3072,256]{1,0:T(8,128)(2,1)}, bf16[3072,256]{1,0:T(8,128)(2,1)S(1)}, u32[]{:S(2)}, u32[]{:S(2)}) collective-permute-start(bf16[3072,256]{1,0:T(8,128)(2,1)} %cot.1), channel_id=1, source_target_pairs={{0,1},{1,0},{2,3},{3,2},{4,5},{5,4},{6,7},{7,6},{8,9},{9,8},{10,11... | collective-permute-start | bytes 4718600 | tf_op jit(solution)/shard_map/ppermute | solution.py:262
  1.2 5.9 %collective-permute-start = (bf16[384,256]{1,0:T(8,128)(2,1)}, bf16[384,256]{1,0:T(8,128)(2,1)S(1)}, u32[]{:S(2)}, u32[]{:S(2)}) collective-permute-start(bf16[384,256]{1,0:T(8,128)(2,1)} %refs_1_.1), channel_id=1, source_target_pairs={{0,1},{1,0},{2,3},{3,2},{4,5},{5,4},{6,7},{7,6},{8,9},{9,8},{10,11... | collective-permute-start | bytes 589832 | tf_op jit(solution)/shard_map/ppermute | solution.py:262
  1.7 5.5 %collective-permute-start.2 = (bf16[256,256]{1,0:T(8,128)(2,1)}, bf16[256,256]{1,0:T(8,128)(2,1)S(1)}, u32[]{:S(2)}, u32[]{:S(2)}) collective-permute-start(bf16[256,256]{1,0:T(8,128)(2,1)} %refs_5_.1), channel_id=1, source_target_pairs={{0,1},{1,0},{2,3},{3,2},{4,5},{5,4},{6,7},{7,6},{8,9},{9,8},{10,11... | collective-permute-start | bytes 393224 | tf_op jit(solution)/shard_map/ppermute | solution.py:262
  1.7 5.4 %collective-permute-start.1 = (f32[1,256]{1,0:T(1,128)}, f32[1,256]{1,0:T(1,128)S(1)}, u32[]{:S(2)}, u32[]{:S(2)}) collective-permute-start(f32[1,256]{1,0:T(1,128)} %bitcast.11), channel_id=1, source_target_pairs={{0,1},{1,0},{2,3},{3,2},{4,5},{5,4},{6,7},{7,6},{8,9},{9,8},{10,11... | collective-permute-start | bytes 3080 | tf_op jit(solution)/shard_map/ppermute | solution.py:262
  7.1 1.1 %copy-start.7 = (bf16[3072,256]{1,0:T(8,128)(2,1)}, bf16[3072,256]{1,0:T(8,128)(2,1)S(1)}, u32[]{:S(2)}) copy-start(bf16[3072,256]{1,0:T(8,128)(2,1)S(1)} %collective-permute-done.3.refs_8_) | copy-start | bytes 4718596
  7.2 1.7 %copy-start.8 = (bf16[3072,256]{1,0:T(8,128)(2,1)}, bf16[3072,256]{1,0:T(8,128)(2,1)S(1)}, u32[]{:S(2)}) copy-start(bf16[3072,256]{1,0:T(8,128)(2,1)S(1)} %collective-permute-done.4.refs_10_) | copy-start | bytes 4718596
  8.8 10.8 %copy-start.2 = (s32[3072]{0:T(1024)S(1)}, s32[3072]{0:T(1024)}, u32[]{:S(2)}) copy-start(s32[3072]{0:T(1024)} %param.21) | copy-start | bytes 36868
  8.8 10.8 %copy-start.4 = (bf16[3072,256]{1,0:T(8,128)(2,1)S(1)}, bf16[3072,256]{1,0:T(8,128)(2,1)}, u32[]{:S(2)}) copy-start(bf16[3072,256]{1,0:T(8,128)(2,1)} %edge_lat.1) | copy-start | bytes 4718596
  8.8 10.8 %copy-start.5 = (bf16[384,256]{1,0:T(8,128)(2,1)S(1)}, bf16[384,256]{1,0:T(8,128)(2,1)}, u32[]{:S(2)}) copy-start(bf16[384,256]{1,0:T(8,128)(2,1)} %node_lat.1) | copy-start | bytes 589828
  8.8 10.8 %copy-start.6 = (s32[3072]{0:T(1024)S(1)}, s32[3072]{0:T(1024)}, u32[]{:S(2)}) copy-start(s32[3072]{0:T(1024)} %param.20) | copy-start | bytes 36868
  15.2 4.4 %collective-permute-start.5 = (bf16[1536,256]{1,0:T(8,128)(2,1)S(1)}, bf16[1536,256]{1,0:T(8,128)(2,1)S(1)}, u32[]{:S(2)}, u32[]{:S(2)}) collective-permute-start(bf16[1536,256]{1,0:T(8,128)(2,1)S(1)} %get-tuple-element.22.g_own.refs_0_), channel_id=1, source_target_pairs={{0,1},{1,0},{2,3},{3,2},{4,5},{5,4},{6,7},{7,6},{8,9},{9,8},{10,11... | collective-permute-start | bytes 2359304 | tf_op jit(solution)/shard_map/ppermute | solution.py:262
  15.6 34.2 %collective-permute-start.17 = (bf16[1536,256]{1,0:T(8,128)(2,1)S(1)}, bf16[1536,256]{1,0:T(8,128)(2,1)S(1)}, u32[]{:S(2)}, u32[]{:S(2)}) collective-permute-start(bf16[1536,256]{1,0:T(8,128)(2,1)S(1)} %get-tuple-element.22.g_own.refs_0_), channel_id=1, source_target_pairs={{0,2},{2,0},{1,3},{3,1},{4,6},{6,4},{5,7},{7,5},{8,10},{10,8},{9,1... | collective-permute-start | bytes 2359304 | tf_op jit(solution)/shard_map/ppermute | solution.py:317
  18.2 1.4 %collective-permute-start.6 = (bf16[272,256]{1,0:T(8,128)(2,1)S(1)}, bf16[272,256]{1,0:T(8,128)(2,1)S(1)}, u32[]{:S(2)}, u32[]{:S(2)}) collective-permute-start(bf16[272,256]{1,0:T(8,128)(2,1)S(1)} %get-tuple-element.25), channel_id=1, source_target_pairs={{0,1},{1,0},{2,3},{3,2},{4,5},{5,4},{6,7},{7,6},{8,9},{9,8},{10,11... | collective-permute-start | bytes 417800 | tf_op jit(solution)/shard_map/ppermute | solution.py:262
  19.6 39.7 %copy-start.1 = (bf16[3072,256]{1,0:T(8,128)(2,1)S(1)}, bf16[3072,256]{1,0:T(8,128)(2,1)}, u32[]{:S(2)}) copy-start(bf16[3072,256]{1,0:T(8,128)(2,1)} %cot.1) | copy-start | bytes 4718596
  25.5 33.8 %copy-start = (bf16[3,256,512]{2,1,0:T(8,128)(2,1)S(1)}, bf16[3,256,512]{2,1,0:T(8,128)(2,1)}, u32[]{:S(2)}) copy-start(bf16[3,256,512]{2,1,0:T(8,128)(2,1)} %w_recv.1) | copy-start | bytes 2359300
  25.5 15.0 %collective-permute-start.10 = (bf16[464,256]{1,0:T(8,128)(2,1)S(1)}, bf16[464,256]{1,0:T(8,128)(2,1)S(1)}, u32[]{:S(2)}, u32[]{:S(2)}) collective-permute-start(bf16[464,256]{1,0:T(8,128)(2,1)S(1)} %get-tuple-element.30), channel_id=1, source_target_pairs={{0,12},{4,0},{8,4},{12,8},{1,13},{5,1},{9,5},{13,9},{2,14},{6,2},{... | collective-permute-start | bytes 712712 | tf_op jit(solution)/shard_map/ppermute | solution.py:366
  29.2 12.2 %collective-permute-start.8 = (bf16[464,256]{1,0:T(8,128)(2,1)S(1)}, bf16[464,256]{1,0:T(8,128)(2,1)S(1)}, u32[]{:S(2)}, u32[]{:S(2)}) collective-permute-start(bf16[464,256]{1,0:T(8,128)(2,1)S(1)} %get-tuple-element.28), channel_id=1, source_target_pairs={{0,4},{4,8},{8,12},{12,0},{1,5},{5,9},{9,13},{13,1},{2,6},{6,10},{... | collective-permute-start | bytes 712712 | tf_op jit(solution)/shard_map/ppermute | solution.py:366
  29.2 20.5 %collective-permute-start.9 = (bf16[464,256]{1,0:T(8,128)(2,1)S(1)}, bf16[464,256]{1,0:T(8,128)(2,1)S(1)}, u32[]{:S(2)}, u32[]{:S(2)}) collective-permute-start(bf16[464,256]{1,0:T(8,128)(2,1)S(1)} %get-tuple-element.29), channel_id=1, source_target_pairs={{0,8},{4,12},{8,0},{12,4},{1,9},{5,13},{9,1},{13,5},{2,10},{6,14},... | collective-permute-start | bytes 712712 | tf_op jit(solution)/shard_map/ppermute | solution.py:366
  30.2 10.3 %collective-permute-start.7 = (bf16[384,256]{1,0:T(8,128)(2,1)S(1)}, bf16[384,256]{1,0:T(8,128)(2,1)S(1)}, u32[]{:S(2)}, u32[]{:S(2)}) collective-permute-start(bf16[384,256]{1,0:T(8,128)(2,1)S(1)} %get-tuple-element.26.refs_0_), channel_id=1, source_target_pairs={{0,2},{2,0},{1,3},{3,1},{4,6},{6,4},{5,7},{7,5},{8,10},{10,8},{9,1... | collective-permute-start | bytes 589832 | tf_op jit(solution)/shard_map/ppermute | solution.py:367
  49.8 9.5 %collective-permute-start.18 = (bf16[1536,256]{1,0:T(8,128)(2,1)S(1)}, bf16[1536,256]{1,0:T(8,128)(2,1)S(1)}, u32[]{:S(2)}, u32[]{:S(2)}) collective-permute-start(bf16[1536,256]{1,0:T(8,128)(2,1)S(1)} %collective-permute-done.17.refs_1_), channel_id=1, source_target_pairs={{0,1},{1,0},{2,3},{3,2},{4,5},{5,4},{6,7},{7,6},{8,9},{9,8},{10,11... | collective-permute-start | bytes 2359304 | tf_op jit(solution)/shard_map/ppermute | solution.py:262
  49.9 8.5 %collective-permute-start.14 = (bf16[272,256]{1,0:T(8,128)(2,1)S(1)}, bf16[272,256]{1,0:T(8,128)(2,1)S(1)}, u32[]{:S(2)}, u32[]{:S(2)}) collective-permute-start(bf16[272,256]{1,0:T(8,128)(2,1)S(1)} %get-tuple-element.32.refs_0_), channel_id=1, source_target_pairs={{0,4},{4,8},{8,12},{12,0},{1,5},{5,9},{9,13},{13,1},{2,6},{6,10},{... | collective-permute-start | bytes 417800 | tf_op jit(solution)/shard_map/ppermute | solution.py:379
  50.0 13.6 %collective-permute-start.15 = (bf16[272,256]{1,0:T(8,128)(2,1)S(1)}, bf16[272,256]{1,0:T(8,128)(2,1)S(1)}, u32[]{:S(2)}, u32[]{:S(2)}) collective-permute-start(bf16[272,256]{1,0:T(8,128)(2,1)S(1)} %get-tuple-element.32.refs_0_), channel_id=1, source_target_pairs={{0,8},{4,12},{8,0},{12,4},{1,9},{5,13},{9,1},{13,5},{2,10},{6,14},... | collective-permute-start | bytes 417800 | tf_op jit(solution)/shard_map/ppermute | solution.py:379
  53.2 10.5 %collective-permute-start.16 = (bf16[272,256]{1,0:T(8,128)(2,1)S(1)}, bf16[272,256]{1,0:T(8,128)(2,1)S(1)}, u32[]{:S(2)}, u32[]{:S(2)}) collective-permute-start(bf16[272,256]{1,0:T(8,128)(2,1)S(1)} %get-tuple-element.32.refs_0_), channel_id=1, source_target_pairs={{0,12},{4,0},{8,4},{12,8},{1,13},{5,1},{9,5},{13,9},{2,14},{6,2},{... | collective-permute-start | bytes 417800 | tf_op jit(solution)/shard_map/ppermute | solution.py:379
  53.8 11.5 %collective-permute-start.11 = (bf16[192,256]{1,0:T(8,128)(2,1)S(1)}, bf16[192,256]{1,0:T(8,128)(2,1)S(1)}, u32[]{:S(2)}, u32[]{:S(2)}) collective-permute-start(bf16[192,256]{1,0:T(8,128)(2,1)S(1)} %get-tuple-element.31.refs_2_), channel_id=1, source_target_pairs={{0,1},{1,0},{2,3},{3,2},{4,5},{5,4},{6,7},{7,6},{8,9},{9,8},{10,11... | collective-permute-start | bytes 294920 | tf_op jit(solution)/shard_map/ppermute | solution.py:262
  58.4 7.0 %collective-permute-start.12 = (bf16[192,256]{1,0:T(8,128)(2,1)S(1)}, bf16[192,256]{1,0:T(8,128)(2,1)S(1)}, u32[]{:S(2)}, u32[]{:S(2)}) collective-permute-start(bf16[192,256]{1,0:T(8,128)(2,1)S(1)} %get-tuple-element.31.refs_2_), channel_id=1, source_target_pairs={{0,2},{2,0},{1,3},{3,1},{4,6},{6,4},{5,7},{7,5},{8,10},{10,8},{9,1... | collective-permute-start | bytes 294920 | tf_op jit(solution)/shard_map/ppermute | solution.py:382
  59.3 6.0 %collective-permute-start.13 = (bf16[192,256]{1,0:T(8,128)(2,1)S(1)}, bf16[192,256]{1,0:T(8,128)(2,1)S(1)}, u32[]{:S(2)}, u32[]{:S(2)}) collective-permute-start(bf16[192,256]{1,0:T(8,128)(2,1)S(1)} %get-tuple-element.31.refs_2_), channel_id=1, source_target_pairs={{0,3},{1,2},{2,1},{3,0},{4,7},{5,6},{6,5},{7,4},{8,11},{9,10},{10,... | collective-permute-start | bytes 294920 | tf_op jit(solution)/shard_map/ppermute | solution.py:384
  65.3 0.7 %copy-start.3 = (f32[1,256]{1,0:T(1,128)S(1)}, f32[1,256]{1,0:T(1,128)}, u32[]{:S(2)}) copy-start(f32[1,256]{1,0:T(1,128)} %get-tuple-element.35.refs_6_) | copy-start | bytes 3076

commit v3 on v2

--- a/solution.py
+++ b/solution.py
@@ -193,26 +193,6 @@
     s_total[...] = total[rows:].astype(BF16)
 
 
-def place_kernel(shards, scale, idx, *refs):
-    totals = refs[:shards]
-    w_in_grad, w_out_grad, gain_grad, held = refs[-4:]
-    half_width, feat_width = w_in_grad.shape[1:]
-    block = 4 * half_width // shards
-    for k in range(shards):
-        source = lax.rem(idx[1] - k + shards, shards)
-        held[pl.ds(pl.multiple_of(source * block, 16), block), :] = totals[k][:block, :].astype(F32) * scale
-
-        @pl.when(source == 0)
-        def _(k=k):
-            rows = totals[k][block:, :].astype(F32) * scale
-            for j in range(half_width // feat_width):
-                gain_grad[:, j * feat_width : (j + 1) * feat_width] = rows[j : j + 1, :]
-
-    for k in range(3):
-        w_in_grad[k] = held[k * half_width : (k + 1) * half_width, :]
-    w_out_grad[...] = jnp.transpose(held[3 * half_width :, :])
-
-
 def edge_out_kernel(feats, steps, idx, cot, w_edge, *refs):
     own = refs[:feats]
     sib = refs[feats : 2 * feats]
@@ -227,10 +207,12 @@
     out[...] = (cot[...].astype(F32) + dot_nt(held[...], w_edge[...])).astype(BF16)
 
 
-def node_out_kernel(feats, idx, w_send, w_recv, *refs):
-    by_recv = refs[:feats]
-    sums = refs[feats : 3 * feats]
-    out, held_send, held_recv = refs[-3:]
+def finish_kernel(shards, feats, scale, idx, *refs):
+    totals = refs[:shards]
+    w_send, w_recv = refs[shards : shards + 2]
+    by_recv = refs[shards + 2 : shards + 2 + feats]
+    sums = refs[shards + 2 + feats : shards + 2 + 3 * feats]
+    w_in_grad, w_out_grad, gain_grad, node_grad, held, held_send, held_recv = refs[-7:]
     rows, feat_width = sums[0].shape
     for k in range(feats):
         source = lax.rem(idx[2] - k + feats, feats)
@@ -239,7 +221,23 @@
         for side in range(2):
             at = pl.ds(pl.multiple_of((idx[0] if side == 0 else 1 - idx[0]) * rows, 16), rows)
             held_send[at, there] = sums[2 * k + side][...]
-    out[...] = dot_nt(held_send[...], w_send[...]) + dot_nt(held_recv[...], w_recv[...])
+    node_grad[...] = dot_nt(held_send[...], w_send[...]) + dot_nt(held_recv[...], w_recv[...])
+
+    half_width = w_in_grad.shape[1]
+    block = 4 * half_width // shards
+    for k in range(shards):
+        source = lax.rem(idx[1] - k + shards, shards)
+        held[pl.ds(pl.multiple_of(source * block, 16), block), :] = totals[k][:block, :].astype(F32) * scale
+
+        @pl.when(source == 0)
+        def _(k=k):
+            gain = totals[k][block:, :].astype(F32) * scale
+            for j in range(half_width // feat_width):
+                gain_grad[:, j * feat_width : (j + 1) * feat_width] = gain[j : j + 1, :]
+
+    for k in range(3):
+        w_in_grad[k] = held[k * half_width : (k + 1) * half_width, :]
+    w_out_grad[...] = jnp.transpose(held[3 * half_width :, :])
 
 
 def body(
@@ -309,7 +307,7 @@
         name="edge_norm",
     )(
         idx, in_hbm(recv_row), in_hbm(agg_cotangent), agg_sib, in_hbm(gain_own), gain_sib, in_hbm(w_out), w_out_sib,
-        in_hbm(pre_norm), in_hbm(pre_norm_sib), in_hbm(edge_cotangent), in_hbm(cot_sib), in_hbm(pre_hidden),
+        in_hbm(pre_norm), pre_norm_sib, in_hbm(edge_cotangent), cot_sib, in_hbm(pre_hidden),
     )
 
     pre_sib = over_chan(pre_own)
@@ -407,41 +405,39 @@
         name="edge_out",
     )(idx, edge_cotangent, w_in, *crossed_own, *crossed_sib)
 
-    w_in_grad, w_out_grad, gain_grad = pl.pallas_call(
-        functools.partial(place_kernel, shards, scale),
-        in_specs=[smem] + [vmem] * shards + [pl.BlockSpec(memory_space=pl.ANY)],
-        out_shape=[
-            jax.ShapeDtypeStruct((3, half_width, feat_width), F32),
-            jax.ShapeDtypeStruct((feat_width, half_width), F32),
-            jax.ShapeDtypeStruct((1, half_width), F32),
-        ],
-        scratch_shapes=[pltpu.VMEM((4 * half_width, feat_width), F32)],
-        compiler_params=params(),
-        cost_estimate=cost(8 * half_width * feat_width, 24 * half_width * feat_width),
-        name="place",
-    )(idx, *w_all, edge_token)
-    node_grad = pl.pallas_call(
-        functools.partial(node_out_kernel, feats),
+    w_in_grad, w_out_grad, gain_grad, node_grad = pl.pallas_call(
+        functools.partial(finish_kernel, shards, feats, scale),
         grid=(1,),
-        in_specs=[
-            smem,
+        in_specs=[smem]
+        + [whole((block + PAD, feat_width))] * shards
+        + [
             pl.BlockSpec((None, half_width, hidden_width), lambda *_: (1, 0, 0)),
             pl.BlockSpec((None, half_width, hidden_width), lambda *_: (2, 0, 0)),
         ]
         + [whole((nodes_dev, feat_width))] * feats
         + [whole((half_nodes, feat_width))] * (2 * feats)
         + [pl.BlockSpec(memory_space=pl.ANY)],
-        out_specs=whole((nodes_dev, half_width)),
-        out_shape=jax.ShapeDtypeStruct((nodes_dev, half_width), F32),
+        out_specs=[
+            whole((3, half_width, feat_width)),
+            whole((feat_width, half_width)),
+            whole((1, half_width)),
+            whole((nodes_dev, half_width)),
+        ],
+        out_shape=[
+            jax.ShapeDtypeStruct((3, half_width, feat_width), F32),
+            jax.ShapeDtypeStruct((feat_width, half_width), F32),
+            jax.ShapeDtypeStruct((1, half_width), F32),
+            jax.ShapeDtypeStruct((nodes_dev, half_width), F32),
+        ],
         scratch_shapes=[
+            pltpu.VMEM((4 * half_width, feat_width), F32),
             pltpu.VMEM((nodes_dev, hidden_width), BF16),
             pltpu.VMEM((nodes_dev, hidden_width), BF16),
         ],
         compiler_params=params(),
         cost_estimate=cost(4 * nodes_dev * hidden_width * half_width, 8 * nodes_dev * hidden_width),
-        name="node_out",
-    )(idx, w_in, w_in, *recv_all, *s_all, gain_grad)
-
+        name="finish",
+    )(idx, *w_all, w_in, w_in, *recv_all, *s_all, edge_token)
     return (node_grad, edge_grad, w_in_grad, w_out_grad, gain_grad.reshape(half_width))
 
 

time: 68 us -> 63.9 us (0.940)
  waiting for transfers between devices: 30.1 us -> 23.9 us
  starting transfers between devices: 15.2 us -> 20.7 us
  local copies, waits for them, and re-layouts: 2.39 us -> 0.04 us
  Pallas kernels: 19.2 us -> 17.7 us
    ppermute x3, waiting for transfers between devices: 9.19 us -> 5.04 us  [body(): lax.ppermute(parts[k], 'nodes', ring(shards, k))]
    ppermute x3, starting transfers between devices: 3.87 us -> 7.92 us  [body(): lax.ppermute(w_total, 'nodes', ring(shards, k))]
    ppermute x3, waiting for transfers between devices: 5.35 us -> 2.66 us  [body(): lax.ppermute(w_total, 'nodes', ring(shards, k))]
    unnamed x18 -> x12, local copies, waits for them, and re-layouts: 2.39 us -> 0.04 us
    pallas_call x2 -> x1, Pallas kernels: 3.41 us -> 2.14 us  [body(): pl.pallas_call(functools.partial(finish_kernel, shards, feats, scale), gr...]
    ppermute x1, waiting for transfers between devices: 0.01 us -> 0.9 us  [body(): s_all.append(lax.ppermute(s_total, 'feat', ring(feats, k)))]
    ppermute x3, starting transfers between devices: 4.68 us -> 5.58 us  [body(): lax.ppermute(parts[k], 'nodes', ring(shards, k))]
    ppermute x1, waiting for transfers between devices: 9.34 us -> 8.48 us  [body(): lax.ppermute(by_recv, 'feat', ring(feats, k))]
  transfers between devices with their start and end apart: 19 -> 19, of which waited for: 7 -> 7; matrix products, arithmetic and copies ran while one was open for 0% -> 0% of each run, Pallas kernels for 17% -> 15%
where the time goes in v3:
time: 63.9 us; the launch traced here: 63.1 us
  waiting for transfers between devices  23.9 us (37%)
  starting transfers between devices  20.7 us (32%)
  Pallas kernels  17.7 us (28%)
  between operations  0.77 us (1%)
    ppermute x1, waiting for transfers between devices, body(): lax.ppermute(by_recv, 'feat', ring(feats, k))  8.48 us
    ppermute x3, starting transfers between devices, body(): lax.ppermute(w_total, 'nodes', ring(shards, k))  7.92 us
    ppermute x9, waiting for transfers between devices, over_chan(): return lax.ppermute(x, 'chan', [(0, 1), (1, 0)])  6.17 us
    pallas_call x1, Pallas kernels, body(): pl.pallas_call(functools.partial(edge_kernel, edge_steps), in_specs=[smem...  6.12 us
    pallas_call x1, Pallas kernels, body(): pl.pallas_call(functools.partial(pool_kernel, shards, 2 * steps), grid_sp...  5.82 us
    ppermute x3, starting transfers between devices, body(): lax.ppermute(parts[k], 'nodes', ring(shards, k))  5.58 us
    ppermute x3, waiting for transfers between devices, body(): lax.ppermute(parts[k], 'nodes', ring(shards, k))  5.04 us
    pallas_call x1, Pallas kernels, body(): pl.pallas_call(functools.partial(edge_out_kernel, feats, 2 * steps), grid...  3.48 us
  transfers between devices with their start and end apart: 19, of which 7 were waited for; matrix products, arithmetic and copies ran while one was open for 0% of the time, Pallas kernels for 15%

profile of v3, /device:TPU:0, one launch (start us, length us, event | category | flops | bytes accessed | tf_op | source)
XLA Modules:
  0.0 63.1 jit_solution(5481729543688043074)
XLA Ops:
  0.6 0.5 collective-permute-start.3
  1.1 0.1 collective-permute-start.4
  1.2 0.4 collective-permute-start
  1.7 0.1 collective-permute-start.2
  1.7 0.4 collective-permute-start.1
  2.2 0.1 pad_add_fusion.idx
  2.2 4.9 %collective-permute-done.1.refs_4_ = f32[1,256]{1,0:T(1,128)S(1)} collective-permute-done((f32[1,256]{1,0:T(1,128)}, f32[1,256]{1,0:T(1,128)S(1)}, u32[]{:S(2)}, u32[]{:S(2)}) %collective-permute-start.1) | collective-permute-done | bytes 1056 | tf_op jit(solution)/shard_map/ppermute | solution.py:260
  7.1 0.0 collective-permute-done.2.refs_6_
  7.1 0.0 collective-permute-done.refs_2_
  7.1 0.0 collective-permute-done.3.refs_8_
  7.1 0.0 collective-permute-done.4.refs_10_
  7.1 0.0 copy-start.2
  7.2 0.0 copy-start.3
  7.2 0.0 copy-start.4
  7.2 0.0 copy-start.5
  7.2 6.1 %edge_norm.1 = (bf16[1536,256]{1,0:T(8,128)(2,1)S(1)}, f32[256,256]{1,0:T(8,128)S(1)}, f32[1,256]{1,0:T(1,128)S(1)}, bf16[272,256]{1,0:T(8,128)(2,1)S(1)}) custom-call(s32[3]{0:T(128)S(1)} %pad_add_fusion.idx, s32[1,3072]{1,0:T(1,128)} %bitcast.7, bf16[384,256]{1,0:T(8,128)(2,1)} %refs_1_.1, bf16[384,256]{1,0:T(8,128)(2,1)S(1)} %collective-permute-done.refs_2_, ...), custom_call_target="tpu_custom_call" | custom-call | flops 1409286144 | bytes 3932160 | tf_op jit(solution)/shard_map/edge_norm/pallas_call | solution.py:278
  13.3 0.4 collective-permute-start.5
  13.8 2.6 %collective-permute-start.17 = (bf16[1536,256]{1,0:T(8,128)(2,1)S(1)}, bf16[1536,256]{1,0:T(8,128)(2,1)S(1)}, u32[]{:S(2)}, u32[]{:S(2)}) collective-permute-start(bf16[1536,256]{1,0:T(8,128)(2,1)S(1)} %get-tuple-element.23.g_own.refs_0_), channel_id=1, source_target_pairs={{0,2},{2,0},{1,3},{3,1},{4,6},{6,4},{5,7},{7,5},{8,10},{10,8},{9,1... | collective-permute-start | bytes 2359304 | tf_op jit(solution)/shard_map/ppermute | solution.py:315
  16.4 0.1 collective-permute-start.6
  16.5 1.3 %collective-permute-done.6.small = bf16[272,256]{1,0:T(8,128)(2,1)S(1)} collective-permute-done((bf16[272,256]{1,0:T(8,128)(2,1)S(1)}, bf16[272,256]{1,0:T(8,128)(2,1)S(1)}, u32[]{:S(2)}, u32[]{:S(2)}) %collective-permute-start.6) | collective-permute-done | bytes 139296 | tf_op jit(solution)/shard_map/ppermute | solution.py:260
  17.7 0.0 collective-permute-done.5.g_sib.refs_2_
  17.8 0.0 copy-done.2
  17.8 0.0 copy-done.3
  17.8 0.0 copy-done.4
  17.8 0.0 copy-done.5
  17.8 0.0 copy-start.1
  17.8 5.8 %pool.1 = (f32[464,256]{1,0:T(8,128)S(1)}, bf16[464,256]{1,0:T(8,128)(2,1)S(1)}, bf16[464,256]{1,0:T(8,128)(2,1)S(1)}, bf16[464,256]{1,0:T(8,128)(2,1)S(1)}, bf16[384,256]{1,0:T(8,128)(2,1)S(1)}) custom-call(s32[3]{0:T(128)S(1)} %pad_add_fusion.idx, bf16[1536,256]{1,0:T(8,128)(2,1)S(1)} %get-tuple-element.23.g_own.refs_0_, ...), custom_call_target="tpu_custom_call" | custom-call | flops 2617245696 | bytes 6291456 | tf_op jit(solution)/shard_map/pool/pallas_call | solution.py:330
  23.6 0.0 copy-start
  23.6 1.6 %collective-permute-start.7 = (bf16[464,256]{1,0:T(8,128)(2,1)S(1)}, bf16[464,256]{1,0:T(8,128)(2,1)S(1)}, u32[]{:S(2)}, u32[]{:S(2)}) collective-permute-start(bf16[464,256]{1,0:T(8,128)(2,1)S(1)} %get-tuple-element.28), channel_id=1, source_target_pairs={{0,4},{4,8},{8,12},{12,0},{1,5},{5,9},{9,13},{13,1},{2,6},{6,10},{... | collective-permute-start | bytes 712712 | tf_op jit(solution)/shard_map/ppermute | solution.py:364
  25.3 2.6 %collective-permute-start.8 = (bf16[464,256]{1,0:T(8,128)(2,1)S(1)}, bf16[464,256]{1,0:T(8,128)(2,1)S(1)}, u32[]{:S(2)}, u32[]{:S(2)}) collective-permute-start(bf16[464,256]{1,0:T(8,128)(2,1)S(1)} %get-tuple-element.29), channel_id=1, source_target_pairs={{0,8},{4,12},{8,0},{12,4},{1,9},{5,13},{9,1},{13,5},{2,10},{6,14},... | collective-permute-start | bytes 712712 | tf_op jit(solution)/shard_map/ppermute | solution.py:364
  27.9 1.4 %collective-permute-start.9 = (bf16[464,256]{1,0:T(8,128)(2,1)S(1)}, bf16[464,256]{1,0:T(8,128)(2,1)S(1)}, u32[]{:S(2)}, u32[]{:S(2)}) collective-permute-start(bf16[464,256]{1,0:T(8,128)(2,1)S(1)} %get-tuple-element.30), channel_id=1, source_target_pairs={{0,12},{4,0},{8,4},{12,8},{1,13},{5,1},{9,5},{13,9},{2,14},{6,2},{... | collective-permute-start | bytes 712712 | tf_op jit(solution)/shard_map/ppermute | solution.py:364
  29.2 1.0 %collective-permute-start.10 = (bf16[384,256]{1,0:T(8,128)(2,1)S(1)}, bf16[384,256]{1,0:T(8,128)(2,1)S(1)}, u32[]{:S(2)}, u32[]{:S(2)}) collective-permute-start(bf16[384,256]{1,0:T(8,128)(2,1)S(1)} %get-tuple-element.31.refs_6_), channel_id=1, source_target_pairs={{0,2},{2,0},{1,3},{3,1},{4,6},{6,4},{5,7},{7,5},{8,10},{10,8},{9,1... | collective-permute-start | bytes 589832 | tf_op jit(solution)/shard_map/ppermute | solution.py:365
  30.2 8.5 %collective-permute-done.10.refs_4_.refs_7_ = bf16[384,256]{1,0:T(8,128)(2,1)S(1)} collective-permute-done((bf16[384,256]{1,0:T(8,128)(2,1)S(1)}, bf16[384,256]{1,0:T(8,128)(2,1)S(1)}, u32[]{:S(2)}, u32[]{:S(2)}) %collective-permute-start.10) | collective-permute-done | bytes 196640 | tf_op jit(solution)/shard_map/ppermute | solution.py:365
  38.7 0.0 collective-permute-done.7.refs_1_
  38.7 5.0 %collective-permute-done.8.refs_2_ = bf16[464,256]{1,0:T(8,128)(2,1)S(1)} collective-permute-done((bf16[464,256]{1,0:T(8,128)(2,1)S(1)}, bf16[464,256]{1,0:T(8,128)(2,1)S(1)}, u32[]{:S(2)}, u32[]{:S(2)}) %collective-permute-start.8) | collective-permute-done | bytes 237600 | tf_op jit(solution)/shard_map/ppermute | solution.py:364
  43.7 0.0 collective-permute-done.9.refs_3_
  43.7 0.1 sum_parts.1
  43.8 0.0 collective-permute-done.17.refs_1_
  43.8 0.1 collective-permute-start.18
  43.9 0.5 collective-permute-start.14
  44.4 5.6 %collective-permute-start.11 = (bf16[272,256]{1,0:T(8,128)(2,1)S(1)}, bf16[272,256]{1,0:T(8,128)(2,1)S(1)}, u32[]{:S(2)}, u32[]{:S(2)}) collective-permute-start(bf16[272,256]{1,0:T(8,128)(2,1)S(1)} %get-tuple-element.32.refs_0_), channel_id=1, source_target_pairs={{0,4},{4,8},{8,12},{12,0},{1,5},{5,9},{9,13},{13,1},{2,6},{6,10},{... | collective-permute-start | bytes 417800 | tf_op jit(solution)/shard_map/ppermute | solution.py:377
  50.0 1.6 %collective-permute-start.12 = (bf16[272,256]{1,0:T(8,128)(2,1)S(1)}, bf16[272,256]{1,0:T(8,128)(2,1)S(1)}, u32[]{:S(2)}, u32[]{:S(2)}) collective-permute-start(bf16[272,256]{1,0:T(8,128)(2,1)S(1)} %get-tuple-element.32.refs_0_), channel_id=1, source_target_pairs={{0,8},{4,12},{8,0},{12,4},{1,9},{5,13},{9,1},{13,5},{2,10},{6,14},... | collective-permute-start | bytes 417800 | tf_op jit(solution)/shard_map/ppermute | solution.py:377
  51.6 0.8 %collective-permute-start.13 = (bf16[272,256]{1,0:T(8,128)(2,1)S(1)}, bf16[272,256]{1,0:T(8,128)(2,1)S(1)}, u32[]{:S(2)}, u32[]{:S(2)}) collective-permute-start(bf16[272,256]{1,0:T(8,128)(2,1)S(1)} %get-tuple-element.32.refs_0_), channel_id=1, source_target_pairs={{0,12},{4,0},{8,4},{12,8},{1,13},{5,1},{9,5},{13,9},{2,14},{6,2},{... | collective-permute-start | bytes 417800 | tf_op jit(solution)/shard_map/ppermute | solution.py:377
  52.3 0.0 collective-permute-done.14.refs_9_
  52.3 1.0 %collective-permute-start.15 = (bf16[192,256]{1,0:T(8,128)(2,1)S(1)}, bf16[192,256]{1,0:T(8,128)(2,1)S(1)}, u32[]{:S(2)}, u32[]{:S(2)}) collective-permute-start(bf16[192,256]{1,0:T(8,128)(2,1)S(1)} %get-tuple-element.33.refs_8_), channel_id=1, source_target_pairs={{0,2},{2,0},{1,3},{3,1},{4,6},{6,4},{5,7},{7,5},{8,10},{10,8},{9,1... | collective-permute-start | bytes 294920 | tf_op jit(solution)/shard_map/ppermute | solution.py:380
  53.3 0.0 collective-permute-done.18.refs_3_
  53.3 0.0 collective-permute-start.16
  53.3 0.0 copy-done.1
  53.3 0.0 copy-done
  53.3 3.5 %edge_out.1 = (bf16[3072,256]{1,0:T(8,128)(2,1)}, f32[8,128]{1,0:T(8,128)S(1)}) custom-call(s32[3]{0:T(128)S(1)} %pad_add_fusion.idx, bf16[3072,256]{1,0:T(8,128)(2,1)S(1)} %copy-done.1, bf16[3,256,512]{2,1,0:T(8,128)(2,1)S(1)} %copy-done, bf16[1536,256]{1,0:T(8,128)(2,1)S(1)} %get-tuple-element.23.g_own.refs_0_, ...), custom_call_target="tpu_custom_call" | custom-call | flops 805306368 | bytes 6291456 | tf_op jit(solution)/shard_map/edge_out/pallas_call | solution.py:388
  56.8 0.9 %collective-permute-done.15.refs_10_ = bf16[192,256]{1,0:T(8,128)(2,1)S(1)} collective-permute-done((bf16[192,256]{1,0:T(8,128)(2,1)S(1)}, bf16[192,256]{1,0:T(8,128)(2,1)S(1)}, u32[]{:S(2)}, u32[]{:S(2)}) %collective-permute-start.15) | collective-permute-done | bytes 98336 | tf_op jit(solution)/shard_map/ppermute | solution.py:380
  57.7 0.6 collective-permute-done.16.refs_11_
  58.3 0.0 collective-permute-done.11.refs_1_
  58.3 2.7 %collective-permute-done.12.refs_2_ = bf16[272,256]{1,0:T(8,128)(2,1)S(1)} collective-permute-done((bf16[272,256]{1,0:T(8,128)(2,1)S(1)}, bf16[272,256]{1,0:T(8,128)(2,1)S(1)}, u32[]{:S(2)}, u32[]{:S(2)}) %collective-permute-start.12) | collective-permute-done | bytes 139296 | tf_op jit(solution)/shard_map/ppermute | solution.py:377
  61.0 0.0 collective-permute-done.13.refs_3_
  61.0 2.1 %finish.1 = (f32[3,256,256]{2,1,0:T(8,128)}, f32[256,256]{1,0:T(8,128)}, f32[1,256]{1,0:T(1,128)}, f32[384,256]{1,0:T(8,128)}) custom-call(s32[3]{0:T(128)S(1)} %pad_add_fusion.idx, bf16[272,256]{1,0:T(8,128)(2,1)S(1)} %get-tuple-element.32.refs_0_, bf16[272,256]{1,0:T(8,128)(2,1)S(1)} %collective-permute-done.11.refs_1_, ...), custom_call_target="tpu_custom_call" | custom-call | flops 201326592 | bytes 1572864 | tf_op jit(solution)/shard_map/finish/pallas_call | solution.py:408
Async XLA Ops:
  0.6 6.5 %collective-permute-start.3 = (bf16[3072,256]{1,0:T(8,128)(2,1)}, bf16[3072,256]{1,0:T(8,128)(2,1)S(1)}, u32[]{:S(2)}, u32[]{:S(2)}) collective-permute-start(bf16[3072,256]{1,0:T(8,128)(2,1)} %refs_7_.1), channel_id=1, source_target_pairs={{0,1},{1,0},{2,3},{3,2},{4,5},{5,4},{6,7},{7,6},{8,9},{9,8},{10,11... | collective-permute-start | bytes 4718600 | tf_op jit(solution)/shard_map/ppermute | solution.py:260
  1.1 6.0 %collective-permute-start.4 = (bf16[3072,256]{1,0:T(8,128)(2,1)}, bf16[3072,256]{1,0:T(8,128)(2,1)S(1)}, u32[]{:S(2)}, u32[]{:S(2)}) collective-permute-start(bf16[3072,256]{1,0:T(8,128)(2,1)} %cot.1), channel_id=1, source_target_pairs={{0,1},{1,0},{2,3},{3,2},{4,5},{5,4},{6,7},{7,6},{8,9},{9,8},{10,11... | collective-permute-start | bytes 4718600 | tf_op jit(solution)/shard_map/ppermute | solution.py:260
  1.2 5.9 %collective-permute-start = (bf16[384,256]{1,0:T(8,128)(2,1)}, bf16[384,256]{1,0:T(8,128)(2,1)S(1)}, u32[]{:S(2)}, u32[]{:S(2)}) collective-permute-start(bf16[384,256]{1,0:T(8,128)(2,1)} %refs_1_.1), channel_id=1, source_target_pairs={{0,1},{1,0},{2,3},{3,2},{4,5},{5,4},{6,7},{7,6},{8,9},{9,8},{10,11... | collective-permute-start | bytes 589832 | tf_op jit(solution)/shard_map/ppermute | solution.py:260
  1.7 5.5 %collective-permute-start.2 = (bf16[256,256]{1,0:T(8,128)(2,1)}, bf16[256,256]{1,0:T(8,128)(2,1)S(1)}, u32[]{:S(2)}, u32[]{:S(2)}) collective-permute-start(bf16[256,256]{1,0:T(8,128)(2,1)} %refs_5_.2), channel_id=1, source_target_pairs={{0,1},{1,0},{2,3},{3,2},{4,5},{5,4},{6,7},{7,6},{8,9},{9,8},{10,11... | collective-permute-start | bytes 393224 | tf_op jit(solution)/shard_map/ppermute | solution.py:260
  1.7 5.4 %collective-permute-start.1 = (f32[1,256]{1,0:T(1,128)}, f32[1,256]{1,0:T(1,128)S(1)}, u32[]{:S(2)}, u32[]{:S(2)}) collective-permute-start(f32[1,256]{1,0:T(1,128)} %bitcast.10), channel_id=1, source_target_pairs={{0,1},{1,0},{2,3},{3,2},{4,5},{5,4},{6,7},{7,6},{8,9},{9,8},{10,11... | collective-permute-start | bytes 3080 | tf_op jit(solution)/shard_map/ppermute | solution.py:260
  7.1 10.6 %copy-start.2 = (s32[3072]{0:T(1024)S(1)}, s32[3072]{0:T(1024)}, u32[]{:S(2)}) copy-start(s32[3072]{0:T(1024)} %param.21) | copy-start | bytes 36868
  7.2 10.6 %copy-start.3 = (bf16[3072,256]{1,0:T(8,128)(2,1)S(1)}, bf16[3072,256]{1,0:T(8,128)(2,1)}, u32[]{:S(2)}) copy-start(bf16[3072,256]{1,0:T(8,128)(2,1)} %edge_lat.1) | copy-start | bytes 4718596
  7.2 10.6 %copy-start.4 = (bf16[384,256]{1,0:T(8,128)(2,1)S(1)}, bf16[384,256]{1,0:T(8,128)(2,1)}, u32[]{:S(2)}) copy-start(bf16[384,256]{1,0:T(8,128)(2,1)} %node_lat.1) | copy-start | bytes 589828
  7.2 10.6 %copy-start.5 = (s32[3072]{0:T(1024)S(1)}, s32[3072]{0:T(1024)}, u32[]{:S(2)}) copy-start(s32[3072]{0:T(1024)} %param.20) | copy-start | bytes 36868
  13.3 4.4 %collective-permute-start.5 = (bf16[1536,256]{1,0:T(8,128)(2,1)S(1)}, bf16[1536,256]{1,0:T(8,128)(2,1)S(1)}, u32[]{:S(2)}, u32[]{:S(2)}) collective-permute-start(bf16[1536,256]{1,0:T(8,128)(2,1)S(1)} %get-tuple-element.23.g_own.refs_0_), channel_id=1, source_target_pairs={{0,1},{1,0},{2,3},{3,2},{4,5},{5,4},{6,7},{7,6},{8,9},{9,8},{10,11... | collective-permute-start | bytes 2359304 | tf_op jit(solution)/shard_map/ppermute | solution.py:260
  13.8 30.1 %collective-permute-start.17 = (bf16[1536,256]{1,0:T(8,128)(2,1)S(1)}, bf16[1536,256]{1,0:T(8,128)(2,1)S(1)}, u32[]{:S(2)}, u32[]{:S(2)}) collective-permute-start(bf16[1536,256]{1,0:T(8,128)(2,1)S(1)} %get-tuple-element.23.g_own.refs_0_), channel_id=1, source_target_pairs={{0,2},{2,0},{1,3},{3,1},{4,6},{6,4},{5,7},{7,5},{8,10},{10,8},{9,1... | collective-permute-start | bytes 2359304 | tf_op jit(solution)/shard_map/ppermute | solution.py:315
  16.4 1.4 %collective-permute-start.6 = (bf16[272,256]{1,0:T(8,128)(2,1)S(1)}, bf16[272,256]{1,0:T(8,128)(2,1)S(1)}, u32[]{:S(2)}, u32[]{:S(2)}) collective-permute-start(bf16[272,256]{1,0:T(8,128)(2,1)S(1)} %get-tuple-element.26), channel_id=1, source_target_pairs={{0,1},{1,0},{2,3},{3,2},{4,5},{5,4},{6,7},{7,6},{8,9},{9,8},{10,11... | collective-permute-start | bytes 417800 | tf_op jit(solution)/shard_map/ppermute | solution.py:260
  17.8 35.5 %copy-start.1 = (bf16[3072,256]{1,0:T(8,128)(2,1)S(1)}, bf16[3072,256]{1,0:T(8,128)(2,1)}, u32[]{:S(2)}) copy-start(bf16[3072,256]{1,0:T(8,128)(2,1)} %cot.1) | copy-start | bytes 4718596
  23.6 29.7 %copy-start = (bf16[3,256,512]{2,1,0:T(8,128)(2,1)S(1)}, bf16[3,256,512]{2,1,0:T(8,128)(2,1)}, u32[]{:S(2)}) copy-start(bf16[3,256,512]{2,1,0:T(8,128)(2,1)} %refs_5_.3) | copy-start | bytes 2359300
  23.6 15.0 %collective-permute-start.7 = (bf16[464,256]{1,0:T(8,128)(2,1)S(1)}, bf16[464,256]{1,0:T(8,128)(2,1)S(1)}, u32[]{:S(2)}, u32[]{:S(2)}) collective-permute-start(bf16[464,256]{1,0:T(8,128)(2,1)S(1)} %get-tuple-element.28), channel_id=1, source_target_pairs={{0,4},{4,8},{8,12},{12,0},{1,5},{5,9},{9,13},{13,1},{2,6},{6,10},{... | collective-permute-start | bytes 712712 | tf_op jit(solution)/shard_map/ppermute | solution.py:364
  25.3 18.4 %collective-permute-start.8 = (bf16[464,256]{1,0:T(8,128)(2,1)S(1)}, bf16[464,256]{1,0:T(8,128)(2,1)S(1)}, u32[]{:S(2)}, u32[]{:S(2)}) collective-permute-start(bf16[464,256]{1,0:T(8,128)(2,1)S(1)} %get-tuple-element.29), channel_id=1, source_target_pairs={{0,8},{4,12},{8,0},{12,4},{1,9},{5,13},{9,1},{13,5},{2,10},{6,14},... | collective-permute-start | bytes 712712 | tf_op jit(solution)/shard_map/ppermute | solution.py:364
  27.9 15.8 %collective-permute-start.9 = (bf16[464,256]{1,0:T(8,128)(2,1)S(1)}, bf16[464,256]{1,0:T(8,128)(2,1)S(1)}, u32[]{:S(2)}, u32[]{:S(2)}) collective-permute-start(bf16[464,256]{1,0:T(8,128)(2,1)S(1)} %get-tuple-element.30), channel_id=1, source_target_pairs={{0,12},{4,0},{8,4},{12,8},{1,13},{5,1},{9,5},{13,9},{2,14},{6,2},{... | collective-permute-start | bytes 712712 | tf_op jit(solution)/shard_map/ppermute | solution.py:364
  29.2 9.5 %collective-permute-start.10 = (bf16[384,256]{1,0:T(8,128)(2,1)S(1)}, bf16[384,256]{1,0:T(8,128)(2,1)S(1)}, u32[]{:S(2)}, u32[]{:S(2)}) collective-permute-start(bf16[384,256]{1,0:T(8,128)(2,1)S(1)} %get-tuple-element.31.refs_6_), channel_id=1, source_target_pairs={{0,2},{2,0},{1,3},{3,1},{4,6},{6,4},{5,7},{7,5},{8,10},{10,8},{9,1... | collective-permute-start | bytes 589832 | tf_op jit(solution)/shard_map/ppermute | solution.py:365
  43.8 9.5 %collective-permute-start.18 = (bf16[1536,256]{1,0:T(8,128)(2,1)S(1)}, bf16[1536,256]{1,0:T(8,128)(2,1)S(1)}, u32[]{:S(2)}, u32[]{:S(2)}) collective-permute-start(bf16[1536,256]{1,0:T(8,128)(2,1)S(1)} %collective-permute-done.17.refs_1_), channel_id=1, source_target_pairs={{0,1},{1,0},{2,3},{3,2},{4,5},{5,4},{6,7},{7,6},{8,9},{9,8},{10,11... | collective-permute-start | bytes 2359304 | tf_op jit(solution)/shard_map/ppermute | solution.py:260
  43.9 8.4 %collective-permute-start.14 = (bf16[192,256]{1,0:T(8,128)(2,1)S(1)}, bf16[192,256]{1,0:T(8,128)(2,1)S(1)}, u32[]{:S(2)}, u32[]{:S(2)}) collective-permute-start(bf16[192,256]{1,0:T(8,128)(2,1)S(1)} %get-tuple-element.33.refs_8_), channel_id=1, source_target_pairs={{0,1},{1,0},{2,3},{3,2},{4,5},{5,4},{6,7},{7,6},{8,9},{9,8},{10,11... | collective-permute-start | bytes 294920 | tf_op jit(solution)/shard_map/ppermute | solution.py:260
  44.4 13.9 %collective-permute-start.11 = (bf16[272,256]{1,0:T(8,128)(2,1)S(1)}, bf16[272,256]{1,0:T(8,128)(2,1)S(1)}, u32[]{:S(2)}, u32[]{:S(2)}) collective-permute-start(bf16[272,256]{1,0:T(8,128)(2,1)S(1)} %get-tuple-element.32.refs_0_), channel_id=1, source_target_pairs={{0,4},{4,8},{8,12},{12,0},{1,5},{5,9},{9,13},{13,1},{2,6},{6,10},{... | collective-permute-start | bytes 417800 | tf_op jit(solution)/shard_map/ppermute | solution.py:377
  50.0 11.0 %collective-permute-start.12 = (bf16[272,256]{1,0:T(8,128)(2,1)S(1)}, bf16[272,256]{1,0:T(8,128)(2,1)S(1)}, u32[]{:S(2)}, u32[]{:S(2)}) collective-permute-start(bf16[272,256]{1,0:T(8,128)(2,1)S(1)} %get-tuple-element.32.refs_0_), channel_id=1, source_target_pairs={{0,8},{4,12},{8,0},{12,4},{1,9},{5,13},{9,1},{13,5},{2,10},{6,14},... | collective-permute-start | bytes 417800 | tf_op jit(solution)/shard_map/ppermute | solution.py:377
  51.6 9.4 %collective-permute-start.13 = (bf16[272,256]{1,0:T(8,128)(2,1)S(1)}, bf16[272,256]{1,0:T(8,128)(2,1)S(1)}, u32[]{:S(2)}, u32[]{:S(2)}) collective-permute-start(bf16[272,256]{1,0:T(8,128)(2,1)S(1)} %get-tuple-element.32.refs_0_), channel_id=1, source_target_pairs={{0,12},{4,0},{8,4},{12,8},{1,13},{5,1},{9,5},{13,9},{2,14},{6,2},{... | collective-permute-start | bytes 417800 | tf_op jit(solution)/shard_map/ppermute | solution.py:377
  52.3 5.4 %collective-permute-start.15 = (bf16[192,256]{1,0:T(8,128)(2,1)S(1)}, bf16[192,256]{1,0:T(8,128)(2,1)S(1)}, u32[]{:S(2)}, u32[]{:S(2)}) collective-permute-start(bf16[192,256]{1,0:T(8,128)(2,1)S(1)} %get-tuple-element.33.refs_8_), channel_id=1, source_target_pairs={{0,2},{2,0},{1,3},{3,1},{4,6},{6,4},{5,7},{7,5},{8,10},{10,8},{9,1... | collective-permute-start | bytes 294920 | tf_op jit(solution)/shard_map/ppermute | solution.py:380
  53.3 5.0 %collective-permute-start.16 = (bf16[192,256]{1,0:T(8,128)(2,1)S(1)}, bf16[192,256]{1,0:T(8,128)(2,1)S(1)}, u32[]{:S(2)}, u32[]{:S(2)}) collective-permute-start(bf16[192,256]{1,0:T(8,128)(2,1)S(1)} %get-tuple-element.33.refs_8_), channel_id=1, source_target_pairs={{0,3},{1,2},{2,1},{3,0},{4,7},{5,6},{6,5},{7,4},{8,11},{9,10},{10,... | collective-permute-start | bytes 294920 | tf_op jit(solution)/shard_map/ppermute | solution.py:382

commit v4 on v3

v4 whole, which is shorter than its diff:
```python
import functools
import math

import jax
import jax.numpy as jnp
from jax import lax
from jax.experimental import pallas as pl
from jax.experimental.pallas import tpu as pltpu
from jax.sharding import PartitionSpec as P

F32 = jnp.float32
BF16 = jnp.bfloat16
PAD = 16


def dot_nn(a, b):
    return lax.dot_general(a, b, (((1,), (0,)), ((), ())), preferred_element_type=F32)


def dot_nt(a, b):
    return lax.dot_general(a, b, (((1,), (1,)), ((), ())), preferred_element_type=F32)


def dot_tn(a, b):
    return lax.dot_general(a, b, (((0,), (0,)), ((), ())), preferred_element_type=F32)


def params(mib=48):
    return pltpu.CompilerParams(vmem_limit_bytes=mib * 1024 * 1024)


def cost(flops, nbytes):
    return pl.CostEstimate(flops=int(flops), bytes_accessed=int(nbytes), transcendentals=0)


def whole(shape):
    return pl.BlockSpec(shape, lambda *_: (0,) * len(shape))


def in_hbm(x):
    return pltpu.with_memory_space_constraint(x, pltpu.HBM)


def ring(size, step):
    return [(i, (i + step) % size) for i in range(size)]


def split_rows(row, width):
    parts = [row[:, j * width : (j + 1) * width] for j in range(row.shape[1] // width)]
    parts.append(jnp.zeros((PAD - len(parts), width), row.dtype))
    return jnp.concatenate(parts, axis=0)


def own_kernel(steps, idx, *refs):
    recv_in, agg_in, cot_in, hid_in, x_in = refs[:5]
    upstream, picked, act_out, slope_out, x_out = refs[5:10]
    recv, agg, cot, hid, sems, x_sem = refs[10:]
    half, feat_width = act_out.shape
    nodes_dev = agg.shape[0]
    rows = half // steps
    first = pl.multiple_of(idx[0] * half, 128)
    copies = [
        pltpu.make_async_copy(recv_in.at[:, pl.ds(first, half)], recv, sems.at[0]),
        pltpu.make_async_copy(agg_in, agg, sems.at[1]),
        pltpu.make_async_copy(hid_in.at[pl.ds(first, half), :], hid, sems.at[2]),
        pltpu.make_async_copy(cot_in.at[pl.ds(first, half), :], cot, sems.at[3]),
    ]
    x_copy = pltpu.make_async_copy(x_in.at[pl.ds(first, half), :], x_out, x_sem)
    for copy in copies:
        copy.start()
    x_copy.start()
    for copy in copies:
        copy.wait()
    for step in range(steps):
        at = slice(step * rows, (step + 1) * rows)
        column = jnp.transpose(jnp.broadcast_to(recv[:, at], (8, rows)))[:, :1] - idx[1] * nodes_dev
        picks = lax.broadcasted_iota(jnp.int32, (rows, nodes_dev), 1) == column
        picks = jnp.where(picks, 1.0, 0.0).astype(BF16)
        picked[at, :] = picks
        upstream[at, :] = cot[at, :].astype(F32) + dot_nn(picks, agg[...])
        value = hid[at, :].astype(F32)
        sig = 1.0 / (1.0 + jnp.exp(-value))
        act_out[at, :] = (value * sig).astype(BF16)
        slope_out[at, :] = sig * (1.0 + value * (1.0 - sig))
    x_copy.wait()


def edge_kernel(steps, idx, *refs):
    upstream, picked, act_in, slope, x_in, gain_own, gain_sib, w_own, w_sib, agg_sib, x_far, cot_far = refs[:12]
    pre_grad, wo_own, gain_out, small = refs[12:16]
    x_held, cot_held, acc_sib, sems = refs[16:]
    half, feat_width = pre_grad.shape
    half_width = x_in.shape[1]
    width = 2 * half_width
    rows = half // steps
    first = pl.multiple_of(idx[0] * half, 128)
    tiles = []
    for step in range(steps):
        here = pl.ds(step * rows, rows)
        there = pl.ds(pl.multiple_of(first + step * rows, 128), rows)
        tiles.append(
            (
                pltpu.make_async_copy(x_far.at[there, :], x_held.at[here, :], sems.at[0, step]),
                pltpu.make_async_copy(cot_far.at[there, :], cot_held.at[here, :], sems.at[1, step]),
            )
        )
    for copies in tiles:
        for copy in copies:
            copy.start()
    gsum_own = jnp.zeros((1, half_width), F32)
    gsum_sib = jnp.zeros((1, half_width), F32)

    def row_mean(a, b):
        return jnp.sum(a + b, axis=1, keepdims=True) * (1.0 / width)

    for step in range(steps):
        at = slice(step * rows, (step + 1) * rows)
        for copy in tiles[step]:
            copy.wait()
        v_own = x_in[at, :].astype(F32)
        v_sib = x_held[at, :].astype(F32)
        mean = row_mean(v_own, v_sib)
        v_own = v_own - mean
        v_sib = v_sib - mean
        inv = lax.rsqrt(row_mean(v_own * v_own, v_sib * v_sib) + 1e-05)
        n_own = v_own * inv
        n_sib = v_sib * inv
        up_own = upstream[at, :]
        up_sib = cot_held[at, :].astype(F32) + dot_nn(picked[at, :], agg_sib[...])
        wt_own = gain_own[...] * up_own
        wt_sib = gain_sib[...] * up_sib
        mean_first = row_mean(wt_own, wt_sib)
        mean_cross = row_mean(wt_own * n_own, wt_sib * n_sib)
        g_own = (inv * (wt_own - mean_first - n_own * mean_cross)).astype(BF16)
        g_sib = (inv * (wt_sib - mean_first - n_sib * mean_cross)).astype(BF16)
        hidden = dot_nt(g_own, w_own[...]) + dot_nt(g_sib, w_sib[...])
        pre_grad[at, :] = (hidden * slope[at, :]).astype(BF16)
        act = act_in[at, :]
        if step == 0:
            wo_own[...] = dot_tn(g_own, act)
            acc_sib[...] = dot_tn(g_sib, act)
        else:
            wo_own[...] += dot_tn(g_own, act)
            acc_sib[...] += dot_tn(g_sib, act)
        gsum_own = gsum_own + jnp.sum(up_own * n_own, axis=0, keepdims=True)
        gsum_sib = gsum_sib + jnp.sum(up_sib * n_sib, axis=0, keepdims=True)

    gain_out[...] = gsum_own
    small[:half_width, :] = acc_sib[...].astype(BF16)
    small[half_width:, :] = split_rows(gsum_sib, feat_width).astype(BF16)


def add_edges(sibling, steps, idx, grad, ins, helds, sems, sums, fresh):
    grads, pooled, by_recv = sums
    core, shard = idx[0], idx[1]
    half, feat_width = grad.shape
    rows = half // steps
    side = 1 - core if sibling else core
    first = pl.multiple_of(side * half, 128)
    copies = []
    for j, (src, dst) in enumerate(zip(ins, helds)):
        src = src.at[:, pl.ds(first, half)] if j < 2 else src.at[pl.ds(first, half), :]
        copies.append(pltpu.make_async_copy(src, dst, sems.at[j]))
    for copy in copies:
        copy.start()
    send_row, recv_row, edge_lat, send_lat = helds
    nodes_dev, half_width = by_recv.shape[0], edge_lat.shape[1]
    half_nodes = nodes_dev // 2

    def put(ref, at, value, step):
        ref[at, :] = value if fresh and step == 0 else ref[at, :] + value

    copies[0].wait()
    copies[1].wait()
    for step in range(steps):
        at = slice(step * rows, (step + 1) * rows)
        node_id = lax.broadcasted_iota(jnp.int32, (nodes_dev, rows), 0) + shard * nodes_dev
        picks = jnp.where(node_id == recv_row[:, at], 1.0, 0.0).astype(BF16)
        put(by_recv, slice(0, nodes_dev), dot_nn(picks, grad[at, :]), step)
        half_id = lax.broadcasted_iota(jnp.int32, (half_nodes, rows), 0) + core * half_nodes
        for dest in range(pooled.shape[0] // half_nodes):
            picks = jnp.where(half_id + dest * nodes_dev == send_row[:, at], 1.0, 0.0).astype(BF16)
            put(pooled, slice(dest * half_nodes, (dest + 1) * half_nodes), dot_nn(picks, grad[at, :]), step)
    copies[2].wait()
    copies[3].wait()
    for step in range(steps):
        at = slice(step * rows, (step + 1) * rows)
        put(grads, slice(0, half_width), dot_tn(edge_lat[at, :], grad[at, :]), step)
        put(grads, slice(half_width, 2 * half_width), dot_tn(send_lat[at, :], grad[at, :]), step)


def pool_own_kernel(steps, idx, grad, *refs):
    add_edges(False, steps, idx, grad, refs[:4], refs[7:11], refs[11], refs[4:7], True)


def pool_kernel(shards, steps, idx, grad, *refs):
    ins, (part_grads, part_pooled, part_recv) = refs[:4], refs[4:7]
    node_lat, wo_own, gain_own, small = refs[7:11]
    outs, recv_out = refs[11 : 11 + shards], refs[11 + shards]
    grads, pooled, by_recv, *helds, sems = refs[12 + shards :]
    shard = idx[1]
    half_width, feat_width = wo_own.shape
    half_nodes = node_lat.shape[0] // 2
    grads[: 2 * half_width, :] = part_grads[...]
    pooled[...] = part_pooled[...]
    by_recv[...] = part_recv[...]
    add_edges(True, steps, idx, grad, ins, helds, sems, (grads, pooled, by_recv), False)
    sums = by_recv[...]
    high = sums.astype(BF16)
    low = (sums - high.astype(F32)).astype(BF16)
    grads[2 * half_width : 3 * half_width, :] = dot_tn(node_lat[...], high) + dot_tn(node_lat[...], low)
    grads[3 * half_width :, :] = wo_own[...] + small[:half_width, :].astype(F32)
    gain = split_rows(gain_own[...], feat_width) + small[half_width:, :].astype(F32)
    recv_out[...] = high
    block = 4 * half_width // shards
    for k in range(shards):
        dest = lax.rem(shard + k, shards)
        kind = outs[k].dtype
        w_rows = grads[pl.ds(pl.multiple_of(dest * block, 16), block), :]
        outs[k][:block, :] = w_rows.astype(kind)
        outs[k][block : block + PAD, :] = gain.astype(kind)
        s_rows = pooled[pl.ds(pl.multiple_of(dest * half_nodes, 16), half_nodes), :]
        outs[k][block + PAD :, :] = s_rows.astype(kind)


def sum_kernel(shards, scale, idx, *refs):
    blocks = refs[:shards]
    w_total, s_total, gain_total, gain_held = refs[-4:]
    total = blocks[0][...].astype(F32)
    for ref in blocks[1:]:
        total = total + ref[...].astype(F32)
    rows = w_total.shape[0]
    w_total[...] = total[:rows].astype(BF16)
    s_total[...] = total[rows + PAD :].astype(BF16)
    for k in range(shards):
        source = lax.rem(idx[1] - k + shards, shards)
        sent = blocks[k][rows : rows + PAD, :].astype(BF16).astype(F32)
        gain_held[pl.ds(pl.multiple_of(source * PAD, PAD), PAD), :] = sent
    gain = gain_held[:PAD, :]
    for k in range(1, shards):
        gain = gain + gain_held[k * PAD : (k + 1) * PAD, :]
    feat_width = gain.shape[1]
    for j in range(gain_total.shape[1] // feat_width):
        gain_total[:, j * feat_width : (j + 1) * feat_width] = gain[j : j + 1, :] * scale


def edge_out_kernel(feats, steps, idx, cot, w_edge, *refs):
    own = refs[:feats]
    sib = refs[feats : 2 * feats]
    out, token, held = refs[2 * feats :]
    token[...] = jnp.zeros_like(token)
    step = pl.program_id(0)
    feat_width = own[0].shape[1]
    for k in range(feats):
        source = lax.rem(idx[2] - k + feats, feats)
        piece = jnp.where(step < steps // 2, own[k][...], sib[k][...])
        held[:, pl.ds(pl.multiple_of(source * feat_width, 128), feat_width)] = piece
    out[...] = (cot[...].astype(F32) + dot_nt(held[...], w_edge[...])).astype(BF16)


def finish_kernel(shards, feats, scale, idx, *refs):
    totals = refs[:1] + refs[1:shards][::-1]
    w_send, w_recv = refs[shards : shards + 2]
    by_recv = refs[shards + 2 : shards + 2 + feats]
    sums = refs[shards + 2 + feats : shards + 2 + 3 * feats][::-1]
    gain_in = refs[shards + 2 + 3 * feats]
    w_in_grad, w_out_grad, gain_grad, node_grad, held, held_send, held_recv = refs[-7:]
    gain_grad[...] = gain_in[...]
    rows, feat_width = sums[0].shape
    for k in range(feats):
        source = lax.rem(idx[2] - k + feats, feats)
        there = pl.ds(pl.multiple_of(source * feat_width, 128), feat_width)
        held_recv[:, there] = by_recv[k][...]
        for side in range(2):
            at = pl.ds(pl.multiple_of((idx[0] if side == 0 else 1 - idx[0]) * rows, 16), rows)
            held_send[at, there] = sums[2 * k + side][...]
    node_grad[...] = dot_nt(held_send[...], w_send[...]) + dot_nt(held_recv[...], w_recv[...])

    half_width = w_in_grad.shape[1]
    block = 4 * half_width // shards
    for k in range(shards):
        source = lax.rem(idx[1] - k + shards, shards)
        held[pl.ds(pl.multiple_of(source * block, 16), block), :] = totals[k][...].astype(F32) * scale

    for k in range(3):
        w_in_grad[k] = held[k * half_width : (k + 1) * half_width, :]
    w_out_grad[...] = jnp.transpose(held[3 * half_width :, :])


def body(
    node_latents, edge_latents, sender_latents, pre_hidden, pre_norm, norm_gain, w_in, w_out, senders, receivers,
    edge_cotangent, agg_cotangent,
):
    shards = lax.axis_size("nodes")
    feats = lax.axis_size("feat")
    core, shard, feat = (lax.axis_index(name) for name in ("chan", "nodes", "feat"))
    idx = jnp.stack([core, shard, feat]).astype(jnp.int32)
    nodes_dev, half_width = node_latents.shape
    edges = edge_latents.shape[0]
    feat_width = pre_hidden.shape[1]
    hidden_width = w_in.shape[2]
    half = edges // 2
    half_nodes = nodes_dev // 2
    scale = 1.0 / math.sqrt(edges * shards)

    def over_chan(x):
        return lax.ppermute(x, "chan", [(0, 1), (1, 0)])

    pre_norm_sib = over_chan(pre_norm)
    cot_sib = over_chan(edge_cotangent)
    agg_sib = over_chan(agg_cotangent)
    w_out_sib = over_chan(w_out)
    gain_own = norm_gain.reshape(1, half_width)
    gain_sib = over_chan(gain_own)
    recv_row = receivers.reshape(1, edges)
    send_row = senders.reshape(1, edges)

    tile = 768
    steps = half // tile
    wide = (tile, half_width)
    narrow = (tile, feat_width)
    smem = pl.BlockSpec(memory_space=pltpu.SMEM)
    vmem = pl.BlockSpec(memory_space=pltpu.VMEM)
    edge_steps = 3
    any_space = pl.BlockSpec(memory_space=pl.ANY)
    upstream, picked, act, slope, x_near = pl.pallas_call(
        functools.partial(own_kernel, edge_steps),
        in_specs=[smem] + [any_space] * 5,
        out_specs=[vmem] * 5,
        out_shape=[
            jax.ShapeDtypeStruct((half, half_width), F32),
            jax.ShapeDtypeStruct((half, nodes_dev), BF16),
            jax.ShapeDtypeStruct((half, feat_width), BF16),
            jax.ShapeDtypeStruct((half, feat_width), F32),
            jax.ShapeDtypeStruct((half, half_width), BF16),
        ],
        scratch_shapes=[
            pltpu.VMEM((1, half), jnp.int32),
            pltpu.VMEM((nodes_dev, half_width), BF16),
            pltpu.VMEM((half, half_width), BF16),
            pltpu.VMEM((half, feat_width), BF16),
            pltpu.SemaphoreType.DMA((4,)),
            pltpu.SemaphoreType.DMA,
        ],
        compiler_params=params(24),
        cost_estimate=cost(2 * half * nodes_dev * half_width, 8 * half * half_width),
        name="own_edges",
    )(idx, *(in_hbm(x) for x in (recv_row, agg_cotangent, edge_cotangent, pre_hidden, pre_norm)))
    pre_own, wo_own, gain_sum, small = pl.pallas_call(
        functools.partial(edge_kernel, edge_steps),
        in_specs=[smem] + [vmem] * 10 + [any_space] * 2,
        out_specs=[vmem] * 4,
        out_shape=[
            jax.ShapeDtypeStruct((half, feat_width), BF16),
            jax.ShapeDtypeStruct((half_width, feat_width), F32),
            jax.ShapeDtypeStruct((1, half_width), F32),
            jax.ShapeDtypeStruct((half_width + PAD, feat_width), BF16),
        ],
        scratch_shapes=[
            pltpu.VMEM((half, half_width), BF16),
            pltpu.VMEM((half, half_width), BF16),
            pltpu.VMEM((half_width, feat_width), F32),
            pltpu.SemaphoreType.DMA((2, edge_steps)),
        ],
        compiler_params=params(32),
        cost_estimate=cost(4 * half * (nodes_dev + 2 * feat_width) * half_width, 10 * half * half_width),
        name="edge_norm",
    )(
        idx, upstream, picked, act, slope, x_near, gain_own, gain_sib, w_out, w_out_sib, agg_sib, pre_norm_sib,
        cot_sib,
    )

    pre_sib = over_chan(pre_own)
    small_sib = over_chan(small)

    def by_edge(i, s):
        return jnp.where(i < steps, s[0] * steps + i, (1 - s[0]) * steps + i - steps)

    def first_half(i, s):
        return (jnp.minimum(i, steps - 1), 0)

    def second_half(i, s):
        return (jnp.maximum(i - steps, 0), 0)

    block = 4 * half_width // shards
    rows_out = block + PAD + half_nodes
    pool_outs = [jax.ShapeDtypeStruct((rows_out, feat_width), F32 if k == 0 else BF16) for k in range(shards)]
    pool_outs.append(jax.ShapeDtypeStruct((nodes_dev, feat_width), BF16))
    pool_steps = 1
    sum_shapes = [
        jax.ShapeDtypeStruct((rows, feat_width), F32) for rows in (2 * half_width, shards * half_nodes, nodes_dev)
    ]
    held_shapes = [
        pltpu.VMEM((1, half), jnp.int32),
        pltpu.VMEM((1, half), jnp.int32),
        pltpu.VMEM((half, half_width), BF16),
        pltpu.VMEM((half, half_width), BF16),
        pltpu.SemaphoreType.DMA((4,)),
    ]
    pool_cost = cost(
        edges * feat_width * (nodes_dev + shards * half_nodes + 2 * half_width), 4 * edges * half_width
    )
    by_edge_args = [in_hbm(x) for x in (send_row, recv_row, edge_latents, sender_latents)]
    any_space = pl.BlockSpec(memory_space=pl.ANY)
    part_sums = pl.pallas_call(
        functools.partial(pool_own_kernel, pool_steps),
        in_specs=[smem, vmem] + [any_space] * 4,
        out_specs=[vmem] * 3,
        out_shape=sum_shapes,
        scratch_shapes=held_shapes,
        compiler_params=params(),
        cost_estimate=pool_cost,
        name="pool_own",
    )(idx, pre_own, *by_edge_args)
    *parts, by_recv = pl.pallas_call(
        functools.partial(pool_kernel, shards, pool_steps),
        in_specs=[smem, vmem] + [any_space] * 4 + [vmem] * 7,
        out_specs=[vmem] * (shards + 1),
        out_shape=pool_outs,
        scratch_shapes=[
            pltpu.VMEM((4 * half_width, feat_width), F32),
            pltpu.VMEM((shards * half_nodes, feat_width), F32),
            pltpu.VMEM((nodes_dev, feat_width), F32),
        ]
        + held_shapes,
        compiler_params=params(),
        cost_estimate=pool_cost,
        name="pool",
    )(idx, pre_sib, *by_edge_args, *part_sums, node_latents, wo_own, gain_sum, small_sib)
    pre_sent, by_recv = lax.optimization_barrier((pre_own, by_recv))
    crossed_own = [pre_own] + [lax.ppermute(pre_sent, "feat", ring(feats, k)) for k in range(1, feats)]
    arrived = [parts[0]] + [lax.ppermute(parts[k], "nodes", ring(shards, k)) for k in range(1, shards)]
    recv_all = [by_recv] + [lax.ppermute(by_recv, "feat", ring(feats, k)) for k in range(1, feats)]
    w_total, s_total, gain_sum = pl.pallas_call(
        functools.partial(sum_kernel, shards, scale),
        in_specs=[smem] + [vmem] * shards + [any_space] * (feats - 1),
        out_shape=[
            jax.ShapeDtypeStruct((block, feat_width), BF16),
            jax.ShapeDtypeStruct((half_nodes, feat_width), BF16),
            jax.ShapeDtypeStruct((1, half_width), F32),
        ],
        scratch_shapes=[pltpu.VMEM((shards * PAD, feat_width), F32)],
        compiler_params=params(),
        cost_estimate=cost(rows_out * feat_width * shards, 4 * rows_out * feat_width * shards),
        name="sum_parts",
    )(idx, *arrived, *recv_all[1:])
    w_all = [w_total] + [lax.ppermute(w_total, "nodes", ring(shards, k)) for k in range(1, shards)]
    s_all = [s_total, over_chan(s_total)]
    for k in range(1, feats):
        s_all.append(lax.ppermute(s_total, "feat", ring(feats, k)))
        flip = [(2 * f + c, 2 * ((f + k) % feats) + 1 - c) for f in range(feats) for c in range(2)]
        s_all.append(lax.ppermute(s_total, ("feat", "chan"), flip))

    passed, _ = lax.optimization_barrier((crossed_own[1:], s_total))
    crossed_own = [pre_own] + passed
    crossed_sib = [pre_sib] + [over_chan(x) for x in passed]

    edge_grad, edge_token = pl.pallas_call(
        functools.partial(edge_out_kernel, feats, 2 * steps),
        grid_spec=pltpu.PrefetchScalarGridSpec(
            num_scalar_prefetch=1,
            grid=(2 * steps,),
            in_specs=[
                pl.BlockSpec(wide, lambda i, s: (by_edge(i, s), 0)),
                pl.BlockSpec((None, half_width, hidden_width), lambda i, s: (0, 0, 0)),
            ]
            + [pl.BlockSpec(narrow, first_half)] * feats
            + [pl.BlockSpec(narrow, second_half)] * feats,
            out_specs=[pl.BlockSpec(wide, lambda i, s: (by_edge(i, s), 0)), whole((8, 128))],
            scratch_shapes=[pltpu.VMEM((tile, hidden_width), BF16)],
        ),
        out_shape=[jax.ShapeDtypeStruct((edges, half_width), BF16), jax.ShapeDtypeStruct((8, 128), F32)],
        compiler_params=params(),
        cost_estimate=cost(2 * edges * hidden_width * half_width, 8 * edges * half_width),
        name="edge_out",
    )(idx, edge_cotangent, w_in, *crossed_own, *crossed_sib)

    w_in_grad, w_out_grad, gain_grad, node_grad = pl.pallas_call(
        functools.partial(finish_kernel, shards, feats, scale),
        grid=(1,),
        in_specs=[smem]
        + [whole((block, feat_width))] * shards
        + [
            pl.BlockSpec((None, half_width, hidden_width), lambda *_: (1, 0, 0)),
            pl.BlockSpec((None, half_width, hidden_width), lambda *_: (2, 0, 0)),
        ]
        + [whole((nodes_dev, feat_width))] * feats
        + [whole((half_nodes, feat_width))] * (2 * feats)
        + [whole((1, half_width))]
        + [pl.BlockSpec(memory_space=pl.ANY)],
        out_specs=[
            whole((3, half_width, feat_width)),
            whole((feat_width, half_width)),
            whole((1, half_width)),
            whole((nodes_dev, half_width)),
        ],
        out_shape=[
            jax.ShapeDtypeStruct((3, half_width, feat_width), F32),
            jax.ShapeDtypeStruct((feat_width, half_width), F32),
            jax.ShapeDtypeStruct((1, half_width), F32),
            jax.ShapeDtypeStruct((nodes_dev, half_width), F32),
        ],
        scratch_shapes=[
            pltpu.VMEM((4 * half_width, feat_width), F32),
            pltpu.VMEM((nodes_dev, hidden_width), BF16),
            pltpu.VMEM((nodes_dev, hidden_width), BF16),
        ],
        compiler_params=params(),
        cost_estimate=cost(4 * nodes_dev * hidden_width * half_width, 8 * nodes_dev * hidden_width),
        name="finish",
    )(idx, w_total, *w_all[:0:-1], w_in, w_in, *recv_all, *s_all[::-1], gain_sum, edge_token)
    return (node_grad, edge_grad, w_in_grad, w_out_grad, gain_grad.reshape(half_width))


def solution(mesh):
    placed = (
        P(("groups", "nodes"), "chan"),
        P(("groups", "nodes"), "chan"),
        P(("groups", "nodes"), "chan"),
        P(("groups", "nodes"), "feat"),
        P(("groups", "nodes"), "chan"),
        P("chan"),
        P(None, "chan", None),
        P("feat", "chan"),
        P(("groups", "nodes")),
        P(("groups", "nodes")),
        P(("groups", "nodes"), "chan"),
        P(("groups", "nodes"), "chan"),
    )
    return jax.shard_map(
        body,
        mesh=mesh,
        in_specs=placed,
        out_specs=(
            P(("groups", "nodes"), "chan"),
            P(("groups", "nodes"), "chan"),
            P("groups", "chan", "feat"),
            P(("groups", "feat"), "chan"),
            P(("groups", "chan")),
        ),
        check_vma=False,
    )
```

time: 63.9 us -> 61.3 us (0.959)
  waiting for transfers between devices: 23.9 us -> 20.1 us
  Pallas kernels: 17.7 us -> 20.8 us
  starting transfers between devices: 20.7 us -> 18.9 us
    ppermute x1, waiting for transfers between devices: 8.48 us -> 16 us  [body(): lax.ppermute(by_recv, 'feat', ring(feats, k))]
    pallas_call x2 -> x4, Pallas kernels: 5.93 us -> 11.1 us  [the longest x1 3.71 us: body(): pl.pallas_call(functools.partial(own_kernel, edge_steps), in_specs=[smem]...]
    ppermute x3, waiting for transfers between devices: 5.04 us -> 0.01 us  [body(): lax.ppermute(parts[k], 'nodes', ring(shards, k))]
    ppermute x9, waiting for transfers between devices: 6.17 us -> 1.17 us  [over_chan(): return lax.ppermute(x, 'chan', [(0, 1), (1, 0)])]
    ppermute x3, starting transfers between devices: 7.92 us -> 5.76 us  [body(): lax.ppermute(w_total, 'nodes', ring(shards, k))]
    pallas_call x1, Pallas kernels: 6.12 us -> 4.02 us  [body(): pl.pallas_call(functools.partial(edge_kernel, edge_steps), in_specs=[smem...]
    ppermute x3, waiting for transfers between devices: 2.66 us -> 1.34 us  [body(): lax.ppermute(w_total, 'nodes', ring(shards, k))]
    ppermute x1, waiting for transfers between devices: 0.61 us -> 1.58 us  [body(): s_all.append(lax.ppermute(s_total, ('feat', 'chan'), flip))]
  transfers between devices with their start and end apart: 19 -> 19, of which waited for: 7 -> 5; matrix products, arithmetic and copies ran while one was open for 0% -> 0% of each run, Pallas kernels for 15% -> 18%
where the time goes in v4:
time: 61.3 us; the launch traced here: 60.7 us
  Pallas kernels  20.8 us (34%)
  waiting for transfers between devices  20.1 us (33%)
  starting transfers between devices  18.9 us (31%)
  between operations  0.77 us (1%)
    ppermute x1, waiting for transfers between devices, body(): lax.ppermute(by_recv, 'feat', ring(feats, k))  16 us
    ppermute x3, starting transfers between devices, body(): lax.ppermute(w_total, 'nodes', ring(shards, k))  5.76 us
    ppermute x3, starting transfers between devices, body(): lax.ppermute(parts[k], 'nodes', ring(shards, k))  5.52 us
    pallas_call x1, Pallas kernels, body(): pl.pallas_call(functools.partial(edge_kernel, edge_steps), in_specs=[smem...  4.02 us
    pallas_call x1, Pallas kernels, body(): pl.pallas_call(functools.partial(own_kernel, edge_steps), in_specs=[smem]...  3.71 us
    pallas_call x1, Pallas kernels, body(): pl.pallas_call(functools.partial(pool_kernel, shards, pool_steps), in_spe...  3.64 us
    pallas_call x1, Pallas kernels, body(): pl.pallas_call(functools.partial(edge_out_kernel, feats, 2 * steps), grid...  3.48 us
    pallas_call x1, Pallas kernels, body(): pl.pallas_call(functools.partial(pool_own_kernel, pool_steps), in_specs=[...  3.02 us
  transfers between devices with their start and end apart: 19, of which 5 were waited for; matrix products, arithmetic and copies ran while one was open for 0% of the time, Pallas kernels for 18%

profile of v4, /device:TPU:0, one launch (start us, length us, event | category | flops | bytes accessed | tf_op | source)
XLA Modules:
  0.0 60.7 jit_solution(5898749010202691608)
XLA Ops:
  0.6 0.5 collective-permute-start.3
  1.1 0.1 collective-permute-start.4
  1.2 0.4 collective-permute-start.2
  1.7 0.1 collective-permute-start
  1.7 0.4 collective-permute-start.1
  2.2 0.1 pad_add_fusion.idx
  2.2 0.0 copy-start.3
  2.2 0.0 copy-start.4
  2.3 3.7 %own_edges.1 = (f32[1536,256]{1,0:T(8,128)S(1)}, bf16[1536,384]{1,0:T(8,128)(2,1)S(1)}, bf16[1536,256]{1,0:T(8,128)(2,1)S(1)}, f32[1536,256]{1,0:T(8,128)S(1)}, bf16[1536,256]{1,0:T(8,128)(2,1)S(1)}) custom-call(s32[3]{0:T(128)S(1)} %pad_add_fusion.idx, s32[1,3072]{1,0:T(1,128)} %bitcast.9, bf16[384,256]{1,0:T(8,128)(2,1)} %refs_1_.1, ...), custom_call_target="tpu_custom_call" | custom-call | flops 301989888 | bytes 3145728 | tf_op jit(solution)/shard_map/own_edges/pallas_call | solution.py:326
  6.0 1.0 %collective-permute-done.refs_6_ = f32[1,256]{1,0:T(1,128)S(1)} collective-permute-done((f32[1,256]{1,0:T(1,128)}, f32[1,256]{1,0:T(1,128)S(1)}, u32[]{:S(2)}, u32[]{:S(2)}) %collective-permute-start) | collective-permute-done | bytes 1056 | tf_op jit(solution)/shard_map/ppermute | solution.py:307
  6.9 0.2 collective-permute-done.1.refs_8_
  7.1 0.0 collective-permute-done.2.refs_9_
  7.1 0.0 collective-permute-done.3.refs_10_
  7.1 0.0 collective-permute-done.4.refs_11_
  7.1 0.0 copy-done.3
  7.1 0.0 copy-done.4
  7.2 4.0 %edge_norm.1 = (bf16[1536,256]{1,0:T(8,128)(2,1)S(1)}, f32[256,256]{1,0:T(8,128)S(1)}, f32[1,256]{1,0:T(1,128)S(1)}, bf16[272,256]{1,0:T(8,128)(2,1)S(1)}) custom-call(s32[3]{0:T(128)S(1)} %pad_add_fusion.idx, f32[1536,256]{1,0:T(8,128)S(1)} %get-tuple-element.34.refs_0_, bf16[1536,384]{1,0:T(8,128)(2,1)S(1)} %get-tuple-element.35.refs_1_, ...), custom_call_target="tpu_custom_call" | custom-call | flops 1409286144 | bytes 3932160 | tf_op jit(solution)/shard_map/edge_norm/pallas_call | solution.py:349
  11.2 0.4 collective-permute-start.5
  11.6 0.1 collective-permute-start.6
  11.8 0.0 copy-start.2
  11.8 3.0 %pool_own.1 = (f32[512,256]{1,0:T(8,128)S(1)}, f32[768,256]{1,0:T(8,128)S(1)}, f32[384,256]{1,0:T(8,128)S(1)}) custom-call(s32[3]{0:T(128)S(1)} %pad_add_fusion.idx, bf16[1536,256]{1,0:T(8,128)(2,1)S(1)} %get-tuple-element.55.grad.refs_0_, s32[1,3072]{1,0:T(1,128)} %bitcast.12, s32[1,3072]{1,0:T(1,128)} %bitcast.10, bf16[3072,256]{1,0:T(8,128)(2,1)} %refs_2_.5, ...), custom_call_target="tpu_custom_call" | custom-call | flops 1308622848 | bytes 3145728 | tf_op jit(solution)/shard_map/pool_own/pallas_call | solution.py:405
  14.8 0.0 collective-permute-done.6.refs_10_
  14.8 0.0 collective-permute-done.5.grad.refs_2_
  14.8 0.0 copy-done.2
  14.8 0.0 copy-start.1
  14.8 3.6 %pool.1 = (f32[464,256]{1,0:T(8,128)S(1)}, bf16[464,256]{1,0:T(8,128)(2,1)S(1)}, bf16[464,256]{1,0:T(8,128)(2,1)S(1)}, bf16[464,256]{1,0:T(8,128)(2,1)S(1)}, bf16[384,256]{1,0:T(8,128)(2,1)S(1)}) custom-call(s32[3]{0:T(128)S(1)} %pad_add_fusion.idx, bf16[1536,256]{1,0:T(8,128)(2,1)S(1)} %collective-permute-done.5.grad.refs_2_, s32[1,3072]{1,0:T(1,128)} %bitcast.13, ...), custom_call_target="tpu_custom_call" | custom-call | flops 1308622848 | bytes 3145728 | tf_op jit(solution)/shard_map/pool/pallas_call | solution.py:415
  18.5 0.0 copy-start
  18.5 2.9 %collective-permute-start.17 = (bf16[1536,256]{1,0:T(8,128)(2,1)S(1)}, bf16[1536,256]{1,0:T(8,128)(2,1)S(1)}, u32[]{:S(2)}, u32[]{:S(2)}) collective-permute-start(bf16[1536,256]{1,0:T(8,128)(2,1)S(1)} %get-tuple-element.55.grad.refs_0_), channel_id=1, source_target_pairs={{0,2},{2,0},{1,3},{3,1},{4,6},{6,4},{5,7},{7,5},{8,10},{10,8},{9,1... | collective-permute-start | bytes 2359304 | tf_op jit(solution)/shard_map/ppermute | solution.py:431
  21.4 1.6 %collective-permute-start.7 = (bf16[464,256]{1,0:T(8,128)(2,1)S(1)}, bf16[464,256]{1,0:T(8,128)(2,1)S(1)}, u32[]{:S(2)}, u32[]{:S(2)}) collective-permute-start(bf16[464,256]{1,0:T(8,128)(2,1)S(1)} %get-tuple-element.47), channel_id=1, source_target_pairs={{0,4},{4,8},{8,12},{12,0},{1,5},{5,9},{9,13},{13,1},{2,6},{6,10},{... | collective-permute-start | bytes 712712 | tf_op jit(solution)/shard_map/ppermute | solution.py:432
  23.0 2.6 %collective-permute-start.8 = (bf16[464,256]{1,0:T(8,128)(2,1)S(1)}, bf16[464,256]{1,0:T(8,128)(2,1)S(1)}, u32[]{:S(2)}, u32[]{:S(2)}) collective-permute-start(bf16[464,256]{1,0:T(8,128)(2,1)S(1)} %get-tuple-element.48), channel_id=1, source_target_pairs={{0,8},{4,12},{8,0},{12,4},{1,9},{5,13},{9,1},{13,5},{2,10},{6,14},... | collective-permute-start | bytes 712712 | tf_op jit(solution)/shard_map/ppermute | solution.py:432
  25.6 1.3 %collective-permute-start.9 = (bf16[464,256]{1,0:T(8,128)(2,1)S(1)}, bf16[464,256]{1,0:T(8,128)(2,1)S(1)}, u32[]{:S(2)}, u32[]{:S(2)}) collective-permute-start(bf16[464,256]{1,0:T(8,128)(2,1)S(1)} %get-tuple-element.49), channel_id=1, source_target_pairs={{0,12},{4,0},{8,4},{12,8},{1,13},{5,1},{9,5},{13,9},{2,14},{6,2},{... | collective-permute-start | bytes 712712 | tf_op jit(solution)/shard_map/ppermute | solution.py:432
  26.9 0.5 collective-permute-start.10
  27.5 16.0 %collective-permute-done.10.refs_4_.refs_7_ = bf16[384,256]{1,0:T(8,128)(2,1)S(1)} collective-permute-done((bf16[384,256]{1,0:T(8,128)(2,1)S(1)}, bf16[384,256]{1,0:T(8,128)(2,1)S(1)}, u32[]{:S(2)}, u32[]{:S(2)}) %collective-permute-start.10) | collective-permute-done | bytes 196640 | tf_op jit(solution)/shard_map/ppermute | solution.py:433
  43.5 0.0 collective-permute-done.7.refs_1_
  43.5 0.0 collective-permute-done.8.refs_2_
  43.5 0.0 collective-permute-done.9.refs_3_
  43.5 0.7 %sum_parts.1 = (bf16[256,256]{1,0:T(8,128)(2,1)S(1)}, bf16[192,256]{1,0:T(8,128)(2,1)S(1)}, f32[1,256]{1,0:T(1,128)S(1)}) custom-call(s32[3]{0:T(128)S(1)} %pad_add_fusion.idx, f32[464,256]{1,0:T(8,128)S(1)} %get-tuple-element.46.refs_0_, bf16[464,256]{1,0:T(8,128)(2,1)S(1)} %collective-permute-done.7.refs_1_, ...), custom_call_target="tpu_custom_call" | custom-call | flops 475136 | bytes 1900544 | tf_op jit(solution)/shard_map/sum_parts/pallas_call | solution.py:434
  44.2 0.0 collective-permute-done.17.refs_1_
  44.2 0.1 collective-permute-start.18
  44.3 0.5 collective-permute-start.16
  44.8 3.2 %collective-permute-start.13 = (bf16[256,256]{1,0:T(8,128)(2,1)S(1)}, bf16[256,256]{1,0:T(8,128)(2,1)S(1)}, u32[]{:S(2)}, u32[]{:S(2)}) collective-permute-start(bf16[256,256]{1,0:T(8,128)(2,1)S(1)} %get-tuple-element.52.refs_0_), channel_id=1, source_target_pairs={{0,4},{4,8},{8,12},{12,0},{1,5},{5,9},{9,13},{13,1},{2,6},{6,10},{... | collective-permute-start | bytes 393224 | tf_op jit(solution)/shard_map/ppermute | solution.py:447
  48.0 1.6 %collective-permute-start.12 = (bf16[256,256]{1,0:T(8,128)(2,1)S(1)}, bf16[256,256]{1,0:T(8,128)(2,1)S(1)}, u32[]{:S(2)}, u32[]{:S(2)}) collective-permute-start(bf16[256,256]{1,0:T(8,128)(2,1)S(1)} %get-tuple-element.52.refs_0_), channel_id=1, source_target_pairs={{0,8},{4,12},{8,0},{12,4},{1,9},{5,13},{9,1},{13,5},{2,10},{6,14},... | collective-permute-start | bytes 393224 | tf_op jit(solution)/shard_map/ppermute | solution.py:447
  49.6 1.0 %collective-permute-start.11 = (bf16[256,256]{1,0:T(8,128)(2,1)S(1)}, bf16[256,256]{1,0:T(8,128)(2,1)S(1)}, u32[]{:S(2)}, u32[]{:S(2)}) collective-permute-start(bf16[256,256]{1,0:T(8,128)(2,1)S(1)} %get-tuple-element.52.refs_0_), channel_id=1, source_target_pairs={{0,12},{4,0},{8,4},{12,8},{1,13},{5,1},{9,5},{13,9},{2,14},{6,2},{... | collective-permute-start | bytes 393224 | tf_op jit(solution)/shard_map/ppermute | solution.py:447
  50.6 0.0 collective-permute-done.16.refs_10_
  50.6 1.5 %collective-permute-start.15 = (bf16[192,256]{1,0:T(8,128)(2,1)S(1)}, bf16[192,256]{1,0:T(8,128)(2,1)S(1)}, u32[]{:S(2)}, u32[]{:S(2)}) collective-permute-start(bf16[192,256]{1,0:T(8,128)(2,1)S(1)} %get-tuple-element.53.refs_11_), channel_id=1, source_target_pairs={{0,2},{2,0},{1,3},{3,1},{4,6},{6,4},{5,7},{7,5},{8,10},{10,8},{9,1... | collective-permute-start | bytes 294920 | tf_op jit(solution)/shard_map/ppermute | solution.py:450
  52.1 0.0 collective-permute-done.18.refs_3_
  52.1 0.0 collective-permute-start.14
  52.1 0.0 copy-done.1
  52.1 0.0 copy-done
  52.1 3.5 %edge_out.1 = (bf16[3072,256]{1,0:T(8,128)(2,1)}, f32[8,128]{1,0:T(8,128)S(1)}) custom-call(s32[3]{0:T(128)S(1)} %pad_add_fusion.idx, bf16[3072,256]{1,0:T(8,128)(2,1)S(1)} %copy-done.1, bf16[3,256,512]{2,1,0:T(8,128)(2,1)S(1)} %copy-done, bf16[1536,256]{1,0:T(8,128)(2,1)S(1)} %get-tuple-element.55.grad.refs_0_, ...), custom_call_target="tpu_custom_call" | custom-call | flops 805306368 | bytes 6291456 | tf_op jit(solution)/shard_map/edge_out/pallas_call | solution.py:458
  55.6 0.0 collective-permute-done.15.refs_9_
  55.6 1.6 %collective-permute-done.14.refs_8_ = bf16[192,256]{1,0:T(8,128)(2,1)S(1)} collective-permute-done((bf16[192,256]{1,0:T(8,128)(2,1)S(1)}, bf16[192,256]{1,0:T(8,128)(2,1)S(1)}, u32[]{:S(2)}, u32[]{:S(2)}) %collective-permute-start.14) | collective-permute-done | bytes 98336 | tf_op jit(solution)/shard_map/ppermute | solution.py:452
  57.1 0.0 collective-permute-done.13.refs_3_
  57.1 1.3 %collective-permute-done.12.refs_2_ = bf16[256,256]{1,0:T(8,128)(2,1)S(1)} collective-permute-done((bf16[256,256]{1,0:T(8,128)(2,1)S(1)}, bf16[256,256]{1,0:T(8,128)(2,1)S(1)}, u32[]{:S(2)}, u32[]{:S(2)}) %collective-permute-start.12) | collective-permute-done | bytes 131104 | tf_op jit(solution)/shard_map/ppermute | solution.py:447
  58.5 0.0 collective-permute-done.11.refs_1_
  58.5 2.2 %finish.1 = (f32[3,256,256]{2,1,0:T(8,128)}, f32[256,256]{1,0:T(8,128)}, f32[1,256]{1,0:T(1,128)}, f32[384,256]{1,0:T(8,128)}) custom-call(s32[3]{0:T(128)S(1)} %pad_add_fusion.idx, bf16[256,256]{1,0:T(8,128)(2,1)S(1)} %get-tuple-element.52.refs_0_, bf16[256,256]{1,0:T(8,128)(2,1)S(1)} %collective-permute-done.11.refs_1_, ...), custom_call_target="tpu_custom_call" | custom-call | flops 201326592 | bytes 1572864 | tf_op jit(solution)/shard_map/finish/pallas_call | solution.py:478
Async XLA Ops:
  0.6 6.5 %collective-permute-start.3 = (bf16[3072,256]{1,0:T(8,128)(2,1)}, bf16[3072,256]{1,0:T(8,128)(2,1)S(1)}, u32[]{:S(2)}, u32[]{:S(2)}) collective-permute-start(bf16[3072,256]{1,0:T(8,128)(2,1)} %refs_4_.2), channel_id=1, source_target_pairs={{0,1},{1,0},{2,3},{3,2},{4,5},{5,4},{6,7},{7,6},{8,9},{9,8},{10,11... | collective-permute-start | bytes 4718600 | tf_op jit(solution)/shard_map/ppermute | solution.py:307
  1.1 6.0 %collective-permute-start.4 = (bf16[3072,256]{1,0:T(8,128)(2,1)}, bf16[3072,256]{1,0:T(8,128)(2,1)S(1)}, u32[]{:S(2)}, u32[]{:S(2)}) collective-permute-start(bf16[3072,256]{1,0:T(8,128)(2,1)} %cot.1), channel_id=1, source_target_pairs={{0,1},{1,0},{2,3},{3,2},{4,5},{5,4},{6,7},{7,6},{8,9},{9,8},{10,11... | collective-permute-start | bytes 4718600 | tf_op jit(solution)/shard_map/ppermute | solution.py:307
  1.2 5.9 %collective-permute-start.2 = (bf16[384,256]{1,0:T(8,128)(2,1)}, bf16[384,256]{1,0:T(8,128)(2,1)S(1)}, u32[]{:S(2)}, u32[]{:S(2)}) collective-permute-start(bf16[384,256]{1,0:T(8,128)(2,1)} %refs_1_.1), channel_id=1, source_target_pairs={{0,1},{1,0},{2,3},{3,2},{4,5},{5,4},{6,7},{7,6},{8,9},{9,8},{10,11... | collective-permute-start | bytes 589832 | tf_op jit(solution)/shard_map/ppermute | solution.py:307
  1.7 5.3 %collective-permute-start = (f32[1,256]{1,0:T(1,128)}, f32[1,256]{1,0:T(1,128)S(1)}, u32[]{:S(2)}, u32[]{:S(2)}) collective-permute-start(f32[1,256]{1,0:T(1,128)} %bitcast.7), channel_id=1, source_target_pairs={{0,1},{1,0},{2,3},{3,2},{4,5},{5,4},{6,7},{7,6},{8,9},{9,8},{10,11... | collective-permute-start | bytes 3080 | tf_op jit(solution)/shard_map/ppermute | solution.py:307
  1.7 5.4 %collective-permute-start.1 = (bf16[256,256]{1,0:T(8,128)(2,1)}, bf16[256,256]{1,0:T(8,128)(2,1)S(1)}, u32[]{:S(2)}, u32[]{:S(2)}) collective-permute-start(bf16[256,256]{1,0:T(8,128)(2,1)} %refs_7_.2), channel_id=1, source_target_pairs={{0,1},{1,0},{2,3},{3,2},{4,5},{5,4},{6,7},{7,6},{8,9},{9,8},{10,11... | collective-permute-start | bytes 393224 | tf_op jit(solution)/shard_map/ppermute | solution.py:307
  2.2 4.9 %copy-start.3 = (bf16[256,256]{1,0:T(8,128)(2,1)S(1)}, bf16[256,256]{1,0:T(8,128)(2,1)}, u32[]{:S(2)}) copy-start(bf16[256,256]{1,0:T(8,128)(2,1)} %refs_7_.2) | copy-start | bytes 393220
  2.2 4.9 %copy-start.4 = (f32[256]{0:T(256)S(1)}, f32[256]{0:T(256)}, u32[]{:S(2)}) copy-start(f32[256]{0:T(256)} %param.17) | copy-start | bytes 3076
  11.2 3.6 %collective-permute-start.5 = (bf16[1536,256]{1,0:T(8,128)(2,1)S(1)}, bf16[1536,256]{1,0:T(8,128)(2,1)S(1)}, u32[]{:S(2)}, u32[]{:S(2)}) collective-permute-start(bf16[1536,256]{1,0:T(8,128)(2,1)S(1)} %get-tuple-element.55.grad.refs_0_), channel_id=1, source_target_pairs={{0,1},{1,0},{2,3},{3,2},{4,5},{5,4},{6,7},{7,6},{8,9},{9,8},{10,11... | collective-permute-start | bytes 2359304 | tf_op jit(solution)/shard_map/ppermute | solution.py:307
  11.6 3.2 %collective-permute-start.6 = (bf16[272,256]{1,0:T(8,128)(2,1)S(1)}, bf16[272,256]{1,0:T(8,128)(2,1)S(1)}, u32[]{:S(2)}, u32[]{:S(2)}) collective-permute-start(bf16[272,256]{1,0:T(8,128)(2,1)S(1)} %get-tuple-element.45), channel_id=1, source_target_pairs={{0,1},{1,0},{2,3},{3,2},{4,5},{5,4},{6,7},{7,6},{8,9},{9,8},{10,11... | collective-permute-start | bytes 417800 | tf_op jit(solution)/shard_map/ppermute | solution.py:307
  11.8 3.1 %copy-start.2 = (bf16[384,256]{1,0:T(8,128)(2,1)S(1)}, bf16[384,256]{1,0:T(8,128)(2,1)}, u32[]{:S(2)}) copy-start(bf16[384,256]{1,0:T(8,128)(2,1)} %refs_7_.3) | copy-start | bytes 589828
  14.8 37.2 %copy-start.1 = (bf16[3072,256]{1,0:T(8,128)(2,1)S(1)}, bf16[3072,256]{1,0:T(8,128)(2,1)}, u32[]{:S(2)}) copy-start(bf16[3072,256]{1,0:T(8,128)(2,1)} %cot.1) | copy-start | bytes 4718596
  18.5 33.6 %copy-start = (bf16[3,256,512]{2,1,0:T(8,128)(2,1)S(1)}, bf16[3,256,512]{2,1,0:T(8,128)(2,1)}, u32[]{:S(2)}) copy-start(bf16[3,256,512]{2,1,0:T(8,128)(2,1)} %refs_5_.1) | copy-start | bytes 2359300
  18.5 25.7 %collective-permute-start.17 = (bf16[1536,256]{1,0:T(8,128)(2,1)S(1)}, bf16[1536,256]{1,0:T(8,128)(2,1)S(1)}, u32[]{:S(2)}, u32[]{:S(2)}) collective-permute-start(bf16[1536,256]{1,0:T(8,128)(2,1)S(1)} %get-tuple-element.55.grad.refs_0_), channel_id=1, source_target_pairs={{0,2},{2,0},{1,3},{3,1},{4,6},{6,4},{5,7},{7,5},{8,10},{10,8},{9,1... | collective-permute-start | bytes 2359304 | tf_op jit(solution)/shard_map/ppermute | solution.py:431
  21.4 22.1 %collective-permute-start.7 = (bf16[464,256]{1,0:T(8,128)(2,1)S(1)}, bf16[464,256]{1,0:T(8,128)(2,1)S(1)}, u32[]{:S(2)}, u32[]{:S(2)}) collective-permute-start(bf16[464,256]{1,0:T(8,128)(2,1)S(1)} %get-tuple-element.47), channel_id=1, source_target_pairs={{0,4},{4,8},{8,12},{12,0},{1,5},{5,9},{9,13},{13,1},{2,6},{6,10},{... | collective-permute-start | bytes 712712 | tf_op jit(solution)/shard_map/ppermute | solution.py:432
  23.0 20.5 %collective-permute-start.8 = (bf16[464,256]{1,0:T(8,128)(2,1)S(1)}, bf16[464,256]{1,0:T(8,128)(2,1)S(1)}, u32[]{:S(2)}, u32[]{:S(2)}) collective-permute-start(bf16[464,256]{1,0:T(8,128)(2,1)S(1)} %get-tuple-element.48), channel_id=1, source_target_pairs={{0,8},{4,12},{8,0},{12,4},{1,9},{5,13},{9,1},{13,5},{2,10},{6,14},... | collective-permute-start | bytes 712712 | tf_op jit(solution)/shard_map/ppermute | solution.py:432
  25.6 17.9 %collective-permute-start.9 = (bf16[464,256]{1,0:T(8,128)(2,1)S(1)}, bf16[464,256]{1,0:T(8,128)(2,1)S(1)}, u32[]{:S(2)}, u32[]{:S(2)}) collective-permute-start(bf16[464,256]{1,0:T(8,128)(2,1)S(1)} %get-tuple-element.49), channel_id=1, source_target_pairs={{0,12},{4,0},{8,4},{12,8},{1,13},{5,1},{9,5},{13,9},{2,14},{6,2},{... | collective-permute-start | bytes 712712 | tf_op jit(solution)/shard_map/ppermute | solution.py:432
  26.9 16.5 %collective-permute-start.10 = (bf16[384,256]{1,0:T(8,128)(2,1)S(1)}, bf16[384,256]{1,0:T(8,128)(2,1)S(1)}, u32[]{:S(2)}, u32[]{:S(2)}) collective-permute-start(bf16[384,256]{1,0:T(8,128)(2,1)S(1)} %get-tuple-element.51.refs_6_), channel_id=1, source_target_pairs={{0,2},{2,0},{1,3},{3,1},{4,6},{6,4},{5,7},{7,5},{8,10},{10,8},{9,1... | collective-permute-start | bytes 589832 | tf_op jit(solution)/shard_map/ppermute | solution.py:433
  44.2 7.8 %collective-permute-start.18 = (bf16[1536,256]{1,0:T(8,128)(2,1)S(1)}, bf16[1536,256]{1,0:T(8,128)(2,1)S(1)}, u32[]{:S(2)}, u32[]{:S(2)}) collective-permute-start(bf16[1536,256]{1,0:T(8,128)(2,1)S(1)} %collective-permute-done.17.refs_1_), channel_id=1, source_target_pairs={{0,1},{1,0},{2,3},{3,2},{4,5},{5,4},{6,7},{7,6},{8,9},{9,8},{10,11... | collective-permute-start | bytes 2359304 | tf_op jit(solution)/shard_map/ppermute | solution.py:307
  44.3 6.3 %collective-permute-start.16 = (bf16[192,256]{1,0:T(8,128)(2,1)S(1)}, bf16[192,256]{1,0:T(8,128)(2,1)S(1)}, u32[]{:S(2)}, u32[]{:S(2)}) collective-permute-start(bf16[192,256]{1,0:T(8,128)(2,1)S(1)} %get-tuple-element.53.refs_11_), channel_id=1, source_target_pairs={{0,1},{1,0},{2,3},{3,2},{4,5},{5,4},{6,7},{7,6},{8,9},{9,8},{10,11... | collective-permute-start | bytes 294920 | tf_op jit(solution)/shard_map/ppermute | solution.py:307
  44.8 12.3 %collective-permute-start.13 = (bf16[256,256]{1,0:T(8,128)(2,1)S(1)}, bf16[256,256]{1,0:T(8,128)(2,1)S(1)}, u32[]{:S(2)}, u32[]{:S(2)}) collective-permute-start(bf16[256,256]{1,0:T(8,128)(2,1)S(1)} %get-tuple-element.52.refs_0_), channel_id=1, source_target_pairs={{0,4},{4,8},{8,12},{12,0},{1,5},{5,9},{9,13},{13,1},{2,6},{6,10},{... | collective-permute-start | bytes 393224 | tf_op jit(solution)/shard_map/ppermute | solution.py:447
  48.0 10.5 %collective-permute-start.12 = (bf16[256,256]{1,0:T(8,128)(2,1)S(1)}, bf16[256,256]{1,0:T(8,128)(2,1)S(1)}, u32[]{:S(2)}, u32[]{:S(2)}) collective-permute-start(bf16[256,256]{1,0:T(8,128)(2,1)S(1)} %get-tuple-element.52.refs_0_), channel_id=1, source_target_pairs={{0,8},{4,12},{8,0},{12,4},{1,9},{5,13},{9,1},{13,5},{2,10},{6,14},... | collective-permute-start | bytes 393224 | tf_op jit(solution)/shard_map/ppermute | solution.py:447
  49.6 8.9 %collective-permute-start.11 = (bf16[256,256]{1,0:T(8,128)(2,1)S(1)}, bf16[256,256]{1,0:T(8,128)(2,1)S(1)}, u32[]{:S(2)}, u32[]{:S(2)}) collective-permute-start(bf16[256,256]{1,0:T(8,128)(2,1)S(1)} %get-tuple-element.52.refs_0_), channel_id=1, source_target_pairs={{0,12},{4,0},{8,4},{12,8},{1,13},{5,1},{9,5},{13,9},{2,14},{6,2},{... | collective-permute-start | bytes 393224 | tf_op jit(solution)/shard_map/ppermute | solution.py:447
  50.6 5.0 %collective-permute-start.15 = (bf16[192,256]{1,0:T(8,128)(2,1)S(1)}, bf16[192,256]{1,0:T(8,128)(2,1)S(1)}, u32[]{:S(2)}, u32[]{:S(2)}) collective-permute-start(bf16[192,256]{1,0:T(8,128)(2,1)S(1)} %get-tuple-element.53.refs_11_), channel_id=1, source_target_pairs={{0,2},{2,0},{1,3},{3,1},{4,6},{6,4},{5,7},{7,5},{8,10},{10,8},{9,1... | collective-permute-start | bytes 294920 | tf_op jit(solution)/shard_map/ppermute | solution.py:450
  52.1 5.1 %collective-permute-start.14 = (bf16[192,256]{1,0:T(8,128)(2,1)S(1)}, bf16[192,256]{1,0:T(8,128)(2,1)S(1)}, u32[]{:S(2)}, u32[]{:S(2)}) collective-permute-start(bf16[192,256]{1,0:T(8,128)(2,1)S(1)} %get-tuple-element.53.refs_11_), channel_id=1, source_target_pairs={{0,3},{1,2},{2,1},{3,0},{4,7},{5,6},{6,5},{7,4},{8,11},{9,10},{10,... | collective-permute-start | bytes 294920 | tf_op jit(solution)/shard_map/ppermute | solution.py:452
